TPU v7x, 32 devices: a whole 2x2x4 slice. The times are simulated.
32 devices in a mesh: batch: 8 (over z, x), tm: 4 (over y, core).
Axes of the slice: x: 2, y: 2, z: 4, core: 2. Of those that a mesh axis runs over, the one named last changes fastest.
Arguments:
- inputs: bfloat16 [96, 256, 25, 128], P('batch', 'tm'), may hold values from -6 to 6
- cotangent: bfloat16 [96, 128, 25, 256], P('batch', 'tm'), may hold values from -6 to 6
- lengths: int32 [96], P('batch'), may hold values from 64 to 256, as said below
- frame_mask: int32 [96, 256], P('batch', 'tm'), may hold values 0 or 1
- subsets: int32 [25, 25], replicated, may hold values from 0 to 3, as said below
- graph_weight: float32 [128, 768], replicated, may hold values from -0.5 to 0.5
- graph_moment: float32 [128, 768], replicated, may hold values from -0.00030517578 to 0.00030517578
- graph_square: float32 [128, 768], replicated, may hold values from 2.0768907e-10 to 8.307563e-10
- graph_average: float32 [128, 768], replicated, may hold values from -0.5 to 0.5
- temporal_weight: float32 [9, 256, 256], replicated, may hold values from -0.125 to 0.125
- temporal_moment: float32 [9, 256, 256], replicated, may hold values from -0.0008544922 to 0.0008544922
- temporal_square: float32 [9, 256, 256], replicated, may hold values from 1.695421e-09 to 6.781684e-09
- temporal_average: float32 [9, 256, 256], replicated, may hold values from -0.125 to 0.125
- shortcut_weight: float32 [128, 256], replicated, may hold values from -0.5 to 0.5
- shortcut_moment: float32 [128, 256], replicated, may hold values from -0.0007324219 to 0.0007324219
- shortcut_square: float32 [128, 256], replicated, may hold values from 1.373291e-09 to 5.493164e-09
- shortcut_average: float32 [128, 256], replicated, may hold values from -0.5 to 0.5
- edge_weight: float32 [3, 25, 25], replicated, may hold values from 0.25 to 1.75
- edge_moment: float32 [3, 25, 25], replicated, may hold values from -0.0012207031 to 0.0012207031
- edge_square: float32 [3, 25, 25], replicated, may hold values from 3.390842e-09 to 1.3563368e-08
- edge_average: float32 [3, 25, 25], replicated, may hold values from 0.25 to 1.75
- norm_params: float32 [6, 256], replicated, may hold values from 0.25 to 1.75
- norm_moment: float32 [6, 256], replicated, may hold values from -0.0007324219 to 0.0007324219
- norm_square: float32 [6, 256], replicated, may hold values from 1.373291e-09 to 5.493164e-09
- norm_average: float32 [6, 256], replicated, may hold values from 0.25 to 1.75
Outputs:
- outputs: bfloat16 [96, 128, 25, 256], P('batch', 'tm')
- input_grad: bfloat16 [96, 256, 25, 128], P('batch', 'tm')
- grad_norm: float32 [1], replicated
- graph_weight_new: float32 [128, 768], replicated
- graph_moment_new: float32 [128, 768], replicated
- graph_square_new: float32 [128, 768], replicated
- graph_average_new: float32 [128, 768], replicated
- temporal_weight_new: float32 [9, 256, 256], replicated
- temporal_moment_new: float32 [9, 256, 256], replicated
- temporal_square_new: float32 [9, 256, 256], replicated
- temporal_average_new: float32 [9, 256, 256], replicated
- shortcut_weight_new: float32 [128, 256], replicated
- shortcut_moment_new: float32 [128, 256], replicated
- shortcut_square_new: float32 [128, 256], replicated
- shortcut_average_new: float32 [128, 256], replicated
- edge_weight_new: float32 [3, 25, 25], replicated
- edge_moment_new: float32 [3, 25, 25], replicated
- edge_square_new: float32 [3, 25, 25], replicated
- edge_average_new: float32 [3, 25, 25], replicated
- norm_params_new: float32 [6, 256], replicated
- norm_moment_new: float32 [6, 256], replicated
- norm_square_new: float32 [6, 256], replicated
- norm_average_new: float32 [6, 256], replicated
Inputs may be any that keep to these rules, and one draw needn't show every extreme that they name: `lengths`: clips at even positions have all 256 frames; each other clip has at most 129. `subsets`: A synthetic graph, not a real skeleton: label 1 on the diagonal only; joints whose numbers differ by one are linked, and further pairs are linked at random; a link from v to w has label 2 where w < v and 3 where w > v; 0 means no link; the pattern of links is symmetric.
All inputs are finite; a program needn't handle non-finite values. No bound on the sum of `frame_mask` on one device may be relied on, other than what follows from the above.
Results may differ from a plain program's by a relative error of at most 0.0076.
Values may be sent and summed in bfloat16 or wider, within the bound.
A program may use at most 384 MiB of HBM per device.

v0:
```python
import jax
import jax.numpy as jnp
from jax import lax
from jax.sharding import PartitionSpec as P

C_IN = 128
C_OUT = 256
JOINTS = 25
SUBSETS = 3
TAPS = 9


norm_epsilon = 1e-05
beta_first = 0.9
beta_second = 0.999
adam_epsilon = 1e-08
clip_limit = 1.0
average_decay = 0.9
rate_matrix = 0.05
rate_small = 0.3
decay_matrix = 0.01
steps_taken = 3.0


def with_halo(cells, sides, width):
    for axis, dim in sides:
        count = lax.axis_size(axis)
        ends = count - 1
        head = lax.slice_in_dim(cells, 0, width, axis=dim)
        tail = lax.slice_in_dim(cells, cells.shape[dim] - width, cells.shape[dim], axis=dim)
        cells = jnp.concatenate(
            [
                lax.ppermute(tail, axis, [(i, (i + 1) % count) for i in range(ends)]),
                cells,
                lax.ppermute(head, axis, [((i + 1) % count, i) for i in range(ends)]),
            ],
            axis=dim,
        )
    return cells


def adjacency(subsets):
    linked = (subsets > 0).astype(jnp.float32)
    degree = jnp.sum(linked, axis=0)
    labels = jnp.arange(SUBSETS, dtype=jnp.int32) + 1
    chosen = (subsets[None, :, :] == labels[:, None, None]).astype(jnp.float32)
    return chosen / degree[None, None, :]


def silu_slope(values):
    sigmoid_part = jax.nn.sigmoid(values)
    return sigmoid_part * (1.0 + values * (1.0 - sigmoid_part))


def adam_update(
    weight, moment, square, average, gradient, factor, rate, decay, fix_first, fix_second
):
    clipped = gradient * factor
    moment_new = beta_first * moment + (1.0 - beta_first) * clipped
    square_new = beta_second * square + (1.0 - beta_second) * clipped * clipped
    stepped = moment_new / fix_first / (jnp.sqrt(square_new / fix_second) + adam_epsilon)
    weight_new = weight - rate * (stepped + decay * weight)
    average_new = average_decay * average + (1.0 - average_decay) * weight_new
    return (weight_new, moment_new, square_new, average_new)


def masked_sums(values, wide_mask):
    return (
        jnp.sum(values * wide_mask, axis=(0, 1, 2)),
        jnp.sum(values * values * wide_mask, axis=(0, 1, 2)),
    )


def shards(
    inputs,
    cotangent,
    lengths,
    frame_mask,
    subsets,
    graph_weight,
    graph_moment,
    graph_square,
    graph_average,
    temporal_weight,
    temporal_moment,
    temporal_square,
    temporal_average,
    shortcut_weight,
    shortcut_moment,
    shortcut_square,
    shortcut_average,
    edge_weight,
    edge_moment,
    edge_square,
    edge_average,
    norm_params,
    norm_moment,
    norm_square,
    norm_average,
):
    low_type = jnp.bfloat16
    clips_here = inputs.shape[0]
    frames_here = inputs.shape[1]
    half_frames = frames_here // 2
    first_frame = lax.axis_index("tm") * frames_here
    frame_ids = first_frame + jnp.arange(frames_here, dtype=jnp.int32)
    mask_in = ((frame_ids[None, :] < lengths[:, None]) & (frame_mask > 0)).astype(jnp.float32)
    mask_out = mask_in[:, ::2]
    wide_in = mask_in[:, :, None, None]
    wide_out = mask_out[:, :, None, None]
    graph_mask = adjacency(subsets)
    graph_low = (graph_mask * edge_weight).astype(low_type)
    weight_low = graph_weight.astype(low_type)
    flat_in = inputs.reshape(-1, C_IN)
    mixed_rows = jnp.dot(flat_in, weight_low, preferred_element_type=jnp.float32).astype(low_type)
    mixed_rows = mixed_rows.reshape(clips_here, frames_here, JOINTS, SUBSETS, C_OUT)
    hidden = jnp.einsum(
        "ntvkc,kvw->ntwc", mixed_rows, graph_low, preferred_element_type=jnp.float32
    )
    sum_in, square_in = masked_sums(hidden, wide_in)
    count_here = JOINTS * jnp.sum(mask_in)
    sum_in, square_in, count_in = lax.psum((sum_in, square_in, count_here), ("batch", "tm"))
    mean_in = sum_in / count_in
    rstd_in = lax.rsqrt(square_in / count_in - mean_in * mean_in + norm_epsilon)
    normed_in = (hidden - mean_in) * rstd_in
    first_norm = norm_params[0] * normed_in + norm_params[1]
    active = (jax.nn.silu(first_norm) * wide_in).astype(low_type)
    padded = with_halo(active, (("tm", 1),), 4)
    taps_low = temporal_weight.astype(low_type)
    windows = [
        padded[:, tap_index : tap_index + 2 * half_frames : 2].reshape(-1, C_OUT)
        for tap_index in range(TAPS)
    ]
    conv_flat = jnp.zeros((clips_here * half_frames * JOINTS, C_OUT), jnp.float32)
    for tap_index in range(TAPS):
        conv_flat = conv_flat + jnp.dot(
            windows[tap_index], taps_low[tap_index], preferred_element_type=jnp.float32
        )
    conv_out = conv_flat.reshape(clips_here, half_frames, JOINTS, C_OUT)
    even_inputs = inputs[:, ::2].reshape(-1, C_IN)
    short_low = shortcut_weight.astype(low_type)
    short_out = jnp.dot(even_inputs, short_low, preferred_element_type=jnp.float32).reshape(
        clips_here, half_frames, JOINTS, C_OUT
    )
    sum_conv, square_conv = masked_sums(conv_out, wide_out)
    sum_short, square_short = masked_sums(short_out, wide_out)
    count_here_out = JOINTS * jnp.sum(mask_out)
    sum_conv, square_conv, sum_short, square_short, count_out = lax.psum(
        (sum_conv, square_conv, sum_short, square_short, count_here_out), ("batch", "tm")
    )
    mean_conv = sum_conv / count_out
    rstd_conv = lax.rsqrt(square_conv / count_out - mean_conv * mean_conv + norm_epsilon)
    mean_short = sum_short / count_out
    rstd_short = lax.rsqrt(square_short / count_out - mean_short * mean_short + norm_epsilon)
    normed_conv = (conv_out - mean_conv) * rstd_conv
    normed_short = (short_out - mean_short) * rstd_short
    summed = (
        norm_params[2] * normed_conv
        + norm_params[3]
        + norm_params[4] * normed_short
        + norm_params[5]
    )
    outputs = (jax.nn.silu(summed) * wide_out).astype(low_type)
    upstream = cotangent.astype(jnp.float32) * wide_out * silu_slope(summed)
    back_sum = jnp.sum(upstream, axis=(0, 1, 2))
    back_conv = jnp.sum(upstream * normed_conv, axis=(0, 1, 2))
    back_short = jnp.sum(upstream * normed_short, axis=(0, 1, 2))
    back_sum, back_conv, back_short = lax.psum((back_sum, back_conv, back_short), ("batch", "tm"))
    conv_grad = (
        wide_out
        * norm_params[2]
        * rstd_conv
        * (upstream - back_sum / count_out - normed_conv * back_conv / count_out)
    ).astype(low_type)
    short_grad = (
        wide_out
        * norm_params[4]
        * rstd_short
        * (upstream - back_sum / count_out - normed_short * back_short / count_out)
    ).astype(low_type)
    grad_rims = with_halo(conv_grad, (("tm", 1),), 2)
    grad_slices = [
        grad_rims[:, 4 - shift_index : 4 - shift_index + half_frames].reshape(-1, C_OUT)
        for shift_index in range(5)
    ]
    even_grad = jnp.zeros((clips_here * half_frames * JOINTS, C_OUT), jnp.float32)
    for shift_index in range(5):
        even_grad = even_grad + jnp.einsum(
            "rd,cd->rc",
            grad_slices[shift_index],
            taps_low[2 * shift_index],
            preferred_element_type=jnp.float32,
        )
    odd_grad = jnp.zeros((clips_here * half_frames * JOINTS, C_OUT), jnp.float32)
    for shift_index in range(4):
        odd_grad = odd_grad + jnp.einsum(
            "rd,cd->rc",
            grad_slices[shift_index],
            taps_low[2 * shift_index + 1],
            preferred_element_type=jnp.float32,
        )
    active_grad = jnp.stack(
        [
            even_grad.reshape(clips_here, half_frames, JOINTS, C_OUT),
            odd_grad.reshape(clips_here, half_frames, JOINTS, C_OUT),
        ],
        axis=2,
    )
    active_grad = active_grad.reshape(clips_here, frames_here, JOINTS, C_OUT)
    conv_rows = conv_grad.reshape(-1, C_OUT)
    temporal_grad = jnp.stack(
        [
            jnp.einsum(
                "rc,rd->cd", windows[tap_index], conv_rows, preferred_element_type=jnp.float32
            )
            for tap_index in range(TAPS)
        ]
    )
    short_rows = short_grad.reshape(-1, C_OUT)
    shortcut_grad = jnp.einsum(
        "rc,rd->cd", even_inputs, short_rows, preferred_element_type=jnp.float32
    )
    first_grad = active_grad * wide_in * silu_slope(first_norm)
    back_first_sum = jnp.sum(first_grad, axis=(0, 1, 2))
    back_first_norm = jnp.sum(first_grad * normed_in, axis=(0, 1, 2))
    back_first_sum, back_first_norm = lax.psum((back_first_sum, back_first_norm), ("batch", "tm"))
    hidden_grad = (
        wide_in
        * norm_params[0]
        * rstd_in
        * (first_grad - back_first_sum / count_in - normed_in * back_first_norm / count_in)
    ).astype(low_type)
    mixed_grad = jnp.einsum(
        "ntwc,kvw->ntvkc", hidden_grad, graph_low, preferred_element_type=jnp.float32
    ).astype(low_type)
    edge_grad = (
        jnp.einsum("ntvkc,ntwc->kvw", mixed_rows, hidden_grad, preferred_element_type=jnp.float32)
        * graph_mask
    )
    mixed_flat = mixed_grad.reshape(-1, SUBSETS * C_OUT)
    graph_grad = jnp.einsum("rc,rd->cd", flat_in, mixed_flat, preferred_element_type=jnp.float32)
    input_back = jnp.einsum("rd,cd->rc", mixed_flat, weight_low, preferred_element_type=jnp.float32)
    input_back = input_back.reshape(clips_here, half_frames, 2, JOINTS, C_IN)
    short_back = jnp.einsum("rd,cd->rc", short_rows, short_low, preferred_element_type=jnp.float32)
    short_back = short_back.reshape(clips_here, half_frames, JOINTS, C_IN)
    input_grad = jnp.stack([input_back[:, :, 0] + short_back, input_back[:, :, 1]], axis=2)
    input_grad = input_grad.reshape(clips_here, frames_here, JOINTS, C_IN).astype(low_type)
    norm_grad = jnp.stack(
        [back_first_norm, back_first_sum, back_conv, back_sum, back_short, back_sum]
    )
    fix_first = 1.0 - beta_first**steps_taken
    fix_second = 1.0 - beta_second**steps_taken
    graph_sum, temporal_sum, shortcut_sum, edge_sum = lax.psum(
        (graph_grad, temporal_grad, shortcut_grad, edge_grad), ("batch", "tm")
    )
    squares_total = (
        jnp.sum(graph_sum * graph_sum)
        + jnp.sum(temporal_sum * temporal_sum)
        + jnp.sum(shortcut_sum * shortcut_sum)
        + jnp.sum(edge_sum * edge_sum)
        + jnp.sum(norm_grad * norm_grad)
    )
    norm_total = jnp.sqrt(squares_total)
    factor = jnp.minimum(1.0, clip_limit / (norm_total + 1e-06))
    graph_new = adam_update(
        graph_weight,
        graph_moment,
        graph_square,
        graph_average,
        graph_sum,
        factor,
        rate_matrix,
        decay_matrix,
        fix_first,
        fix_second,
    )
    temporal_new = adam_update(
        temporal_weight,
        temporal_moment,
        temporal_square,
        temporal_average,
        temporal_sum,
        factor,
        rate_matrix,
        decay_matrix,
        fix_first,
        fix_second,
    )
    shortcut_new = adam_update(
        shortcut_weight,
        shortcut_moment,
        shortcut_square,
        shortcut_average,
        shortcut_sum,
        factor,
        rate_matrix,
        decay_matrix,
        fix_first,
        fix_second,
    )
    edge_new = adam_update(
        edge_weight,
        edge_moment,
        edge_square,
        edge_average,
        edge_sum,
        factor,
        rate_small,
        0.0,
        fix_first,
        fix_second,
    )
    norm_new = adam_update(
        norm_params,
        norm_moment,
        norm_square,
        norm_average,
        norm_grad,
        factor,
        rate_small,
        0.0,
        fix_first,
        fix_second,
    )
    return (
        outputs,
        input_grad,
        jnp.reshape(norm_total, (1,)),
        graph_new[0],
        graph_new[1],
        graph_new[2],
        graph_new[3],
        temporal_new[0],
        temporal_new[1],
        temporal_new[2],
        temporal_new[3],
        shortcut_new[0],
        shortcut_new[1],
        shortcut_new[2],
        shortcut_new[3],
        edge_new[0],
        edge_new[1],
        edge_new[2],
        edge_new[3],
        norm_new[0],
        norm_new[1],
        norm_new[2],
        norm_new[3],
    )


def solution(mesh):
    in_specs = (
        P("batch", "tm", None, None),
        P("batch", "tm", None, None),
        P("batch"),
        P("batch", "tm"),
        P(),
        P(),
        P(),
        P(),
        P(),
        P(),
        P(),
        P(),
        P(),
        P(),
        P(),
        P(),
        P(),
        P(),
        P(),
        P(),
        P(),
        P(),
        P(),
        P(),
        P(),
    )
    out_specs = (
        P("batch", "tm", None, None),
        P("batch", "tm", None, None),
        P(),
        P(),
        P(),
        P(),
        P(),
        P(),
        P(),
        P(),
        P(),
        P(),
        P(),
        P(),
        P(),
        P(),
        P(),
        P(),
        P(),
        P(),
        P(),
        P(),
        P(),
    )
    return jax.shard_map(shards, mesh=mesh, in_specs=in_specs, out_specs=out_specs, check_vma=False)
```

profile of v0, /device:TPU:0, one launch (start us, length us, event | category | flops | bytes accessed | tf_op | source)
XLA Modules:
  0.0 1408.0 jit_solution(8751744606187337581)
XLA Ops:
  11.2 9.0 copy.149
  20.3 9.3 reshape.175
  29.6 15.6 %convolution_convert_fusion = bf16[19200,768]{1,0:T(8,128)(2,1)} fusion(bf16[19200,128]{1,0:T(8,128)(2,1)} %reshape.175, f32[128,768]{1,0:T(8,128)S(1)} %copy-done.14), kind=kOutput, calls=%fused_computation.5 | convolution fusion | flops 3789717504 | bytes 34799616 | tf_op jit(solution)/shard_map/dot_general | solution.py:115
  45.2 63.8 %reshape.176 = bf16[12,64,25,3,256]{4,3,2,1,0:T(4,128)(2,1)} reshape(bf16[19200,768]{1,0:T(8,128)(2,1)} %convolution_convert_fusion) | data formatting | bytes 58982400 | tf_op jit(solution)/shard_map/reshape | solution.py:116
  110.3 28.1 %fusion.14 = (f32[256]{0:T(256)S(1)}, f32[256]{0:T(256)S(1)}, f32[25,12,64,256,1]{3,0,4,2,1:T(8,128)}) fusion(f32[12,64]{1,0:T(8,128)S(1)} %get-tuple-element.149, bf16[12,64,25,3,256]{4,3,2,1,0:T(4,128)(2,1)} %reshape.176, f32[3,25,25]{1,2,0:T(8,128)S(1)} %copy.148, f32[25]{0:T(128)S(1)} %convert_reduce_fusion, s32[3]{0:T(128)S(1)} %iota_add_fusion.1, ...), kind=kOutput, calls=%fused_computation.23 | convolution fusion | flops 761864832 | bytes 49167232 | tf_op jit(solution)/shard_map/ntvkc,kvw->ntwc/dot_general | solution.py:117
  138.5 51.5 %all-reduce.4 = (f32[256]{0:T(256)S(1)}, f32[]{:T(128)}, f32[256]{0:T(256)S(1)}) all-reduce(f32[256]{0:T(256)S(1)} %get-tuple-element.93, f32[]{:T(128)S(6)} %mul.590, f32[256]{0:T(256)S(1)} %get-tuple-element.92), channel_id=1, replica_groups=mesh['batch'=8,'tm'=4] {'batch','tm'}, use_global_device_ids=true, to_apply=%region_2.0 | all-reduce | flops 513 | bytes 4104 | tf_op jit(solution)/shard_map/psum | solution.py:122
  190.6 12.7 multiply_convert_fusion
  217.1 25.6 %slice.151 = bf16[12,32,25,128]{3,1,2,0:T(8,128)(2,1)} slice(bf16[12,64,25,128]{3,1,2,0:T(8,128)(2,1)} %param.25), slice={[0:12:1], [0:64:2], [0:25:1], [0:128:1]} | slice | bytes 4915200 | tf_op jit(solution)/shard_map/slice | solution.py:140
  242.8 6.3 slice.138
  260.4 9.1 reshape.181
  269.5 8.1 multiply_reduce_fusion.2
  279.0 12.9 pad_maximum_fusion.1
  291.9 33.4 %fusion.86 = (bf16[12,32,25,256]{3,2,1,0:T(8,128)(2,1)}, bf16[12,32,25,256]{3,2,1,0:T(8,128)(2,1)}, bf16[12,32,25,256]{3,2,1,0:T(8,128)(2,1)}, bf16[12,32,25,256...) fusion(bf16[12,72,25,256]{3,2,1,0:T(8,128)(2,1)} %pad_maximum_f, ...), kind=kLoop, calls=%fused_computation.189 | loop fusion | bytes 78643200 | tf_op jit(solution)/shard_map/slice | solution.py:131
  325.3 8.7 reshape.185
  334.0 8.7 reshape.184
  342.7 8.7 reshape.183
  351.4 8.7 reshape.182
  360.0 8.7 reshape.180
  368.7 8.7 reshape.179
  377.4 8.6 reshape.178
  386.0 9.0 reshape.177
  420.4 7.2 multiply_reduce_fusion.4
  427.7 11.5 reshape.186
  439.2 39.6 %all-reduce.3 = (f32[256]{0:T(256)S(1)}, f32[]{:T(128)}, f32[256]{0:T(256)S(1)}, f32[256]{0:T(256)S(1)}, f32[256]{0:T(256)S(1)}) all-reduce(f32[256]{0:T(256)S(1)} %copy-done.70, f32[]{:T(128)S(6)} %mul.605, f32[256]{0:T(256)S(1)} %copy-done.69, f32[256]{0:T(256)S(1)} %get-tuple-element.97, ...), channel_id=1, replica_groups=mesh['batch'=8,'tm'=4] {'batch','tm'}, use_global_device_ids=true, to_apply=%region_14.15 | all-reduce | flops 1025 | bytes 8200 | tf_op jit(solution)/shard_map/psum | solution.py:148
  480.4 20.9 %multiply_reduce_fusion = (f32[256]{0:T(256)}, f32[256]{0:T(256)S(1)}, f32[256]{0:T(256)S(1)}, f32[12,32,25,256]{3,1,2,0:T(8,128)}, bf16[12,32,25,256]{3,1,2,0:T(8,128)(2,1)}) fusion(f32[12,32,25,256]{3,1,2,0:T(8,128)} %get-tuple-element.178, f32[256]{0:T(256)S(1)} %get-tuple-element.144, f32[256]{0:T(256)S(1)} %get-tuple-element.145, ...), kind=kLoop, calls=%fused_computation.49 | loop fusion | flops 66354432 | bytes 39334400 | tf_op jit(solution)/shard_map/reduce_sum | solution.py:167
  501.4 40.6 %all-reduce.2 = (f32[256]{0:T(256)S(1)}, f32[256]{0:T(256)S(1)}) all-reduce(f32[256]{0:T(256)S(1)} %get-tuple-element.101, f32[256]{0:T(256)S(1)} %get-tuple-element.102), channel_id=1, replica_groups=mesh['batch'=8,'tm'=4] {'batch','tm'}, use_global_device_ids=true, to_apply=%region_20.21 | all-reduce | flops 512 | bytes 4096 | tf_op jit(solution)/shard_map/psum | solution.py:168
  542.7 13.2 multiply_convert_fusion.2
  557.6 7.4 fusion.33
  602.8 6.2 copy.158
  608.9 9.1 reshape.189
  618.0 19.6 %pad_maximum_fusion.2 = (bf16[12,32,25,256]{3,1,2,0:T(8,128)(2,1)}, bf16[12,32,25,256]{3,1,2,0:T(8,128)(2,1)}, bf16[12,32,25,256]{3,1,2,0:T(8,128)(2,1)S(1)}, bf16[12,32,25,256]{3,1,2,0:T(8,128)(2,1)}) fusion(bf16[12,32,25,256]{3,1,2,0:T(8,128)(2,1)} %copy-done.2, bf16[12,2,25,256]{3,1,2,0:T(2,128)(2,1)S(1)} %collective-permute-done.3, ...), kind=kLoop, calls=%fused_computation.71 | loop fusion | flops 39321600 | bytes 25190400 | tf_op jit(solution)/shard_map/concatenate | solution.py:31
  637.5 6.2 copy.156
  643.7 8.9 reshape.187
  652.7 7.7 fusion.48
  665.5 6.2 copy.160
  671.7 8.7 reshape.191
  680.4 8.5 copy.159
  688.9 8.9 reshape.190
  697.8 8.5 copy.157
  706.3 8.7 reshape.188
  715.1 6.9 convolution_add_fusion.2
  723.6 7.8 convolution_add_fusion
  731.5 11.9 stack_reshape.7
  743.4 6.9 convolution_add_fusion.6
  761.6 11.5 stack_reshape.6
  773.1 20.4 %pad_maximum_fusion = f32[12,32,2,25,256]{4,3,1,0,2:T(8,128)} fusion(f32[12,32,1,25,256]{4,3,1,0,2:T(8,128)} %stack_reshape.7, f32[12,32,1,25,256]{4,3,1,0,2:T(8,128)} %stack_reshape.6), kind=kLoop, calls=%fused_computation.8 | loop fusion | flops 4915200 | bytes 39321600 | tf_op jit(solution)/shard_map/stack | solution.py:202
  793.6 19.6 %copy.161 = f32[12,32,2,25,256]{4,3,2,1,0:T(8,128)} copy(f32[12,32,2,25,256]{4,3,1,0,2:T(8,128)} %pad_maximum_fusion) | data formatting | bytes 39321600 | tf_op jit(solution)/shard_map/stack | solution.py:202
  813.3 23.1 %fusion.79 = (f32[256]{0:T(256)S(1)}, f32[256]{0:T(256)S(1)}, f32[12,64,25,256]{3,2,1,0:T(8,128)}) fusion(f32[256]{0:T(256)S(1)} %copy-done.37, f32[256]{0:T(256)S(1)} %copy-done.44, f32[25,12,64,256,1]{3,0,4,2,1:T(8,128)S(1)} %bitcast.267, f32[256]{0:T(256)S(1)} %bitcast.294, f32[256]{0:T(256)S(1)} %bitcast.292, f32[12,64,25,256]{3,2,1,0:T(8,128)} %bitcast.269, ...), kind=kLoop, calls=%fused_computation.187 | loop fusion | flops 78642688 | bytes 58991616 | tf_op jit(solution)/shard_map/reduce_sum | solution.py:224
  836.3 42.7 %all-reduce.1 = (f32[256]{0:T(256)S(1)}, f32[256]{0:T(256)S(1)}) all-reduce(f32[256]{0:T(256)S(1)} %get-tuple-element.95, f32[256]{0:T(256)S(1)} %get-tuple-element.94), channel_id=1, replica_groups=mesh['batch'=8,'tm'=4] {'batch','tm'}, use_global_device_ids=true, to_apply=%region_24.25 | all-reduce | flops 512 | bytes 4096 | tf_op jit(solution)/shard_map/psum | solution.py:226
  879.7 21.9 %fusion.15 = bf16[12,64,25,256]{3,2,1,0:T(8,128)(2,1)} fusion(f32[12,64,25,256]{3,2,1,0:T(8,128)} %get-tuple-element.140, f32[25,12,64,256,1]{3,0,4,2,1:T(8,128)} %get-tuple-element.177, f32[]{:T(128)} %get-tuple-element.115, f32[256]{0:T(256)S(1)} %get-tuple-element.105, f32[256]{0:T(256)S(1)} %broadcast_divide_fusion.3, f32[12,64,256]{2,1,0:T(8,128)S(1)} %copy-done.8, ...), kind=kLoop, calls=%fused_computation.27 | loop fusion | flops 39321600 | bytes 49942532 | tf_op jit(solution)/shard_map/convert_element_type | solution.py:232
  901.6 28.7 %fusion.39 = f32[3,25,25]{1,2,0:T(8,128)S(1)} fusion(bf16[12,64,25,3,256]{4,3,2,1,0:T(4,128)(2,1)} %reshape.176, bf16[12,64,25,256]{3,2,1,0:T(8,128)(2,1)} %fusion.15, f32[25]{0:T(128)S(1)} %copy-done.57, s32[25,25]{0,1:T(8,128)S(1)} %copy-done.24, s32[3]{0:T(128)S(1)} %copy-done.59), kind=kOutput, calls=%fused_computation.102 | convolution fusion | flops 737287424 | bytes 39331712 | tf_op jit(solution)/shard_map/ntvkc,ntwc->kvw/dot_general | solution.py:237
  930.2 22.8 %convert_bitcast_fusion = bf16[12,64,25,3,256]{4,2,1,0,3:T(8,128)(2,1)} fusion(bf16[12,64,25,256]{3,2,1,0:T(8,128)(2,1)} %fusion.15, f32[3,25,25]{1,2,0:T(8,128)S(1)} %copy-done.19, f32[25]{0:T(128)S(1)} %copy-done.57, s32[25,25]{0,1:T(8,128)S(1)} %copy-done.24, s32[3]{0:T(128)S(1)} %copy-done.59), kind=kOutput, calls=%fused_computation.4 | convolution fusion | flops 752034944 | bytes 39331712 | tf_op jit(solution)/shard_map/ntwc,kvw->ntvkc/dot_general | solution.py:233
  953.1 41.6 %copy.167 = bf16[12,64,25,3,256]{4,3,2,1,0:T(4,128)(2,1)} copy(bf16[12,64,25,3,256]{4,2,1,0,3:T(8,128)(2,1)} %convert_bitcast_fusion) | data formatting | bytes 58982400 | tf_op jit(solution)/shard_map/convert_element_type | solution.py:235
  994.7 41.8 %copy.163 = bf16[12,64,25,3,256]{4,3,1,2,0:T(4,128)(2,1)} copy(bf16[12,64,25,3,256]{4,2,1,0,3:T(8,128)(2,1)} %convert_bitcast_fusion) | data formatting | bytes 58982400 | tf_op jit(solution)/shard_map/convert_element_type | solution.py:235
  1036.6 41.4 %all-reduce = (f32[256]{0:T(256)S(1)}, f32[3,25,25]{1,2,0:T(8,128)S(1)}) all-reduce(f32[256]{0:T(256)S(1)} %copy-done.64, f32[3,25,25]{1,2,0:T(8,128)S(1)} %fusion.39), channel_id=1, replica_groups=mesh['batch'=8,'tm'=4] {'batch','tm'}, use_global_device_ids=true, to_apply=%region_26.27 | all-reduce | flops 2131 | bytes 17048 | tf_op jit(solution)/shard_map/psum | solution.py:168
  1078.0 8.7 multiply_convert_fusion.1
  1089.0 23.9 %copy.225 = bf16[2400,8,3,256]{3,1,2,0:T(8,128)(2,1)} copy(bf16[2400,8,3,256]{3,2,1,0:T(4,128)(2,1)} %bitcast.268) | data formatting | bytes 58982400
  1112.9 15.5 %convolution_bitcast_fusion = f32[128,768]{0,1:T(8,128)} fusion(bf16[19200,768]{1,0:T(8,128)(2,1)} %bitcast.278, bf16[19200,128]{1,0:T(8,128)(2,1)} %reshape.175), kind=kOutput, calls=%fused_computation.81 | convolution fusion | flops 3774873600 | bytes 34799616 | tf_op jit(solution)/shard_map/rc,rd->cd/dot_general | solution.py:241
  1128.4 87.2 %dot_general.136 = bf16[12,32,2,25,768]{4,2,1,3,0:T(2,128)(2,1)} reshape(bf16[12,64,25,3,256]{4,3,1,2,0:T(4,128)(2,1)} %copy.163) | data formatting | bytes 58982400 | tf_op jit(solution)/shard_map/rd,cd->rc/dot_general | solution.py:242
  1215.6 20.3 %fusion.4 = f32[12,32,2,25,128]{4,1,3,2,0:T(8,128)} fusion(bf16[12,32,2,25,768]{4,2,1,3,0:T(2,128)(2,1)} %dot_general.136, f32[128,768]{1,0:T(8,128)S(1)} %copy-done.15), kind=kOutput, calls=%fused_computation.6 | convolution fusion | flops 3774971904 | bytes 39714816 | tf_op jit(solution)/shard_map/rd,cd->rc/dot_general | solution.py:242
  1239.0 5.4 fusion.23
  1247.1 9.9 copy.166
  1258.3 95.2 %all-reduce.8.cloned.1.call-done = (f32[128,768]{0,1:T(8,128)}, f32[9,256,256]{2,1,0:T(8,128)}, f32[128,256]{0,1:T(8,128)}) async-done(((f32[128,768]{0,1:T(8,128)}, f32[9,256,256]{2,1,0:T(8,128)}, f32[128,256]{0,1:T(8,128)}), (f32[128,768]{0,1:T(8,128)}, f32[9,256,256]{2,1,0:T(8,128)}, f32[128,256]{0,1:T(8,128)})) %all-reduce.8.cloned.1.call-update) | async-done | bytes 2883600 | tf_op jit(solution)/shard_map/psum | solution.py:253
  1390.8 9.0 multiply_add_fusion
  (304 shorter events, 160.0 us)
Async XLA Ops:
  7.2 1346.2 %all-reduce.8.cloned.1.call-start = ((), (), s32[]{:S(2)}) async-start(), calls=%async_computation | async-start | bytes 5767168 | tf_op jit(solution)/shard_map/psum | solution.py:253
  7.2 103.1 %copy-start.58 = (s32[3]{0:T(128)}, s32[3]{0:T(128)S(1)}, u32[]{:S(2)}) copy-start(s32[3]{0:T(128)S(1)} %iota_add_fusion.1) | copy-start | bytes 40
  8.0 102.3 %copy-start.56 = (f32[25]{0:T(128)}, f32[25]{0:T(128)S(1)}, u32[]{:S(2)}) copy-start(f32[25]{0:T(128)S(1)} %convert_reduce_fusion) | copy-start | bytes 304
  8.8 101.5 %copy-start.23 = (s32[25,25]{0,1:T(8,128)}, s32[25,25]{0,1:T(8,128)S(1)}, u32[]{:S(2)}) copy-start(s32[25,25]{0,1:T(8,128)S(1)} %copy.147) | copy-start | bytes 7504
  10.3 180.3 %copy-start.45 = (f32[1,256]{1,0:T(1,128)}, f32[1,256]{1,0:T(1,128)S(1)}, u32[]{:S(2)}) copy-start(f32[1,256]{1,0:T(1,128)S(1)} %get-tuple-element.174) | copy-start | bytes 3076
  10.3 204.6 %copy-start.39 = (f32[1,256]{1,0:T(1,128)}, f32[1,256]{1,0:T(1,128)S(1)}, u32[]{:S(2)}) copy-start(f32[1,256]{1,0:T(1,128)S(1)} %get-tuple-element.175) | copy-start | bytes 3076
  11.2 99.1 %copy-start.18 = (f32[3,25,25]{1,2,0:T(8,128)}, f32[3,25,25]{1,2,0:T(8,128)S(1)}, u32[]{:S(2)}) copy-start(f32[3,25,25]{1,2,0:T(8,128)S(1)} %copy.148) | copy-start | bytes 22504
  45.2 63.8 %copy-start.55 = (s32[12,64]{1,0:T(8,128)S(1)}, s32[12,64]{1,0:T(8,128)}, u32[]{:S(2)}) copy-start(s32[12,64]{1,0:T(8,128)} %param.28) | copy-start | bytes 9220
  45.2 63.8 %copy-start.71 = (s32[12]{0:T(128)S(1)}, s32[12]{0:T(128)}, u32[]{:S(2)}) copy-start(s32[12]{0:T(128)} %param.27) | copy-start | bytes 148
  109.6 106.4 %copy-start.25 = (f32[12,64]{1,0:T(8,128)}, f32[12,64]{1,0:T(8,128)S(1)}, u32[]{:S(2)}) copy-start(f32[12,64]{1,0:T(8,128)S(1)} %get-tuple-element.149) | copy-start | bytes 9220
  190.6 24.4 %copy-start.36 = (f32[256]{0:T(256)}, f32[256]{0:T(256)S(1)}, u32[]{:S(2)}) copy-start(f32[256]{0:T(256)S(1)} %get-tuple-element.146) | copy-start | bytes 3076
  208.5 69.1 %collective-permute-start.1 = (bf16[12,4,25,256]{3,1,2,0:T(4,128)(2,1)S(1)}, bf16[12,4,25,256]{3,1,2,0:T(4,128)(2,1)S(1)}, u32[]{:S(2)}, u32[]{:S(2)}) collective-permute-start(bf16[12,4,25,256]{3,1,2,0:T(4,128)(2,1)S(1)} %copy.152), channel_id=1, source_target_pairs={{1,0},{2,1},{3,2},{5,4},{6,5},{7,6},{9,8},{10,9},{11,10},{13,12},{... | collective-permute-start | bytes 1843208 | tf_op jit(solution)/shard_map/ppermute | solution.py:35
  211.1 66.6 %collective-permute-start = (bf16[12,4,25,256]{3,1,2,0:T(4,128)(2,1)}, bf16[12,4,25,256]{3,1,2,0:T(4,128)(2,1)}, u32[]{:S(2)}, u32[]{:S(2)}) collective-permute-start(bf16[12,4,25,256]{3,1,2,0:T(4,128)(2,1)} %copy.151), channel_id=1, source_target_pairs={{0,1},{1,2},{2,3},{4,5},{5,6},{6,7},{8,9},{9,10},{10,11},{12,13},{... | collective-permute-start | bytes 1843208 | tf_op jit(solution)/shard_map/ppermute | solution.py:33
  216.2 53.4 %copy-start.27 = (f32[12,32]{1,0:T(8,128)}, f32[12,32]{1,0:T(8,128)S(1)}, u32[]{:S(2)}) copy-start(f32[12,32]{1,0:T(8,128)S(1)} %slice.148) | copy-start | bytes 4612
  242.7 13.1 copy-start.20
  242.7 14.0 copy-start.21
  242.8 14.9 %copy-start.22 = (f32[128,768]{1,0:T(8,128)S(1)}, f32[128,768]{1,0:T(8,128)}, u32[]{:S(2)}) copy-start(f32[128,768]{1,0:T(8,128)} %param.33) | copy-start | bytes 1179652
  260.4 138.6 %copy-start.5 = (bf16[9,256,256]{2,1,0:T(8,128)(2,1)}, bf16[9,256,256]{2,1,0:T(8,128)(2,1)S(1)}, u32[]{:S(2)}) copy-start(bf16[9,256,256]{2,1,0:T(8,128)(2,1)S(1)} %convert_element_type.59) | copy-start | bytes 3538948
  427.7 51.9 %copy-start.28 = (f32[12,32]{1,0:T(8,128)S(1)}, f32[12,32]{1,0:T(8,128)}, u32[]{:S(2)}) copy-start(f32[12,32]{1,0:T(8,128)} %copy-done.27) | copy-start | bytes 4612
  427.7 51.9 %copy-start.47 = (f32[1,256]{1,0:T(1,128)S(1)}, f32[1,256]{1,0:T(1,128)}, u32[]{:S(2)}) copy-start(f32[1,256]{1,0:T(1,128)} %get-tuple-element.171) | copy-start | bytes 3076
  427.7 51.9 %copy-start.48 = (f32[1,256]{1,0:T(1,128)S(1)}, f32[1,256]{1,0:T(1,128)}, u32[]{:S(2)}) copy-start(f32[1,256]{1,0:T(1,128)} %get-tuple-element.172) | copy-start | bytes 3076
  427.7 52.7 %copy-start.62 = (f32[1,256]{1,0:T(1,128)S(1)}, f32[1,256]{1,0:T(1,128)}, u32[]{:S(2)}) copy-start(f32[1,256]{1,0:T(1,128)} %get-tuple-element.173) | copy-start | bytes 3076
  427.7 52.7 %copy-start.63 = (f32[1,256]{1,0:T(1,128)S(1)}, f32[1,256]{1,0:T(1,128)}, u32[]{:S(2)}) copy-start(f32[1,256]{1,0:T(1,128)} %get-tuple-element.176) | copy-start | bytes 3076
  479.5 21.9 %copy-start.41 = (f32[256]{0:T(256)}, f32[256]{0:T(256)S(1)}, u32[]{:S(2)}) copy-start(f32[256]{0:T(256)S(1)} %get-tuple-element.144) | copy-start | bytes 3076
  479.5 21.9 %copy-start.49 = (f32[256]{0:T(256)}, f32[256]{0:T(256)S(1)}, u32[]{:S(2)}) copy-start(f32[256]{0:T(256)S(1)} %get-tuple-element.145) | copy-start | bytes 3076
  542.0 13.9 copy-start.67
  542.7 13.3 copy-start.53
  542.7 25.3 %slice-start = ((s8[14155776]{0:T(1024)(128)(4,1)}), s8[4194304]{0:T(1024)(128)(4,1)S(1)}, s32[]{:S(2)}) async-start(s8[14155776]{0:T(1024)(128)(4,1)} %bitcast.264), calls=%async_computation.1 | async-start | bytes 8388608
  542.7 25.3 %slice-start.1 = ((s8[14155776]{0:T(1024)(128)(4,1)}), s8[4194304]{0:T(1024)(128)(4,1)S(1)}, s32[]{:S(2)}) async-start(s8[14155776]{0:T(1024)(128)(4,1)} %bitcast.264), calls=%async_computation.2 | async-start | bytes 8388608
  555.9 46.8 %copy-start.2 = (bf16[12,32,25,256]{3,1,2,0:T(8,128)(2,1)}, bf16[12,32,25,256]{3,1,2,0:T(8,128)(2,1)S(1)}, u32[]{:S(2)}) copy-start(bf16[12,32,25,256]{3,1,2,0:T(8,128)(2,1)S(1)} %multiply_convert_fusion.2) | copy-start | bytes 14745604
  565.0 52.9 %collective-permute-start.3 = (bf16[12,2,25,256]{3,1,2,0:T(2,128)(2,1)}, bf16[12,2,25,256]{3,1,2,0:T(2,128)(2,1)S(1)}, u32[]{:S(2)}, u32[]{:S(2)}) collective-permute-start(bf16[12,2,25,256]{3,1,2,0:T(2,128)(2,1)} %get-tuple-element.167), channel_id=1, source_target_pairs={{0,1},{1,2},{2,3},{4,5},{5,6},{6,7},{8,9},{9,10},{10,11},{12,13},{... | collective-permute-start | bytes 921608 | tf_op jit(solution)/shard_map/ppermute | solution.py:33
  566.3 51.6 %collective-permute-start.2 = (bf16[12,2,25,256]{3,1,2,0:T(2,128)(2,1)}, bf16[12,2,25,256]{3,1,2,0:T(2,128)(2,1)}, u32[]{:S(2)}, u32[]{:S(2)}) collective-permute-start(bf16[12,2,25,256]{3,1,2,0:T(2,128)(2,1)} %get-tuple-element.168), channel_id=1, source_target_pairs={{1,0},{2,1},{3,2},{5,4},{6,5},{7,6},{9,8},{10,9},{11,10},{13,12},{... | collective-permute-start | bytes 921608 | tf_op jit(solution)/shard_map/ppermute | solution.py:35
  706.3 15.6 %slice-start.13 = ((s8[4915200]{0:T(1024)(128)(4,1)}), s8[720896]{0:T(1024)(128)(4,1)S(1)}, s32[]{:S(2)}) async-start(s8[4915200]{0:T(1024)(128)(4,1)} %bitcast.272), calls=%async_computation.14 | async-start | bytes 1441792
  731.5 18.8 %slice-start.15 = ((s8[4915200]{0:T(1024)(128)(4,1)}), s8[720896]{0:T(1024)(128)(4,1)S(1)}, s32[]{:S(2)}) async-start(s8[4915200]{0:T(1024)(128)(4,1)} %bitcast.274), calls=%async_computation.16 | async-start | bytes 1441792
  773.1 40.1 %slice-start.4 = ((s8[25165824]{0:T(1024)(128)(4,1)}), s8[4194304]{0:T(1024)(128)(4,1)S(1)}, s32[]{:S(2)}) async-start(s8[25165824]{0:T(1024)(128)(4,1)} %bitcast.266), calls=%async_computation.5 | async-start | bytes 8388608
  773.1 40.1 %slice-start.5 = ((s8[25165824]{0:T(1024)(128)(4,1)}), s8[4194304]{0:T(1024)(128)(4,1)S(1)}, s32[]{:S(2)}) async-start(s8[25165824]{0:T(1024)(128)(4,1)} %bitcast.266), calls=%async_computation.6 | async-start | bytes 8388608
  773.1 40.1 %slice-start.6 = ((s8[25165824]{0:T(1024)(128)(4,1)}), s8[4194304]{0:T(1024)(128)(4,1)S(1)}, s32[]{:S(2)}) async-start(s8[25165824]{0:T(1024)(128)(4,1)} %bitcast.266), calls=%async_computation.7 | async-start | bytes 8388608
  793.5 19.7 %slice-start.7 = ((s8[25165824]{0:T(1024)(128)(4,1)}), s8[4194304]{0:T(1024)(128)(4,1)S(1)}, s32[]{:S(2)}) async-start(s8[25165824]{0:T(1024)(128)(4,1)} %bitcast.266), calls=%async_computation.8 | async-start | bytes 8388608
  793.5 19.7 %slice-start.8 = ((s8[25165824]{0:T(1024)(128)(4,1)}), s8[4194304]{0:T(1024)(128)(4,1)S(1)}, s32[]{:S(2)}) async-start(s8[25165824]{0:T(1024)(128)(4,1)} %bitcast.266), calls=%async_computation.9 | async-start | bytes 8388608
  793.5 19.7 %slice-start.9 = ((s8[25165824]{0:T(1024)(128)(4,1)}), s8[4194304]{0:T(1024)(128)(4,1)S(1)}, s32[]{:S(2)}) async-start(s8[25165824]{0:T(1024)(128)(4,1)} %bitcast.266), calls=%async_computation.10 | async-start | bytes 8388608
  793.5 19.7 %copy-start.26 = (f32[12,64]{1,0:T(8,128)S(1)}, f32[12,64]{1,0:T(8,128)}, u32[]{:S(2)}) copy-start(f32[12,64]{1,0:T(8,128)} %copy-done.25) | copy-start | bytes 9220
  793.5 19.7 %copy-start.37 = (f32[256]{0:T(256)S(1)}, f32[256]{0:T(256)}, u32[]{:S(2)}) copy-start(f32[256]{0:T(256)} %copy-done.36) | copy-start | bytes 3076
  793.5 19.7 %copy-start.40 = (f32[1,256]{1,0:T(1,128)S(1)}, f32[1,256]{1,0:T(1,128)}, u32[]{:S(2)}) copy-start(f32[1,256]{1,0:T(1,128)} %copy-done.39) | copy-start | bytes 3076
  793.5 19.7 %copy-start.44 = (f32[256]{0:T(256)S(1)}, f32[256]{0:T(256)}, u32[]{:S(2)}) copy-start(f32[256]{0:T(256)} %copy-done.43) | copy-start | bytes 3076
  793.5 19.7 %copy-start.46 = (f32[1,256]{1,0:T(1,128)S(1)}, f32[1,256]{1,0:T(1,128)}, u32[]{:S(2)}) copy-start(f32[1,256]{1,0:T(1,128)} %copy-done.45) | copy-start | bytes 3076
  813.3 66.4 %copy-start.8 = (f32[12,64,256]{2,1,0:T(8,128)S(1)}, f32[12,64,256]{2,1,0:T(8,128)}, u32[]{:S(2)}) copy-start(f32[12,64,256]{2,1,0:T(8,128)} %multiply_multiply_fusion.3) | copy-start | bytes 2359300
  879.0 22.5 %copy-start.60 = (f32[256]{0:T(256)}, f32[256]{0:T(256)S(1)}, u32[]{:S(2)}) copy-start(f32[256]{0:T(256)S(1)} %get-tuple-element.105) | copy-start | bytes 3076
  879.6 21.9 %copy-start.24 = (s32[25,25]{0,1:T(8,128)S(1)}, s32[25,25]{0,1:T(8,128)}, u32[]{:S(2)}) copy-start(s32[25,25]{0,1:T(8,128)} %copy-done.23) | copy-start | bytes 7504
  879.6 21.9 %copy-start.57 = (f32[25]{0:T(128)S(1)}, f32[25]{0:T(128)}, u32[]{:S(2)}) copy-start(f32[25]{0:T(128)} %copy-done.56) | copy-start | bytes 304
  879.7 21.9 %copy-start.59 = (s32[3]{0:T(128)S(1)}, s32[3]{0:T(128)}, u32[]{:S(2)}) copy-start(s32[3]{0:T(128)} %copy-done.58) | copy-start | bytes 40
  901.5 28.7 %copy-start.19 = (f32[3,25,25]{1,2,0:T(8,128)S(1)}, f32[3,25,25]{1,2,0:T(8,128)}, u32[]{:S(2)}) copy-start(f32[3,25,25]{1,2,0:T(8,128)} %copy-done.18) | copy-start | bytes 22504
  994.7 41.9 %copy-start.64 = (f32[256]{0:T(256)S(1)}, f32[256]{0:T(256)}, u32[]{:S(2)}) copy-start(f32[256]{0:T(256)} %get-tuple-element.100) | copy-start | bytes 3076
  994.7 83.3 %copy-start.13 = (f32[12,32,256]{2,1,0:T(8,128)S(1)}, f32[12,32,256]{2,1,0:T(8,128)}, u32[]{:S(2)}) copy-start(f32[12,32,256]{2,1,0:T(8,128)} %get-tuple-element.169) | copy-start | bytes 1179652
  994.7 83.3 %copy-start.42 = (f32[256]{0:T(256)S(1)}, f32[256]{0:T(256)}, u32[]{:S(2)}) copy-start(f32[256]{0:T(256)} %copy-done.41) | copy-start | bytes 3076
  994.7 83.3 %copy-start.50 = (f32[256]{0:T(256)S(1)}, f32[256]{0:T(256)}, u32[]{:S(2)}) copy-start(f32[256]{0:T(256)} %copy-done.49) | copy-start | bytes 3076
  994.7 83.3 %copy-start.54 = (f32[256]{0:T(256)S(1)}, f32[256]{0:T(256)}, u32[]{:S(2)}) copy-start(f32[256]{0:T(256)} %copy-done.53) | copy-start | bytes 3076
  1077.9 179.7 %copy-start.29 = (f32[3,25,25]{1,2,0:T(8,128)}, f32[3,25,25]{1,2,0:T(8,128)S(1)}, u32[]{:S(2)}) copy-start(f32[3,25,25]{1,2,0:T(8,128)S(1)} %get-tuple-element.104) | copy-start | bytes 22504
  1128.4 87.2 %copy-start.15 = (f32[128,768]{1,0:T(8,128)S(1)}, f32[128,768]{1,0:T(8,128)}, u32[]{:S(2)}) copy-start(f32[128,768]{1,0:T(8,128)} %param.30) | copy-start | bytes 1179652
  1215.6 23.4 %copy-start.17 = (f32[128,256]{1,0:T(8,128)S(1)}, f32[128,256]{1,0:T(8,128)}, u32[]{:S(2)}) copy-start(f32[128,256]{1,0:T(8,128)} %param.38) | copy-start | bytes 393220
  1247.1 122.7 %copy-start.10 = (f32[128,768]{0,1:T(8,128)S(1)}, f32[128,768]{0,1:T(8,128)}, u32[]{:S(2)}) copy-start(f32[128,768]{0,1:T(8,128)} %copy.181) | copy-start | bytes 1179652
  1247.1 122.7 %copy-start.11 = (f32[128,768]{0,1:T(8,128)S(1)}, f32[128,768]{0,1:T(8,128)}, u32[]{:S(2)}) copy-start(f32[128,768]{0,1:T(8,128)} %copy.178) | copy-start | bytes 1179652
  1247.1 122.7 %copy-start.12 = (f32[128,768]{0,1:T(8,128)S(1)}, f32[128,768]{0,1:T(8,128)}, u32[]{:S(2)}) copy-start(f32[128,768]{0,1:T(8,128)} %copy.179) | copy-start | bytes 1179652
  1355.0 34.5 %copy-start.38 = (f32[6,256]{1,0:T(8,128)S(1)}, f32[6,256]{1,0:T(8,128)}, u32[]{:S(2)}) copy-start(f32[6,256]{1,0:T(8,128)} %param.46) | copy-start | bytes 18436
  1355.0 35.9 %copy-start.7 = (f32[9,256,256]{2,1,0:T(8,128)S(1)}, f32[9,256,256]{2,1,0:T(8,128)}, u32[]{:S(2)}) copy-start(f32[9,256,256]{2,1,0:T(8,128)} %param.34) | copy-start | bytes 7077892
  (42 other events, 315.7 us)
Sparse Core Ops, SparseCore 0:
  1215.7 137.6 all-reduce.7
where the time goes:
time: 1430 us; the launch traced here: 1410 us
  local copies, waits for them, and re-layouts  611 us (43%)
  matrix products  269 us (19%)
  blocking collectives  216 us (15%)
  other arithmetic  188 us (13%)
  waiting for transfers between devices  95.2 us (7%)
  between operations  21.4 us (1%)
    psum x1, waiting for transfers between devices, shards(): lax.psum((graph_grad, temporal_grad, shortcut_grad, edge_grad), ('batch',...  95.2 us
    dot_general x1, local copies, waits for them, and re-layouts, shards(): jnp.einsum('rd,cd->rc', mixed_flat, weight_low, preferred_element_type=jn...  87.2 us
    convert_element_type x2, local copies, waits for them, and re-layouts, shards(): mixed_grad = jnp.einsum('ntwc,kvw->ntvkc', hidden_grad, graph_low, prefer...  83.5 us
    psum x2, blocking collectives, shards(): lax.psum((back_sum, back_conv, back_short), ('batch', 'tm'))  82 us
    reshape x9, local copies, waits for them, and re-layouts, shards(): padded[:, tap_index:tap_index + 2 * half_frames:2].reshape(-1, C_OUT)  78.8 us
    unnamed x229, local copies, waits for them, and re-layouts  68.7 us
    reshape x1, local copies, waits for them, and re-layouts, shards(): mixed_rows.reshape(clips_here, frames_here, JOINTS, SUBSETS, C_OUT)  63.8 us
    psum x1, blocking collectives, shards(): lax.psum((sum_in, square_in, count_here), ('batch', 'tm'))  51.5 us
  transfers between devices with their start and end apart: 5, of which 1 were waited for; matrix products, arithmetic and copies ran while one was open for 11% of the time, Pallas kernels for 0%

commit v1 on v0

v1 whole, which is shorter than its diff:
```python
import functools

import jax
import jax.numpy as jnp
from jax import lax
from jax.experimental import pallas as pl
from jax.experimental.pallas import tpu as pltpu
from jax.sharding import PartitionSpec as P

C_IN = 128
C_OUT = 256
JOINTS = 25
SUBSETS = 3
TAPS = 9
GROUP = 8
PHASES = 8
UNITS = 2 * JOINTS
ROWS = UNITS * GROUP
HALF_ROWS = JOINTS * GROUP
HALF = C_IN
CUT = 5

f32 = jnp.float32
bf16 = jnp.bfloat16

norm_epsilon = 1e-05
beta_first = 0.9
beta_second = 0.999
adam_epsilon = 1e-08
clip_limit = 1.0
average_decay = 0.9
rate_matrix = 0.05
rate_small = 0.3
decay_matrix = 0.01
steps_taken = 3.0


def params(**more):
    return pltpu.CompilerParams(
        vmem_limit_bytes=60 * 2**20, dimension_semantics=("arbitrary",), **more
    )


def adjacency(subsets):
    linked = (subsets > 0).astype(f32)
    degree = jnp.sum(linked, axis=0)
    labels = jnp.arange(SUBSETS, dtype=jnp.int32) + 1
    chosen = (subsets[None, :, :] == labels[:, None, None]).astype(f32)
    return chosen / degree[None, None, :]


def adam_update(weight, moment, square, average, gradient, factor, rate, decay):
    fix_first = 1.0 - beta_first**steps_taken
    fix_second = 1.0 - beta_second**steps_taken
    clipped = gradient * factor
    moment_new = beta_first * moment + (1.0 - beta_first) * clipped
    square_new = beta_second * square + (1.0 - beta_second) * clipped * clipped
    stepped = moment_new / fix_first / (jnp.sqrt(square_new / fix_second) + adam_epsilon)
    weight_new = weight - rate * (stepped + decay * weight)
    average_new = average_decay * average + (1.0 - average_decay) * weight_new
    return (weight_new, moment_new, square_new, average_new)


def dot(a, b):
    return jnp.dot(a, b, preferred_element_type=f32)


def dot_nt(a, b):
    return lax.dot_general(a, b, (((1,), (1,)), ((), ())), preferred_element_type=f32)


def dot_tn(a, b):
    return lax.dot_general(a, b, (((0,), (0,)), ((), ())), preferred_element_type=f32)


def fold(values):
    return jnp.sum(values.reshape(-1, GROUP, values.shape[-1]), axis=0)


def first_moments(stats, norm):
    count_in = stats[4:5]
    mean = stats[0:1] / count_in
    rstd = lax.rsqrt(stats[1:2] / count_in - mean * mean + norm_epsilon)
    return mean, rstd, norm[0:1] * rstd, norm[1:2] - norm[0:1] * rstd * mean


def mix_rows(parts, scales, kron_ref, pad_ref):
    wide = jnp.concatenate([part.reshape(HALF_ROWS, C_IN) for part in parts], axis=1)
    pad_ref[0:HALF_ROWS, :] = wide.astype(bf16)
    mixed = dot(kron_ref[...], pad_ref[...])
    sides = []
    for side in range(2):
        lanes = slice(side * HALF, (side + 1) * HALF)
        sides.append(
            jnp.concatenate(
                [
                    parts[side] * scales,
                    mixed[0:HALF_ROWS, lanes].reshape(JOINTS, GROUP, C_IN),
                    mixed[HALF_ROWS : 2 * HALF_ROWS, lanes].reshape(JOINTS, GROUP, C_IN),
                ],
                axis=2,
            )
        )
    return jnp.concatenate(sides, axis=1).reshape(ROWS, SUBSETS * C_IN).astype(bf16)


def graph_forward(
    x_ref, m_ref, kron_ref, own_ref, wg_ref, ws_ref,
    xg_ref, xq_ref, xe_ref, h_ref, st_ref,
    xs, sums, counts,
):
    step = pl.program_id(0)

    @pl.when(step == 0)
    def _():
        sums[...] = jnp.zeros_like(sums)
        counts[...] = jnp.zeros_like(counts)

    for side in range(2):
        for joint in range(JOINTS):
            xs[side, joint] = x_ref[side, joint].astype(f32)
    own = own_ref[...]
    for c in range(PHASES):
        mask = m_ref[0, c]
        parts = [
            xs[side, :, pl.ds(c, GROUP, stride=PHASES), :]
            * mask[side * GROUP : (side + 1) * GROUP][None]
            for side in range(2)
        ]
        xq_ref[0, c, HALF_ROWS:, :] = jnp.zeros((C_OUT - HALF_ROWS, C_OUT), bf16)
        xg = mix_rows(parts, own, kron_ref, xq_ref.at[0, c])
        xg_ref[0, c] = xg
        hidden = dot(xg, wg_ref[...])
        h_ref[0, c] = hidden.astype(bf16)
        sums[0] += fold(hidden)
        sums[1] += fold(hidden * hidden)
        counts[0] += mask
        if c % 2 == 0:
            counts[1] += mask
            even = jnp.concatenate(parts, axis=1).reshape(ROWS, C_IN).astype(bf16)
            xe_ref[0, c // 2] = even
            short = dot(even, ws_ref[...])
            sums[2] += fold(short)
            sums[3] += fold(short * short)

    @pl.when(step == pl.num_programs(0) - 1)
    def _():
        rows = [jnp.sum(sums[k], axis=0, keepdims=True) for k in range(4)]
        for k in range(2):
            total = JOINTS * jnp.sum(counts[k], axis=0, keepdims=True)
            rows.append(jnp.concatenate([total, total], axis=1))
        rows.append(jnp.zeros((2, C_OUT), f32))
        st_ref[...] = jnp.concatenate(rows, axis=0)


def insert_and_roll(tiles, fill, side):
    sub = lax.broadcasted_iota(jnp.int32, tiles.shape, 1)
    joined = jnp.where(sub == side, fill, tiles)
    return pltpu.roll(joined, 1 if side == 7 else GROUP - 1, 1)


def conv_forward(
    h_ref, xh_ref, m_ref, mh_ref, st_ref, norm_ref, kron_ref, own_ref, wg_ref, taps_ref,
    a_ref, conv_ref, out_ref,
    pad, rims, fills, sums,
):
    step = pl.program_id(0)

    @pl.when(step == 0)
    def _():
        sums[...] = jnp.zeros_like(sums)
        pad[...] = jnp.zeros_like(pad)

    _, _, scale, shift = first_moments(st_ref[...], norm_ref[...])
    scale, shift = 0.5 * scale, 0.5 * shift

    def activate(values, mask):
        half = values * scale + shift
        return (half + half * jnp.tanh(half)).reshape(-1, 2 * GROUP, C_OUT) * mask

    def wide(mask):
        return jnp.concatenate([mask, mask], axis=1)[None]

    rim_mask = mh_ref[0]
    parts = [
        xh_ref[side] * rim_mask[side * GROUP : (side + 1) * GROUP][None] for side in range(2)
    ]
    rim_hidden = dot(mix_rows(parts, own_ref[...], kron_ref, pad), wg_ref[...])
    rim_active = activate(rim_hidden, wide(rim_mask)).reshape(ROWS, C_OUT)
    for lane in range(2):
        rims[lane] = rim_active[:, lane * HALF : (lane + 1) * HALF]
    for p in range(2):
        for q in range(2):
            for lane in range(2):
                fills[2 * p + q, lane, pl.ds(7, UNITS, stride=GROUP), :] = rims[
                    lane, pl.ds(2 * q + p, UNITS, stride=GROUP), :
                ]
                fills[2 * p + q, lane, pl.ds(0, UNITS, stride=GROUP), :] = rims[
                    lane, pl.ds(4 + 2 * q + p, UNITS, stride=GROUP), :
                ]

    for c in range(PHASES):
        p, q = c % 2, c // 2
        mask = wide(m_ref[0, c])
        for start in range(0, JOINTS, CUT):
            rows = slice(start * 2 * GROUP, (start + CUT) * 2 * GROUP)
            active = activate(h_ref[0, c, rows, :].astype(f32), mask)
            a_ref[0, p, q + 2, rows, :] = active.reshape(-1, C_OUT).astype(bf16)
            if p == 1 and q == 1:
                continue
            tiles = active.reshape(-1, GROUP, C_OUT)
            fill = jnp.concatenate(
                [fills[2 * p + q % 2, lane, rows, :] for lane in range(2)], axis=1
            ).reshape(-1, GROUP, C_OUT)
            moved = insert_and_roll(tiles, fill, 7 if q >= 2 else 0)
            at = q - 2 if q >= 2 else q + 6
            a_ref[0, p, at, rows, :] = moved.reshape(-1, C_OUT).astype(bf16)

    total = None
    for j in range(TAPS):
        window = a_ref[0, j % 2, j // 2 : j // 2 + 4].reshape(4 * ROWS, C_OUT)
        part = dot(window, taps_ref[j])
        total = part if total is None else total + part
    conv_ref[0] = total.reshape(4, ROWS, C_OUT)
    for q in range(4):
        block = total[q * ROWS : (q + 1) * ROWS].reshape(JOINTS, 2 * GROUP, C_OUT)
        live = block * wide(m_ref[0, 2 * q])
        sums[0] += fold(live)
        sums[1] += fold(live * block)

    @pl.when(step == pl.num_programs(0) - 1)
    def _():
        rows = [jnp.sum(sums[k], axis=0, keepdims=True) for k in range(2)]
        rows.append(jnp.zeros((6, C_OUT), f32))
        out_ref[...] = jnp.concatenate(rows, axis=0)


def second_moments(stats, conv_stats):
    count_out = stats[5:6]
    mean_conv = conv_stats[0:1] / count_out
    rstd_conv = lax.rsqrt(conv_stats[1:2] / count_out - mean_conv * mean_conv + norm_epsilon)
    mean_short = stats[2:3] / count_out
    rstd_short = lax.rsqrt(stats[3:4] / count_out - mean_short * mean_short + norm_epsilon)
    return mean_conv, rstd_conv, mean_short, rstd_short


def output_part(
    conv_ref, xe_ref, cot_ref, m_ref, st_ref, cs_ref, norm_ref, ws_ref,
    o_ref, up_ref, out_ref,
    cots, outs, sums,
):
    step = pl.program_id(0)

    @pl.when(step == 0)
    def _():
        sums[...] = jnp.zeros_like(sums)

    norm = norm_ref[...]
    mean_conv, rstd_conv, mean_short, rstd_short = second_moments(st_ref[...], cs_ref[...])
    scale_conv = 0.5 * norm[2:3] * rstd_conv
    scale_short = 0.5 * norm[4:5] * rstd_short
    shift = 0.5 * (norm[3:4] + norm[5:6]) - scale_conv * mean_conv - scale_short * mean_short
    for side in range(2):
        for joint in range(JOINTS):
            for lane in range(2):
                cots[side, lane, joint] = cot_ref[
                    side, joint, :, lane * HALF : (lane + 1) * HALF
                ].astype(f32)
    for q in range(4):
        mask = m_ref[0, 2 * q]
        mask = jnp.concatenate([mask, mask], axis=1)[None]
        short_all = dot(xe_ref[0, q], ws_ref[...])
        for start in range(0, JOINTS, CUT):
            rows = slice(start * 2 * GROUP, (start + CUT) * 2 * GROUP)
            conv = conv_ref[0, q, rows, :]
            short = short_all[rows]
            half = conv * scale_conv + short * scale_short + shift
            turn = jnp.tanh(half)
            grow = (0.5 + 0.5 * turn).reshape(CUT, 2 * GROUP, C_OUT) * mask
            half = half.reshape(CUT, 2 * GROUP, C_OUT)
            turn = turn.reshape(CUT, 2 * GROUP, C_OUT)
            result = (half + half) * grow
            slope = grow + grow * (half - half * turn)
            cot = jnp.concatenate(
                [
                    jnp.concatenate(
                        [
                            cots[side, lane, start : start + CUT, pl.ds(q, GROUP, stride=4), :]
                            for lane in range(2)
                        ],
                        axis=2,
                    )
                    for side in range(2)
                ],
                axis=1,
            )
            for side in range(2):
                for lane in range(2):
                    outs[side, lane, start : start + CUT, pl.ds(q, GROUP, stride=4), :] = result[
                        :, side * GROUP : (side + 1) * GROUP, lane * HALF : (lane + 1) * HALF
                    ]
            up = (cot * slope).reshape(-1, C_OUT)
            up_ref[0, q, rows, :] = up
            sums[0] += fold(up)
            sums[1] += fold(up * conv)
            sums[2] += fold(up * short)
    for side in range(2):
        for joint in range(JOINTS):
            for lane in range(2):
                o_ref[side, joint, :, lane * HALF : (lane + 1) * HALF] = outs[
                    side, lane, joint
                ].astype(bf16)

    @pl.when(step == pl.num_programs(0) - 1)
    def _():
        rows = [jnp.sum(sums[k], axis=0, keepdims=True) for k in range(3)]
        rows.append(jnp.zeros((5, C_OUT), f32))
        out_ref[...] = jnp.concatenate(rows, axis=0)


def back_totals(back, moments):
    mean_conv, rstd_conv, mean_short, rstd_short = moments
    back_sum = back[0:1]
    back_conv = rstd_conv * (back[1:2] - mean_conv * back_sum)
    back_short = rstd_short * (back[2:3] - mean_short * back_sum)
    return back_sum, back_conv, back_short


def weight_part(
    conv_ref, up_ref, xe_ref, a_ref, m_ref, st_ref, cs_ref, bk_ref, norm_ref, ws_ref,
    cg_ref, sg_ref, lo_ref, hi_ref, tg_ref, shg_ref,
    turned, edges,
):
    step = pl.program_id(0)

    @pl.when(step == 0)
    def _():
        tg_ref[...] = jnp.zeros_like(tg_ref)
        shg_ref[...] = jnp.zeros_like(shg_ref)

    norm = norm_ref[...]
    stats = st_ref[...]
    moments = second_moments(stats, cs_ref[...])
    mean_conv, rstd_conv, mean_short, rstd_short = moments
    back_sum, back_conv, back_short = back_totals(bk_ref[...], moments)
    count_out = stats[5:6]

    def terms(gain, mean, rstd, back):
        lead = gain * rstd
        slope = lead * rstd * back / count_out
        return lead, slope, lead * back_sum / count_out - slope * mean

    lead_c, slope_c, shift_c = terms(norm[2:3], mean_conv, rstd_conv, back_conv)
    lead_s, slope_s, shift_s = terms(norm[4:5], mean_short, rstd_short, back_short)
    for q in range(4):
        mask = m_ref[0, 2 * q]
        mask = jnp.concatenate([mask, mask], axis=1)[None]
        short_all = dot(xe_ref[0, q], ws_ref[...])
        for start in range(0, JOINTS, CUT):
            rows = slice(start * 2 * GROUP, (start + CUT) * 2 * GROUP)
            up = up_ref[0, q, rows, :]

            def masked(values):
                return (values.reshape(CUT, 2 * GROUP, C_OUT) * mask).reshape(-1, C_OUT)

            cg = up * lead_c - masked(conv_ref[0, q, rows, :] * slope_c + shift_c)
            cg_ref[0, q, rows, :] = cg.astype(bf16)
            for lane in range(2):
                edges[lane, rows, :] = cg[:, lane * HALF : (lane + 1) * HALF]
            sg = up * lead_s - masked(short_all[rows] * slope_s + shift_s)
            sg_ref[0, q, rows, :] = sg.astype(bf16)
        for lane in range(2):
            at = slice(lane * HALF, (lane + 1) * HALF)
            if q < 2:
                lo_ref[0, q, :, at] = edges[lane, pl.ds(0, UNITS, stride=GROUP), :].astype(bf16)
            else:
                hi_ref[0, q - 2, :, at] = edges[lane, pl.ds(7, UNITS, stride=GROUP), :].astype(bf16)
    turned[...] = cg_ref[0].reshape(4 * ROWS, C_OUT).T
    for j in range(TAPS):
        window = a_ref[0, j % 2, j // 2 : j // 2 + 4].reshape(4 * ROWS, C_OUT)
        tg_ref[j] += dot(turned[...], window)
    shg_ref[...] += dot_tn(
        xe_ref[0].reshape(4 * ROWS, C_IN), sg_ref[0].reshape(4 * ROWS, C_OUT)
    )


def conv_back(
    cg_ref, left_ref, right_ref, taps_ref, h_ref, m_ref, st_ref, norm_ref,
    fg_ref, out_ref,
    fills, ext, sums,
):
    step = pl.program_id(0)

    @pl.when(step == 0)
    def _():
        sums[...] = jnp.zeros_like(sums)

    _, _, scale, shift = first_moments(st_ref[...], norm_ref[...])
    scale, shift = 0.5 * scale, 0.5 * shift
    for q in range(2):
        for lane in range(2):
            at = slice(lane * HALF, (lane + 1) * HALF)
            fills[q, lane, pl.ds(7, UNITS, stride=GROUP), :] = left_ref[0, q, :, at].astype(f32)
            fills[q, lane, pl.ds(0, UNITS, stride=GROUP), :] = right_ref[0, q, :, at].astype(f32)
    for q in range(4):
        ext[q + 2] = cg_ref[0, q]
        for start in range(0, JOINTS, CUT):
            rows = slice(start * 2 * GROUP, (start + CUT) * 2 * GROUP)
            tiles = cg_ref[0, q, rows, :].astype(f32).reshape(-1, GROUP, C_OUT)
            fill = jnp.concatenate([fills[q % 2, lane, rows, :] for lane in range(2)], axis=1)
            fill = fill.reshape(-1, GROUP, C_OUT)
            moved = insert_and_roll(tiles, fill, 7 if q >= 2 else 0)
            at = q - 2 if q >= 2 else q + 6
            ext[at, rows, :] = moved.reshape(-1, C_OUT).astype(bf16)
    for p in range(2):
        total = None
        for i in range(5 - p):
            window = ext[4 - i : 8 - i].reshape(4 * ROWS, C_OUT)
            part = dot_nt(window, taps_ref[2 * i + p])
            total = part if total is None else total + part
        for q in range(4):
            c = 2 * q + p
            mask = 0.5 * m_ref[0, c]
            mask = jnp.concatenate([mask, mask], axis=1)[None]
            for start in range(0, JOINTS, CUT):
                rows = slice(start * 2 * GROUP, (start + CUT) * 2 * GROUP)
                hidden = h_ref[0, c, rows, :].astype(f32)
                half = hidden * scale + shift
                turn = jnp.tanh(half)
                slope = (1.0 + turn) * (1.0 + (half - half * turn))
                slope = (slope.reshape(CUT, 2 * GROUP, C_OUT) * mask).reshape(-1, C_OUT)
                grad = total[q * ROWS + rows.start : q * ROWS + rows.stop] * slope
                fg_ref[0, c, rows, :] = grad
                sums[0] += fold(grad)
                sums[1] += fold(grad * hidden)

    @pl.when(step == pl.num_programs(0) - 1)
    def _():
        rows = [jnp.sum(sums[k], axis=0, keepdims=True) for k in range(2)]
        rows.append(jnp.zeros((6, C_OUT), f32))
        out_ref[...] = jnp.concatenate(rows, axis=0)


def graph_back(
    fg_ref, h_ref, xg_ref, xq_ref, sg_ref, m_ref, st_ref, fs_ref, norm_ref,
    wg_ref, ws_ref, kront_ref, own_ref,
    ig_ref, gg_ref, eg_ref, own_grad_ref,
    hg_all, spread, natural,
):
    step = pl.program_id(0)

    @pl.when(step == 0)
    def _():
        gg_ref[...] = jnp.zeros_like(gg_ref)
        eg_ref[...] = jnp.zeros_like(eg_ref)
        own_grad_ref[...] = jnp.zeros_like(own_grad_ref)
        spread[...] = jnp.zeros_like(spread)

    norm = norm_ref[...]
    stats = st_ref[...]
    mean, rstd, _, _ = first_moments(stats, norm)
    count_in = stats[4:5]
    back_sum = fs_ref[0:1]
    back_norm = rstd * (fs_ref[1:2] - mean * back_sum)
    lead = norm[0:1] * rstd
    slope = lead * rstd * back_norm / count_in
    shift = lead * back_sum / count_in - slope * mean
    own = own_ref[...]
    for c in range(PHASES):
        mask = m_ref[0, c]
        mask = jnp.concatenate([mask, mask], axis=1)[None]
        for start in range(0, JOINTS, CUT):
            rows = slice(start * 2 * GROUP, (start + CUT) * 2 * GROUP)
            hidden = h_ref[0, c, rows, :].astype(f32)
            taken = ((hidden * slope + shift).reshape(CUT, 2 * GROUP, C_OUT) * mask).reshape(
                -1, C_OUT
            )
            hg_all[c, rows, :] = (fg_ref[0, c, rows, :] * lead - taken).astype(bf16)
        back = dot(hg_all[c], wg_ref[...]).reshape(JOINTS, 2 * GROUP, SUBSETS * C_IN)

        def side_by_side(values):
            return jnp.concatenate([values[:, 0:GROUP], values[:, GROUP : 2 * GROUP]], axis=2)

        for k in range(2):
            lanes = slice((k + 1) * C_IN, (k + 2) * C_IN)
            spread[k, 0:HALF_ROWS, :] = (
                side_by_side(back[:, :, lanes]).reshape(HALF_ROWS, 2 * C_IN).astype(bf16)
            )
        direct = side_by_side(back[:, :, 0:C_IN])
        both = spread[...].reshape(2 * C_OUT, C_OUT)
        whole = dot(kront_ref[...], both)
        result = whole.reshape(JOINTS, GROUP, 2 * C_IN) + direct * jnp.concatenate([own, own], axis=2)
        if c % 2 == 0:
            short = dot(sg_ref[0, c // 2], ws_ref[...]).reshape(JOINTS, 2 * GROUP, C_IN)
            result = result + side_by_side(short)
        for side in range(2):
            natural[side, :, pl.ds(c, GROUP, stride=PHASES), :] = result[
                :, :, side * C_IN : (side + 1) * C_IN
            ]
        eg_ref[...] += dot_nt(both, xq_ref[0, c])
        seen = xq_ref[0, c, 0:HALF_ROWS, :].astype(f32).reshape(JOINTS, GROUP, 2 * C_IN)
        own_grad_ref[...] += seen * direct
    for side in range(2):
        for joint in range(JOINTS):
            ig_ref[side, joint] = natural[side, joint].astype(bf16)
    gg_ref[...] += dot_tn(
        xg_ref[0].reshape(PHASES * ROWS, SUBSETS * C_IN), hg_all[...].reshape(PHASES * ROWS, C_OUT)
    )


def whole_spec(shape):
    return pl.BlockSpec(shape, lambda i: (0,) * len(shape))


def lead_spec(shape):
    return pl.BlockSpec(shape, lambda i: (i,) + (0,) * (len(shape) - 1))


def call(body, pairs, ins, outs, scratch, name):
    in_specs = [
        whole_spec(array.shape) if block is None else lead_spec(block) for array, block in ins
    ]
    out_specs = [whole_spec(shape) if block is None else lead_spec(block) for shape, _, block in outs]
    return pl.pallas_call(
        body,
        grid=(pairs,),
        in_specs=in_specs,
        out_specs=out_specs,
        out_shape=[jax.ShapeDtypeStruct(shape, kind) for shape, kind, _ in outs],
        scratch_shapes=scratch,
        compiler_params=params(),
        name=name,
    )(*[array for array, _ in ins])


def shards(
    inputs, cotangent, lengths, frame_mask, subsets,
    graph_weight, graph_moment, graph_square, graph_average,
    temporal_weight, temporal_moment, temporal_square, temporal_average,
    shortcut_weight, shortcut_moment, shortcut_square, shortcut_average,
    edge_weight, edge_moment, edge_square, edge_average,
    norm_params, norm_moment, norm_square, norm_average,
):
    clips = inputs.shape[0]
    frames = inputs.shape[1]
    pairs = clips // 2
    tm_size = lax.axis_size("tm")
    forward = [(i, i + 1) for i in range(tm_size - 1)]
    backward = [(i + 1, i) for i in range(tm_size - 1)]
    first_frame = lax.axis_index("tm") * frames
    frame_ids = first_frame + jnp.arange(frames, dtype=jnp.int32)
    mask_in = ((frame_ids[None, :] < lengths[:, None]) & (frame_mask > 0)).astype(f32)

    natural = jnp.transpose(inputs, (0, 2, 1, 3))
    before = lax.ppermute(natural[:, :, -4:], "tm", forward)
    after = lax.ppermute(natural[:, :, :4], "tm", backward)
    rim_x = jnp.concatenate([before, after], axis=2).astype(f32)
    mask_before = lax.ppermute(mask_in[:, -4:], "tm", forward)
    mask_after = lax.ppermute(mask_in[:, :4], "tm", backward)
    rim_mask = jnp.concatenate([mask_before, mask_after], axis=1).reshape(pairs, 2 * GROUP)
    rim_mask = jnp.broadcast_to(rim_mask[:, :, None], (pairs, 2 * GROUP, 128))
    masks = mask_in.reshape(pairs, 2, GROUP, PHASES).transpose(0, 3, 1, 2)
    masks = jnp.broadcast_to(
        masks.reshape(pairs, PHASES, 2 * GROUP)[..., None], (pairs, PHASES, 2 * GROUP, 128)
    )

    graph_mask = adjacency(subsets)
    graph_low = (graph_mask * edge_weight).astype(bf16)
    same = jnp.eye(GROUP, dtype=bf16)
    kron = graph_low[1:].transpose(0, 2, 1)[:, :, None, :, None] * same[None, None, :, None, :]
    kron = kron.reshape(2 * HALF_ROWS, HALF_ROWS)
    kron = jnp.pad(kron, ((0, 0), (0, C_OUT - HALF_ROWS)))
    kront = graph_low[1:].transpose(1, 0, 2)[:, None, :, :, None] * same[None, :, None, None, :]
    kront = kront.reshape(HALF_ROWS, 2, HALF_ROWS)
    kront = jnp.pad(kront, ((0, 0), (0, 0), (0, C_OUT - HALF_ROWS))).reshape(HALF_ROWS, 2 * C_OUT)
    own = jnp.diagonal(graph_low[0]).astype(f32)
    own = jnp.broadcast_to(own[:, None, None], (JOINTS, GROUP, C_IN))
    wg = graph_weight.astype(bf16).reshape(C_IN, SUBSETS, C_OUT).transpose(1, 0, 2)
    wg = wg.reshape(SUBSETS * C_IN, C_OUT)
    ws = shortcut_weight.astype(bf16)
    taps = temporal_weight.astype(bf16)

    x_block = (2, JOINTS, frames, C_IN)
    mask_block = (1, PHASES, 2 * GROUP, 128)
    wide_block = (1, PHASES, ROWS, C_OUT)
    out_block = (1, 4, ROWS, C_OUT)
    xe_block = (1, 4, ROWS, C_IN)
    a_block = (1, 2, 8, ROWS, C_OUT)
    rim_block = (1, 2, UNITS, C_OUT)
    small = (8, C_OUT)

    def full(block):
        return (pairs,) + block[1:]

    xg_block = (1, PHASES, ROWS, SUBSETS * C_IN)
    xq_block = (1, PHASES, C_OUT, C_OUT)
    xg, xq, xe, hidden, stats = call(
        graph_forward,
        pairs,
        [(natural, x_block), (masks, mask_block), (kron, None), (own, None), (wg, None), (ws, None)],
        [
            (full(xg_block), bf16, xg_block),
            (full(xq_block), bf16, xq_block),
            (full(xe_block), bf16, xe_block),
            (full(wide_block), bf16, wide_block),
            (small, f32, None),
        ],
        [
            pltpu.VMEM((2, JOINTS, frames, C_IN), f32),
            pltpu.VMEM((4, GROUP, C_OUT), f32),
            pltpu.VMEM((2, 2 * GROUP, 128), f32),
        ],
        "graph_forward",
    )
    stats = lax.psum(stats, ("batch", "tm"))

    active, conv, conv_stats = call(
        conv_forward,
        pairs,
        [
            (hidden, wide_block),
            (rim_x, (2, JOINTS, GROUP, C_IN)),
            (masks, mask_block),
            (rim_mask, (1, 2 * GROUP, 128)),
            (stats, None),
            (norm_params, None),
            (kron, None),
            (own, None),
            (wg, None),
            (taps, None),
        ],
        [
            (full(a_block), bf16, a_block),
            (full(out_block), f32, out_block),
            (small, f32, None),
        ],
        [
            pltpu.VMEM((C_OUT, C_OUT), bf16),
            pltpu.VMEM((2, ROWS, HALF), f32),
            pltpu.VMEM((4, 2, ROWS, HALF), f32),
            pltpu.VMEM((2, GROUP, C_OUT), f32),
        ],
        "conv_forward",
    )
    conv_stats = lax.psum(conv_stats, ("batch", "tm"))

    cot = jnp.transpose(cotangent, (0, 2, 1, 3))
    cot_block = (2, JOINTS, frames // 2, C_OUT)
    outputs, upstream, back = call(
        output_part,
        pairs,
        [
            (conv, out_block),
            (xe, xe_block),
            (cot, cot_block),
            (masks, mask_block),
            (stats, None),
            (conv_stats, None),
            (norm_params, None),
            (ws, None),
        ],
        [
            (cot.shape, bf16, cot_block),
            (full(out_block), f32, out_block),
            (small, f32, None),
        ],
        [
            pltpu.VMEM((2, 2, JOINTS, frames // 2, HALF), f32),
            pltpu.VMEM((2, 2, JOINTS, frames // 2, HALF), f32),
            pltpu.VMEM((3, GROUP, C_OUT), f32),
        ],
        "output_part",
    )
    back = lax.psum(back, ("batch", "tm"))

    conv_grad, short_grad, low_rim, high_rim, temporal_turned, shortcut_grad = call(
        weight_part,
        pairs,
        [
            (conv, out_block),
            (upstream, out_block),
            (xe, xe_block),
            (active, a_block),
            (masks, mask_block),
            (stats, None),
            (conv_stats, None),
            (back, None),
            (norm_params, None),
            (ws, None),
        ],
        [
            (full(out_block), bf16, out_block),
            (full(out_block), bf16, out_block),
            (full(rim_block), bf16, rim_block),
            (full(rim_block), bf16, rim_block),
            ((TAPS, C_OUT, C_OUT), f32, None),
            ((C_IN, C_OUT), f32, None),
        ],
        [
            pltpu.VMEM((C_OUT, 4 * ROWS), bf16),
            pltpu.VMEM((2, ROWS, HALF), f32),
        ],
        "weight_part",
    )
    left_rim = lax.ppermute(high_rim, "tm", forward)
    right_rim = lax.ppermute(low_rim, "tm", backward)

    first_grad, first_sums = call(
        conv_back,
        pairs,
        [
            (conv_grad, out_block),
            (left_rim, rim_block),
            (right_rim, rim_block),
            (taps, None),
            (hidden, wide_block),
            (masks, mask_block),
            (stats, None),
            (norm_params, None),
        ],
        [
            (full(wide_block), f32, wide_block),
            (small, f32, None),
        ],
        [
            pltpu.VMEM((2, 2, ROWS, HALF), f32),
            pltpu.VMEM((8, ROWS, C_OUT), bf16),
            pltpu.VMEM((2, GROUP, C_OUT), f32),
        ],
        "conv_back",
    )
    first_sums = lax.psum(first_sums, ("batch", "tm"))

    input_grad, graph_turned, edge_wide, own_wide = call(
        graph_back,
        pairs,
        [
            (first_grad, wide_block),
            (hidden, wide_block),
            (xg, xg_block),
            (xq, xq_block),
            (short_grad, out_block),
            (masks, mask_block),
            (stats, None),
            (first_sums, None),
            (norm_params, None),
            (wg.T, None),
            (ws.T, None),
            (kront, None),
            (own, None),
        ],
        [
            (natural.shape, bf16, x_block),
            ((SUBSETS * C_IN, C_OUT), f32, None),
            ((2 * C_OUT, C_OUT), f32, None),
            ((JOINTS, GROUP, 2 * C_IN), f32, None),
        ],
        [
            pltpu.VMEM((PHASES, ROWS, C_OUT), bf16),
            pltpu.VMEM((2, C_OUT, C_OUT), bf16),
            pltpu.VMEM((2, JOINTS, frames, C_IN), f32),
        ],
        "graph_back",
    )
    temporal_grad = jnp.swapaxes(temporal_turned, 1, 2)
    graph_grad = graph_turned.reshape(SUBSETS, C_IN, C_OUT).transpose(1, 0, 2)
    graph_grad = graph_grad.reshape(C_IN, SUBSETS * C_OUT)
    edge_wide = edge_wide.reshape(2, C_OUT, C_OUT)[:, :HALF_ROWS, :HALF_ROWS]
    edge_wide = edge_wide.reshape(2, JOINTS, GROUP, JOINTS, GROUP)
    edge_off = jnp.einsum("kwrvr->kvw", edge_wide)
    edge_own = jnp.diag(jnp.sum(own_wide, axis=(1, 2)))
    edge_grad = jnp.concatenate([edge_own[None], edge_off], axis=0) * graph_mask
    graph_sum, temporal_sum, shortcut_sum, edge_sum = lax.psum(
        (graph_grad, temporal_grad, shortcut_grad, edge_grad), ("batch", "tm")
    )

    mean, rstd, _, _ = first_moments(stats, norm_params)
    back_first_sum = first_sums[0:1]
    back_first_norm = rstd * (first_sums[1:2] - mean * back_first_sum)
    back_sum, back_conv, back_short = back_totals(back, second_moments(stats, conv_stats))
    norm_grad = jnp.concatenate(
        [back_first_norm, back_first_sum, back_conv, back_sum, back_short, back_sum], axis=0
    )
    squares_total = (
        jnp.sum(graph_sum * graph_sum)
        + jnp.sum(temporal_sum * temporal_sum)
        + jnp.sum(shortcut_sum * shortcut_sum)
        + jnp.sum(edge_sum * edge_sum)
        + jnp.sum(norm_grad * norm_grad)
    )
    norm_total = jnp.sqrt(squares_total)
    factor = jnp.minimum(1.0, clip_limit / (norm_total + 1e-06))
    graph_new = adam_update(
        graph_weight, graph_moment, graph_square, graph_average,
        graph_sum, factor, rate_matrix, decay_matrix,
    )
    temporal_new = adam_update(
        temporal_weight, temporal_moment, temporal_square, temporal_average,
        temporal_sum, factor, rate_matrix, decay_matrix,
    )
    shortcut_new = adam_update(
        shortcut_weight, shortcut_moment, shortcut_square, shortcut_average,
        shortcut_sum, factor, rate_matrix, decay_matrix,
    )
    edge_new = adam_update(
        edge_weight, edge_moment, edge_square, edge_average, edge_sum, factor, rate_small, 0.0
    )
    norm_new = adam_update(
        norm_params, norm_moment, norm_square, norm_average, norm_grad, factor, rate_small, 0.0
    )
    return (
        jnp.transpose(outputs, (0, 2, 1, 3)),
        jnp.transpose(input_grad, (0, 2, 1, 3)),
        jnp.reshape(norm_total, (1,)),
        *graph_new,
        *temporal_new,
        *shortcut_new,
        *edge_new,
        *norm_new,
    )


def solution(mesh):
    rows = P("batch", "tm", None, None)
    in_specs = (rows, rows, P("batch"), P("batch", "tm")) + (P(),) * 21
    out_specs = (rows, rows) + (P(),) * 21
    return jax.shard_map(shards, mesh=mesh, in_specs=in_specs, out_specs=out_specs, check_vma=False)
```

time: 1430 us -> 559 us (0.39)
  local copies, waits for them, and re-layouts: 611 us -> 64.2 us
  matrix products: 269 us -> 0 us
  other arithmetic: 188 us -> 31.1 us
  Pallas kernels: 0 us -> 139 us
  waiting for transfers between devices: 95.2 us -> 74.5 us
    dot_general x36 -> x0, matrix products: 269 us -> none  [the longest x9 47.3 us: shards(): jnp.einsum('rd,cd->rc', grad_slices[shift_index], taps_low[2 * shift_inde...]
    reshape x17 -> x4, local copies, waits for them, and re-layouts: 208 us -> 8.32 us  [the longest x1 5.37 us: shards(): edge_wide = edge_wide.reshape(2, JOINTS, GROUP, JOINTS, GROUP)]
    pallas_call x0 -> x6, Pallas kernels: none -> 139 us  [call(): pl.pallas_call(body, grid=(pairs,), in_specs=in_specs, out_specs=out_spec...]
    slice x14 -> x3, local copies, waits for them, and re-layouts: 103 us -> 3.04 us  [the longest x1 2.34 us: shards(): before = lax.ppermute(natural[:, :, -4:], 'tm', forward)]
    convert_element_type x3 -> x1, local copies, waits for them, and re-layouts: 89.6 us -> 0.74 us  [shards(): ws = shortcut_weight.astype(bf16)]
    dot_general x1 -> x0, local copies, waits for them, and re-layouts: 87.2 us -> none  [shards(): jnp.einsum('rd,cd->rc', mixed_flat, weight_low, preferred_element_type=jn...]
    convert_element_type x5 -> x6, other arithmetic: 58.3 us -> 5.19 us  [the longest x1 2.37 us: shards(): rim_x = jnp.concatenate([before, after], axis=2).astype(f32)]
    another operation x5 -> x0, local copies, waits for them, and re-layouts: 52.9 us -> none  [the longest x3 43 us: shards(): jnp.stack([even_grad.reshape(clips_here, half_frames, JOINTS, C_OUT), odd...]
  transfers between devices with their start and end apart: 5 -> 7, of which waited for: 1 -> 1; matrix products, arithmetic and copies ran while one was open for 11% -> 9% of each run, Pallas kernels for 0% -> 3%
where the time goes in v1:
time: 559 us; the launch traced here: 550 us
  blocking collectives  207 us (37%)
  Pallas kernels  139 us (25%)
  waiting for transfers between devices  74.5 us (13%)
  local copies, waits for them, and re-layouts  64.2 us (11%)
  other arithmetic  31.1 us (6%)
  between operations  19.3 us (3%)
  starting transfers between devices  14.9 us (3%)
    pallas_call x6, Pallas kernels, call(): pl.pallas_call(body, grid=(pairs,), in_specs=in_specs, out_specs=out_spec...  139 us
    psum x1, waiting for transfers between devices, shards(): lax.psum((graph_grad, temporal_grad, shortcut_grad, edge_grad), ('batch',...  74.5 us
    psum x1, blocking collectives, shards(): first_sums = lax.psum(first_sums, ('batch', 'tm'))  43.1 us
    psum x1, blocking collectives, shards(): conv_stats = lax.psum(conv_stats, ('batch', 'tm'))  41.3 us
    psum x1, blocking collectives, shards(): lax.psum((graph_grad, temporal_grad, shortcut_grad, edge_grad), ('batch',...  41.1 us
    psum x1, blocking collectives, shards(): stats = lax.psum(stats, ('batch', 'tm'))  40.9 us
    psum x1, blocking collectives, shards(): back = lax.psum(back, ('batch', 'tm'))  40.4 us
    unnamed x99, local copies, waits for them, and re-layouts  33.6 us
  transfers between devices with their start and end apart: 7, of which 1 were waited for; matrix products, arithmetic and copies ran while one was open for 9% of the time, Pallas kernels for 3%

profile of v1, /device:TPU:0, one launch (start us, length us, event | category | flops | bytes accessed | tf_op | source)
XLA Modules:
  0.0 550.0 jit_solution(9114031907170771850)
XLA Ops:
  7.2 2.3 fusion.18
  9.6 1.3 collective-permute-start.1
  10.9 3.8 collective-permute-start
  14.6 0.8 and_convert_fusion
  16.1 1.3 collective-permute-start.3
  17.4 5.0 collective-permute-start.2
  22.5 0.7 copy.127
  23.2 0.7 convert_reduce_fusion
  23.9 0.9 multiply_convert_fusion
  26.4 4.2 mul.318
  30.6 1.2 copy.99
  31.8 0.8 copy.100
  32.7 1.0 copy.101
  33.7 0.7 copy.102.ws_ref
  34.4 0.7 pad.8.kron_ref
  35.2 0.7 slice_bitcast_fusion.2
  35.9 0.8 gather_fusion
  36.7 0.9 broadcast_in_dim.59.m_ref
  37.6 0.7 broadcast_in_dim.60.own_ref
  38.4 17.9 %graph_forward.1 = (bf16[6,8,400,384]{3,2,1,0:T(8,128)(2,1)}, bf16[6,8,256,256]{3,2,1,0:T(8,128)(2,1)}, bf16[6,4,400,128]{3,2,1,0:T(8,128)(2,1)}, bf16[6,8,400,256]{3,2,1,0:T(8,128)(2,1)}, f32[8,256]{1,0:T(8,128)}) custom-call(bf16[12,25,64,128]{3,2,1,0:T(8,128)(2,1)} %bitcast.34, f32[6,8,16,128]{3,2,1,0:T(8,128)} %broadcast_in_dim.59.m_ref, ...), custom_call_target="tpu_custom_call" | custom-call | tf_op jit(solution)/shard_map/graph_forward/pallas_call | solution.py:524
  56.2 40.9 %psum.56.st_ref = f32[8,256]{1,0:T(8,128)} all-reduce(f32[8,256]{1,0:T(8,128)} %get-tuple-element.47), channel_id=1, replica_groups=mesh['batch'=8,'tm'=4] {'batch','tm'}, use_global_device_ids=true, to_apply=%region_1.2 | all-reduce | flops 2048 | bytes 16384 | tf_op jit(solution)/shard_map/psum | solution.py:615
  97.1 1.1 convert_element_type.57.taps_ref
  98.3 0.8 pad_maximum_fusion
  99.2 2.4 maximum_convert_fusion.xh_ref
  101.5 0.7 broadcast_in_dim.62.mh_ref
  102.2 22.0 %conv_forward.1 = (bf16[6,2,8,400,256]{4,3,2,1,0:T(8,128)(2,1)}, f32[6,4,400,256]{3,2,1,0:T(8,128)}, f32[8,256]{1,0:T(8,128)}) custom-call(bf16[6,8,400,256]{3,2,1,0:T(8,128)(2,1)} %get-tuple-element.46.h_ref, f32[12,25,8,128]{3,2,1,0:T(8,128)} %maximum_convert_fusion.xh_ref, f32[6,8,16,128]{3,2,1,0:T(8,128)} %broadcast_in_dim.59.m_ref, ...), custom_call_target="tpu_custom_call" | custom-call | tf_op jit(solution)/shard_map/conv_forward/pallas_call | solution.py:524
  124.2 41.3 %psum.57.cs_ref = f32[8,256]{1,0:T(8,128)} all-reduce(f32[8,256]{1,0:T(8,128)} %get-tuple-element.50), channel_id=1, replica_groups=mesh['batch'=8,'tm'=4] {'batch','tm'}, use_global_device_ids=true, to_apply=%region_2.3 | all-reduce | flops 2048 | bytes 16384 | tf_op jit(solution)/shard_map/psum | solution.py:645
  165.5 15.8 %output_part.1 = (bf16[12,25,32,256]{3,2,1,0:T(8,128)(2,1)}, f32[6,4,400,256]{3,2,1,0:T(8,128)}, f32[8,256]{1,0:T(8,128)}) custom-call(f32[6,4,400,256]{3,2,1,0:T(8,128)} %get-tuple-element.48.conv_ref, bf16[6,4,400,128]{3,2,1,0:T(8,128)(2,1)} %get-tuple-element.49.xe_ref, bf16[12,25,32,256]{3,2,1,0:T(8,128)(2,1)} %bitcast.35, ...), custom_call_target="tpu_custom_call" | custom-call | tf_op jit(solution)/shard_map/output_part/pallas_call | solution.py:524
  181.3 40.4 %psum.58.bk_ref = f32[8,256]{1,0:T(8,128)} all-reduce(f32[8,256]{1,0:T(8,128)} %get-tuple-element.54), channel_id=1, replica_groups=mesh['batch'=8,'tm'=4] {'batch','tm'}, use_global_device_ids=true, to_apply=%region_3.4 | all-reduce | flops 2048 | bytes 16384 | tf_op jit(solution)/shard_map/psum | solution.py:674
  221.7 24.8 %weight_part.1 = (bf16[6,4,400,256]{3,2,1,0:T(8,128)(2,1)}, bf16[6,4,400,256]{3,2,1,0:T(8,128)(2,1)}, bf16[6,2,50,256]{3,2,1,0:T(8,128)(2,1)}, bf16[6,2,50,256]{...) custom-call(f32[6,4,400,256]{3,2,1,0:T(8,128)} %get-tuple-element.48.conv_ref, ...), custom_call_target="tpu_custom_call" | custom-call | tf_op jit(solution)/shard_map/weight_part/pallas_call | solution.py:524
  246.5 2.0 collective-permute-start.4
  248.5 1.5 collective-permute-start.5
  250.0 0.8 copy.105
  251.3 4.2 mul.320
  255.9 2.1 mul.322
  258.4 0.7 copy.129
  259.1 25.0 %conv_back.1 = (f32[6,8,400,256]{3,2,1,0:T(8,128)}, f32[8,256]{1,0:T(8,128)}) custom-call(bf16[6,4,400,256]{3,2,1,0:T(8,128)(2,1)} %get-tuple-element.55.cg_ref, bf16[6,2,50,256]{3,2,1,0:T(8,128)(2,1)} %collective-permute-done.4.left_ref, bf16[6,2,50,256]{3,2,1,0:T(8,128)(2,1)} %collective-permute-done.5.right_ref, ...), custom_call_target="tpu_custom_call" | custom-call | tf_op jit(solution)/shard_map/conv_back/pallas_call | solution.py:524
  284.1 43.1 %psum.59.fs_ref = f32[8,256]{1,0:T(8,128)} all-reduce(f32[8,256]{1,0:T(8,128)} %get-tuple-element.62), channel_id=1, replica_groups=mesh['batch'=8,'tm'=4] {'batch','tm'}, use_global_device_ids=true, to_apply=%region_4.5 | all-reduce | flops 2048 | bytes 16384 | tf_op jit(solution)/shard_map/psum | solution.py:732
  327.2 33.9 %graph_back.1 = (bf16[12,25,64,128]{3,2,1,0:T(8,128)(2,1)}, f32[384,256]{1,0:T(8,128)}, f32[512,256]{1,0:T(8,128)}, f32[25,8,256]{2,1,0:T(8,128)}) custom-call(f32[6,8,400,256]{3,2,1,0:T(8,128)} %get-tuple-element.58.fg_ref, bf16[6,8,400,256]{3,2,1,0:T(8,128)(2,1)} %get-tuple-element.46.h_ref, bf16[6,8,400,384]{3,2,1,0:T(8,128)(2,1)} %get-tuple-element.59.xg_ref, ...), custom_call_target="tpu_custom_call" | custom-call | tf_op jit(solution)/shard_map/graph_back/pallas_call | solution.py:524
  361.1 2.1 copy.107
  363.2 2.0 copy.117
  365.5 1.2 copy.110
  366.7 3.2 copy.118
  369.9 1.9 copy.114
  371.8 3.1 copy.115
  375.0 5.4 reshape.153
  380.4 3.8 select_reduce_fusion
  384.6 0.8 fusion.7
  385.6 41.1 %psum.63 = f32[3,25,25]{2,1,0:T(8,128)S(1)} all-reduce(f32[3,25,25]{2,1,0:T(8,128)S(1)} %maximum_multiply_fusion), channel_id=1, replica_groups=mesh['batch'=8,'tm'=4] {'batch','tm'}, use_global_device_ids=true, to_apply=%region_13.14 | all-reduce | flops 1875 | bytes 15000 | tf_op jit(solution)/shard_map/psum | solution.py:773
  427.9 74.5 %all-reduce.5.cloned.1.call-done = (f32[128,768]{0,1:T(8,128)}, f32[9,256,256]{1,2,0:T(8,128)}, f32[128,256]{1,0:T(8,128)}) async-done(((f32[128,768]{0,1:T(8,128)}, f32[9,256,256]{1,2,0:T(8,128)}, f32[128,256]{1,0:T(8,128)}), (f32[128,768]{0,1:T(8,128)}, f32[9,256,256]{1,2,0:T(8,128)}, f32[128,256]{1,0:T(8,128)})) %all-reduce.5.cloned.1.call-update) | async-done | bytes 2883600 | tf_op jit(solution)/shard_map/psum | solution.py:773
  502.4 1.8 multiply_reduce_fusion.1
  504.1 2.9 multiply_reduce_fusion
  511.0 1.4 multiply_add_fusion.2
  512.3 2.1 copy.119
  514.4 1.9 copy.120
  516.3 1.9 copy.121
  518.2 1.9 copy.122
  520.1 8.9 %multiply_add_fusion = (f32[9,256,256]{1,2,0:T(8,128)}, f32[9,256,256]{1,2,0:T(8,128)}, f32[9,256,256]{1,2,0:T(8,128)}, f32[9,256,256]{1,2,0:T(8,128)}) fusion(f32[9,256,256]{1,2,0:T(8,128)} %copy.118, f32[9,256,256]{1,2,0:T(8,128)} %copy.117, f32[9,256,256]{1,2,0:T(8,128)S(1)} %copy-done, f32[]{:T(128)S(6)} %min.3, f32[9,256,256]{1,2,0:T(8,128)} %copy.114, ...), kind=kLoop, calls=%fused_computation.4 | loop fusion | flops 11206656 | bytes 21233668 | tf_op jit(solution)/shard_map/add | solution.py:60
  529.1 3.2 copy.123
  532.3 1.9 copy.124
  534.2 3.2 copy.125
  537.6 2.0 copy.126
  539.5 0.9 multiply_add_fusion.4
  540.4 0.7 multiply_add_fusion.6
  (117 shorter events, 7.3 us)
Async XLA Ops:
  7.2 495.2 %all-reduce.5.cloned.1.call-start = ((), (), s32[]{:S(2)}) async-start(), calls=%async_computation | async-start | bytes 5767168 | tf_op jit(solution)/shard_map/psum | solution.py:773
  9.6 89.6 %collective-permute-start.1 = (bf16[12,25,4,128]{3,2,1,0:T(4,128)(2,1)}, bf16[12,25,4,128]{3,2,1,0:T(4,128)(2,1)}, u32[]{:S(2)}, u32[]{:S(2)}) collective-permute-start(bf16[12,25,4,128]{3,2,1,0:T(4,128)(2,1)} %get-tuple-element.162), channel_id=1, source_target_pairs={{1,0},{2,1},{3,2},{5,4},{6,5},{7,6},{9,8},{10,9},{11,10},{13,12},{... | collective-permute-start | bytes 921608 | tf_op jit(solution)/shard_map/ppermute | solution.py:556
  10.9 88.3 %collective-permute-start = (bf16[12,25,4,128]{3,2,1,0:T(4,128)(2,1)}, bf16[12,25,4,128]{3,2,1,0:T(4,128)(2,1)}, u32[]{:S(2)}, u32[]{:S(2)}) collective-permute-start(bf16[12,25,4,128]{3,2,1,0:T(4,128)(2,1)} %get-tuple-element.161), channel_id=1, source_target_pairs={{0,1},{1,2},{2,3},{4,5},{5,6},{6,7},{8,9},{9,10},{10,11},{12,13},{... | collective-permute-start | bytes 921608 | tf_op jit(solution)/shard_map/ppermute | solution.py:555
  16.1 82.2 %collective-permute-start.3 = (f32[12,4]{1,0:T(8,128)}, f32[12,4]{1,0:T(8,128)}, u32[]{:S(2)}, u32[]{:S(2)}) collective-permute-start(f32[12,4]{1,0:T(8,128)} %get-tuple-element.171), channel_id=1, source_target_pairs={{1,0},{2,1},{3,2},{5,4},{6,5},{7,6},{9,8},{10,9},{11,10},{13,12},{... | collective-permute-start | bytes 584 | tf_op jit(solution)/shard_map/ppermute | solution.py:559
  17.4 80.9 %collective-permute-start.2 = (f32[12,4]{1,0:T(8,128)}, f32[12,4]{1,0:T(8,128)}, u32[]{:S(2)}, u32[]{:S(2)}) collective-permute-start(f32[12,4]{1,0:T(8,128)} %get-tuple-element.170), channel_id=1, source_target_pairs={{0,1},{1,2},{2,3},{4,5},{5,6},{6,7},{8,9},{9,10},{10,11},{12,13},{... | collective-permute-start | bytes 584 | tf_op jit(solution)/shard_map/ppermute | solution.py:558
  22.5 3.6 copy-start.38
  23.9 2.1 copy-start.36
  24.8 0.6 copy-start.28
  30.6 6.1 %copy-start.27 = (f32[6,8,16]{2,1,0:T(8,128)S(1)}, f32[6,8,16]{2,1,0:T(8,128)}, u32[]{:S(2)}) copy-start(f32[6,8,16]{2,1,0:T(8,128)} %copy.127) | copy-start | bytes 9220
  31.8 2.6 copy-start.5
  33.7 22.6 %copy-start.10 = (bf16[128,256]{0,1:T(8,128)(2,1)}, bf16[128,256]{0,1:T(8,128)(2,1)S(1)}, u32[]{:S(2)}) copy-start(bf16[128,256]{0,1:T(8,128)(2,1)S(1)} %copy.101) | copy-start | bytes 196612
  38.4 58.8 %copy-start.3 = (f32[9,256,256]{2,1,0:T(8,128)S(1)}, f32[9,256,256]{2,1,0:T(8,128)}, u32[]{:S(2)}) copy-start(f32[9,256,256]{2,1,0:T(8,128)} %param.34) | copy-start | bytes 7077892
  221.7 28.3 %copy-start.7 = (bf16[3,128,256]{2,1,0:T(8,128)(2,1)S(1)}, bf16[3,128,256]{2,1,0:T(8,128)(2,1)}, u32[]{:S(2)}) copy-start(bf16[3,128,256]{2,1,0:T(8,128)(2,1)} %copy.100) | copy-start | bytes 589828
  221.7 29.1 %copy-start.29 = (bf16[25,2,25]{2,0,1:T(8,128)(2,1)S(1)}, bf16[25,2,25]{2,0,1:T(8,128)(2,1)}, u32[]{:S(2)}) copy-start(bf16[25,2,25]{2,0,1:T(8,128)(2,1)} %get-tuple-element.163) | copy-start | bytes 7504
  246.5 12.6 %collective-permute-start.4 = (bf16[6,2,50,256]{3,2,1,0:T(8,128)(2,1)}, bf16[6,2,50,256]{3,2,1,0:T(8,128)(2,1)}, u32[]{:S(2)}, u32[]{:S(2)}) collective-permute-start(bf16[6,2,50,256]{3,2,1,0:T(8,128)(2,1)} %get-tuple-element.56), channel_id=1, source_target_pairs={{0,1},{1,2},{2,3},{4,5},{5,6},{6,7},{8,9},{9,10},{10,11},{12,13},{... | collective-permute-start | bytes 921608 | tf_op jit(solution)/shard_map/ppermute | solution.py:705
  248.5 10.5 %collective-permute-start.5 = (bf16[6,2,50,256]{3,2,1,0:T(8,128)(2,1)}, bf16[6,2,50,256]{3,2,1,0:T(8,128)(2,1)}, u32[]{:S(2)}, u32[]{:S(2)}) collective-permute-start(bf16[6,2,50,256]{3,2,1,0:T(8,128)(2,1)} %get-tuple-element.57), channel_id=1, source_target_pairs={{1,0},{2,1},{3,2},{5,4},{6,5},{7,6},{9,8},{10,9},{11,10},{13,12},{... | collective-permute-start | bytes 921608 | tf_op jit(solution)/shard_map/ppermute | solution.py:706
  361.1 2.1 copy-start.4
  363.2 2.0 copy-start.16
  363.2 2.1 copy-start.17
  366.6 3.2 copy-start.8
  371.8 3.1 copy-start.19
  380.3 3.9 copy-start.21
  380.3 4.2 copy-start.18
  380.3 5.1 copy-start.23
  380.4 5.1 copy-start.37
  380.4 5.1 copy-start.39
  384.2 126.8 %copy-start.6 = (f32[128,768]{0,1:T(8,128)S(1)}, f32[128,768]{0,1:T(8,128)}, u32[]{:S(2)}) copy-start(f32[128,768]{0,1:T(8,128)} %copy-done.5) | copy-start | bytes 1179652
  426.6 1.2 copy-start.14
  502.3 4.7 copy-start.12
  502.4 8.6 %copy-start.9 = (f32[128,768]{0,1:T(8,128)S(1)}, f32[128,768]{0,1:T(8,128)}, u32[]{:S(2)}) copy-start(f32[128,768]{0,1:T(8,128)} %get-tuple-element.138) | copy-start | bytes 1179652
  512.3 7.8 %copy-start = (f32[9,256,256]{1,2,0:T(8,128)S(1)}, f32[9,256,256]{1,2,0:T(8,128)}, u32[]{:S(2)}) copy-start(f32[9,256,256]{1,2,0:T(8,128)} %get-tuple-element.139) | copy-start | bytes 7077892
  529.1 3.2 copy-start.2
  534.2 3.2 copy-start.1
  537.4 2.1 copy-start.11
  537.4 2.1 copy-start.13
  537.4 2.1 copy-start.24
  537.4 2.1 copy-start.25
  537.4 2.1 copy-start.26
  537.5 3.0 copy-start.15
  537.5 3.0 copy-start.22
  537.5 2.9 copy-start.30
  537.5 2.9 copy-start.31
  537.5 2.9 copy-start.32
  537.5 3.6 copy-start.20
  537.5 3.6 copy-start.33
  537.5 3.6 copy-start.34
  537.6 3.6 copy-start.35
Sparse Core Ops, SparseCore 0:
  363.3 139.0 all-reduce.4

commit v2 on v1

v2 whole, which is shorter than its diff:
```python
import functools

import jax
import jax.numpy as jnp
from jax import lax
from jax.experimental import pallas as pl
from jax.experimental.pallas import tpu as pltpu
from jax.sharding import PartitionSpec as P

C_IN = 128
C_OUT = 256
JOINTS = 25
SUBSETS = 3
TAPS = 9
GROUP = 8
PHASES = 8
UNITS = 2 * JOINTS
ROWS = UNITS * GROUP
HALF_ROWS = JOINTS * GROUP
HALF = C_IN
CUT = 5

f32 = jnp.float32
bf16 = jnp.bfloat16

norm_epsilon = 1e-05
beta_first = 0.9
beta_second = 0.999
adam_epsilon = 1e-08
clip_limit = 1.0
average_decay = 0.9
rate_matrix = 0.05
rate_small = 0.3
decay_matrix = 0.01
steps_taken = 3.0


def params(**more):
    return pltpu.CompilerParams(
        vmem_limit_bytes=60 * 2**20, dimension_semantics=("arbitrary",), **more
    )


def adjacency(subsets):
    linked = (subsets > 0).astype(f32)
    degree = jnp.sum(linked, axis=0)
    labels = jnp.arange(SUBSETS, dtype=jnp.int32) + 1
    chosen = (subsets[None, :, :] == labels[:, None, None]).astype(f32)
    return chosen / degree[None, None, :]


def adam_update(weight, moment, square, average, gradient, factor, rate, decay):
    fix_first = 1.0 - beta_first**steps_taken
    fix_second = 1.0 - beta_second**steps_taken
    clipped = gradient * factor
    moment_new = beta_first * moment + (1.0 - beta_first) * clipped
    square_new = beta_second * square + (1.0 - beta_second) * clipped * clipped
    stepped = moment_new / fix_first / (jnp.sqrt(square_new / fix_second) + adam_epsilon)
    weight_new = weight - rate * (stepped + decay * weight)
    average_new = average_decay * average + (1.0 - average_decay) * weight_new
    return (weight_new, moment_new, square_new, average_new)


def dot(a, b):
    return jnp.dot(a, b, preferred_element_type=f32)


def dot_nt(a, b):
    return lax.dot_general(a, b, (((1,), (1,)), ((), ())), preferred_element_type=f32)


def dot_tn(a, b):
    return lax.dot_general(a, b, (((0,), (0,)), ((), ())), preferred_element_type=f32)


def fold(values):
    return jnp.sum(values.reshape(-1, GROUP, values.shape[-1]), axis=0)


MESH = pl.DeviceIdType.MESH


def peers(axis):
    count = lax.axis_size(axis)
    here = lax.axis_index(axis)
    return [(d, {axis: lax.rem(here + d, count)}) for d in range(1, count)]


def greet():
    barrier = pltpu.get_barrier_semaphore()
    for axis in ("tm", "batch"):
        for _, device in peers(axis):
            pl.semaphore_signal(barrier, inc=1, device_id=device, device_id_type=MESH)


def await_greetings():
    count = lax.axis_size("tm") + lax.axis_size("batch") - 2
    pl.semaphore_wait(pltpu.get_barrier_semaphore(), count)


def sum_all(values, buffers):
    copies = []
    for axis, (slots, sent, received) in zip(("tm", "batch"), buffers):
        here = lax.axis_index(axis)
        slots[here] = values
        started = []
        for d, device in peers(axis):
            copy = pltpu.make_async_remote_copy(
                src_ref=slots.at[here],
                dst_ref=slots.at[here],
                send_sem=sent.at[d],
                recv_sem=received.at[d],
                device_id=device,
                device_id_type=MESH,
            )
            copy.start()
            started.append(copy)
        for copy in started:
            copy.wait_recv()
        values = slots[0]
        for k in range(1, lax.axis_size(axis)):
            values = values + slots[k]
        copies += started
    for copy in copies:
        copy.wait_send()
    return values


def as_buffers(refs):
    return [refs[0:3], refs[3:6]]


def sum_scratch(shape=(8, C_OUT)):
    found = []
    for axis in ("tm", "batch"):
        count = lax.axis_size(axis)
        found += [
            pltpu.VMEM((count, *shape), f32),
            pltpu.SemaphoreType.DMA((count,)),
            pltpu.SemaphoreType.DMA((count,)),
        ]
    return found


def remote(source, target, sent, received, device):
    return pltpu.make_async_remote_copy(
        src_ref=source,
        dst_ref=target,
        send_sem=sent,
        recv_sem=received,
        device_id=device,
        device_id_type=MESH,
    )


def with_neighbours(step, low, high, from_left, from_right, sems, act):
    here = lax.axis_index("tm")
    last = lax.axis_size("tm") - 1
    sent_right, got_left, sent_left, got_right = sems

    def rightward():
        return remote(high, from_left, sent_right.at[step], got_left.at[step], {"tm": here + 1})

    def leftward():
        return remote(low, from_right, sent_left.at[step], got_right.at[step], {"tm": here - 1})

    if act == "start":

        @pl.when(here < last)
        def _():
            rightward().start()

        @pl.when(here > 0)
        def _():
            leftward().start()

    else:

        @pl.when(here < last)
        def _():
            rightward().wait_send()
            leftward().wait_recv()

        @pl.when(here > 0)
        def _():
            leftward().wait_send()
            rightward().wait_recv()


def first_moments(stats, norm):
    count_in = stats[4:5]
    mean = stats[0:1] / count_in
    rstd = lax.rsqrt(stats[1:2] / count_in - mean * mean + norm_epsilon)
    return mean, rstd, norm[0:1] * rstd, norm[1:2] - norm[0:1] * rstd * mean


def one_hot_rows(rows, columns):
    row = lax.broadcasted_iota(jnp.int32, (rows, columns), 0)
    col = lax.broadcasted_iota(jnp.int32, (rows, columns), 1)
    return (row // GROUP == col).astype(bf16)


def prepare(
    length_ref, frame_ref, subset_ref, edge_ref, graph_ref, short_ref, taps_ref,
    m_ref, em_ref, kron_ref, kront_ref, own_ref, gm_ref, wg_ref, wgt_ref, ws_ref, wst_ref, low_ref,
):
    clips, frames = frame_ref.shape
    first = lax.axis_index("tm") * frames
    row = lax.broadcasted_iota(jnp.int32, (clips, frames), 0)
    ids = lax.broadcasted_iota(jnp.int32, (clips, frames), 1) + first
    ends = jnp.zeros((clips, frames), jnp.int32)
    for clip in range(clips):
        ends = jnp.where(row == clip, length_ref[clip], ends)
    mask = ((ids < ends) & (frame_ref[...] > 0)).astype(bf16)
    every = jnp.ones((frames, 128), bf16)

    def spread(rows, clip_of, frame_of):
        at = lax.broadcasted_iota(jnp.int32, (rows, clips), 0)
        chosen = (clip_of(at) == lax.broadcasted_iota(jnp.int32, (rows, clips), 1)).astype(bf16)
        lines = dot(chosen, mask)
        at = lax.broadcasted_iota(jnp.int32, (rows, frames), 0)
        kept = frame_of(at) == lax.broadcasted_iota(jnp.int32, (rows, frames), 1)
        return dot(jnp.where(kept, lines, 0.0).astype(bf16), every)

    side = 2 * GROUP
    m_ref[...] = spread(
        clips * frames,
        lambda at: 2 * (at // (PHASES * side)) + at // GROUP % 2,
        lambda at: PHASES * (at % GROUP) + at // side % PHASES,
    )
    em_ref[...] = spread(
        clips * GROUP, lambda at: at // GROUP, lambda at: (at % GROUP + frames - 4) % frames
    )
    subsets = subset_ref[...]
    degree = jnp.sum((subsets > 0).astype(f32), axis=0, keepdims=True)
    lift = one_hot_rows(HALF_ROWS, JOINTS)
    row = lax.broadcasted_iota(jnp.int32, (JOINTS, C_OUT), 0)
    drop = (row == lax.broadcasted_iota(jnp.int32, (JOINTS, C_OUT), 1) // GROUP).astype(bf16)
    row = lax.broadcasted_iota(jnp.int32, (HALF_ROWS, C_OUT), 0)
    same = row % GROUP == lax.broadcasted_iota(jnp.int32, (HALF_ROWS, C_OUT), 1) % GROUP
    for k in range(SUBSETS):
        share = (subsets == k + 1).astype(f32) / degree
        gm_ref[k] = share
        low = (share * edge_ref[k]).astype(bf16)
        if k == 0:
            row = lax.broadcasted_iota(jnp.int32, (JOINTS, JOINTS), 0)
            col = lax.broadcasted_iota(jnp.int32, (JOINTS, JOINTS), 1)
            diagonal = jnp.sum(jnp.where(row == col, low.astype(f32), 0.0), axis=1, keepdims=True)
            wide = jnp.broadcast_to(diagonal, (JOINTS, C_IN)).astype(bf16)
            own_ref[...] = dot(lift, wide).reshape(JOINTS, GROUP, C_IN)
        else:
            ahead = dot(lift, dot_tn(low, drop).astype(bf16))
            rows = slice((k - 1) * HALF_ROWS, k * HALF_ROWS)
            kron_ref[rows, :] = jnp.where(same, ahead, 0.0).astype(bf16)
            behind = dot(lift, dot(low, drop).astype(bf16))
            lanes = slice((k - 1) * C_OUT, k * C_OUT)
            kront_ref[:, lanes] = jnp.where(same, behind, 0.0).astype(bf16)
        block = graph_ref[:, k * C_OUT : (k + 1) * C_OUT]
        wg_ref[k * C_IN : (k + 1) * C_IN, :] = block.astype(bf16)
        wgt_ref[:, k * C_IN : (k + 1) * C_IN] = block.T.astype(bf16)
    ws_ref[...] = short_ref[...].astype(bf16)
    wst_ref[...] = short_ref[...].T.astype(bf16)
    low_ref[...] = taps_ref[...].astype(bf16)


def mix_rows(parts, scales, kron_ref, pad_ref):
    wide = jnp.concatenate([part.reshape(HALF_ROWS, C_IN) for part in parts], axis=1)
    pad_ref[0:HALF_ROWS, :] = wide.astype(bf16)
    mixed = dot(kron_ref[...], pad_ref[...])
    sides = []
    for side in range(2):
        lanes = slice(side * HALF, (side + 1) * HALF)
        sides.append(
            jnp.concatenate(
                [
                    parts[side] * scales,
                    mixed[0:HALF_ROWS, lanes].reshape(JOINTS, GROUP, C_IN),
                    mixed[HALF_ROWS : 2 * HALF_ROWS, lanes].reshape(JOINTS, GROUP, C_IN),
                ],
                axis=2,
            )
        )
    return jnp.concatenate(sides, axis=1).reshape(ROWS, SUBSETS * C_IN).astype(bf16)


def graph_forward(
    x_ref, m_ref, em_ref, kron_ref, own_ref, wg_ref, ws_ref,
    xg_ref, xq_ref, xe_ref, h_ref, st_ref, rim_ref, rim_mask_ref,
    xs, sums, counts, mine, lefts, rights, mask_lefts, mask_rights,
    sent_right, got_left, sent_left, got_right, *sum_buffers,
):
    step = pl.program_id(0)
    last = pl.num_programs(0) - 1
    sems = (sent_right, got_left, sent_left, got_right)

    def rims(at, act):
        with_neighbours(at, mine.at[at], mine.at[at], lefts.at[at], rights.at[at], sems, act)

    def rim_masks(act):
        with_neighbours(last + 1, em_ref, em_ref, mask_lefts, mask_rights, sems, act)

    @pl.when(step == 0)
    def _():
        for ref in (lefts, rights, mask_lefts, mask_rights):
            ref[...] = jnp.zeros_like(ref)
        greet()
        sums[...] = jnp.zeros_like(sums)
        counts[...] = jnp.zeros_like(counts)

    for side in range(2):
        for joint in range(JOINTS):
            xs[side, joint] = x_ref[side, joint].astype(f32)
    tail = x_ref.shape[2] - 4
    ends = [
        jnp.concatenate([xs[side, :, tail:, :], xs[side, :, 0:4, :]], axis=1) for side in range(2)
    ]
    mine[step] = jnp.concatenate(ends, axis=1).astype(bf16)

    @pl.when(step == 0)
    def _():
        await_greetings()
        rim_masks("start")

    rims(step, "start")
    own = own_ref[...]
    for c in range(PHASES):
        mask = m_ref[0, c]
        parts = [
            xs[side, :, pl.ds(c, GROUP, stride=PHASES), :]
            * mask[side * GROUP : (side + 1) * GROUP][None]
            for side in range(2)
        ]
        xq_ref[0, c, HALF_ROWS:, :] = jnp.zeros((C_OUT - HALF_ROWS, C_OUT), bf16)
        xg = mix_rows(parts, own, kron_ref, xq_ref.at[0, c])
        xg_ref[0, c] = xg
        hidden = dot(xg, wg_ref[...])
        h_ref[0, c] = hidden.astype(bf16)
        sums[0] += fold(hidden)
        sums[1] += fold(hidden * hidden)
        counts[0] += mask
        if c % 2 == 0:
            counts[1] += mask
            even = jnp.concatenate(parts, axis=1).reshape(ROWS, C_IN).astype(bf16)
            xe_ref[0, c // 2] = even
            short = dot(even, ws_ref[...])
            sums[2] += fold(short)
            sums[3] += fold(short * short)

    @pl.when(step == last)
    def _():
        rows = [jnp.sum(sums[k], axis=0, keepdims=True) for k in range(4)]
        for k in range(2):
            total = JOINTS * jnp.sum(counts[k], axis=0, keepdims=True)
            rows.append(jnp.concatenate([total, total], axis=1))
        rows.append(jnp.zeros((2, C_OUT), f32))
        st_ref[...] = sum_all(jnp.concatenate(rows, axis=0), as_buffers(sum_buffers))
        rim_masks("wait")
        sub = lax.broadcasted_iota(jnp.int32, mask_lefts.shape, 0) % GROUP
        rim_mask_ref[...] = jnp.where(sub < 4, mask_lefts[...], mask_rights[...])
        for pair in range(lefts.shape[0]):
            rims(pair, "wait")
            sub = lax.broadcasted_iota(jnp.int32, lefts.shape[1:], 1) % GROUP
            both = jnp.where(sub < 4, lefts[pair].astype(f32), rights[pair].astype(f32))
            rim_ref[pair] = both.astype(bf16)


def insert_and_roll(tiles, fill, side):
    sub = lax.broadcasted_iota(jnp.int32, tiles.shape, 1)
    joined = jnp.where(sub == side, fill, tiles)
    return pltpu.roll(joined, 1 if side == 7 else GROUP - 1, 1)


def conv_forward(
    h_ref, xh_ref, m_ref, mh_ref, st_ref, norm_ref, kron_ref, own_ref, wg_ref, taps_ref,
    a_ref, conv_ref, out_ref,
    pad, rims, fills, sums, *sum_buffers,
):
    step = pl.program_id(0)

    @pl.when(step == 0)
    def _():
        greet()
        sums[...] = jnp.zeros_like(sums)
        pad[...] = jnp.zeros_like(pad)

    _, _, scale, shift = first_moments(st_ref[...], norm_ref[...])
    scale, shift = 0.5 * scale, 0.5 * shift

    def activate(values, mask):
        half = values * scale + shift
        return (half + half * jnp.tanh(half)).reshape(-1, 2 * GROUP, C_OUT) * mask

    def wide(mask):
        return jnp.concatenate([mask, mask], axis=1)[None]

    rim_mask = mh_ref[...]
    rim_rows = xh_ref[0].astype(f32) * rim_mask[None]
    parts = [rim_rows[:, side * GROUP : (side + 1) * GROUP] for side in range(2)]
    rim_hidden = dot(mix_rows(parts, own_ref[...], kron_ref, pad), wg_ref[...])
    rim_active = activate(rim_hidden, wide(rim_mask)).reshape(ROWS, C_OUT)
    for lane in range(2):
        rims[lane] = rim_active[:, lane * HALF : (lane + 1) * HALF]
    for p in range(2):
        for q in range(2):
            for lane in range(2):
                fills[2 * p + q, lane, pl.ds(7, UNITS, stride=GROUP), :] = rims[
                    lane, pl.ds(2 * q + p, UNITS, stride=GROUP), :
                ]
                fills[2 * p + q, lane, pl.ds(0, UNITS, stride=GROUP), :] = rims[
                    lane, pl.ds(4 + 2 * q + p, UNITS, stride=GROUP), :
                ]

    for c in range(PHASES):
        p, q = c % 2, c // 2
        mask = wide(m_ref[0, c])
        for start in range(0, JOINTS, CUT):
            rows = slice(start * 2 * GROUP, (start + CUT) * 2 * GROUP)
            active = activate(h_ref[0, c, rows, :].astype(f32), mask)
            a_ref[0, p, q + 2, rows, :] = active.reshape(-1, C_OUT).astype(bf16)
            if p == 1 and q == 1:
                continue
            tiles = active.reshape(-1, GROUP, C_OUT)
            fill = jnp.concatenate(
                [fills[2 * p + q % 2, lane, rows, :] for lane in range(2)], axis=1
            ).reshape(-1, GROUP, C_OUT)
            moved = insert_and_roll(tiles, fill, 7 if q >= 2 else 0)
            at = q - 2 if q >= 2 else q + 6
            a_ref[0, p, at, rows, :] = moved.reshape(-1, C_OUT).astype(bf16)

    total = None
    for j in range(TAPS):
        window = a_ref[0, j % 2, j // 2 : j // 2 + 4].reshape(4 * ROWS, C_OUT)
        part = dot(window, taps_ref[j])
        total = part if total is None else total + part
    conv_ref[0] = total.reshape(4, ROWS, C_OUT)
    for q in range(4):
        block = total[q * ROWS : (q + 1) * ROWS].reshape(JOINTS, 2 * GROUP, C_OUT)
        live = block * wide(m_ref[0, 2 * q])
        sums[0] += fold(live)
        sums[1] += fold(live * block)

    @pl.when(step == pl.num_programs(0) - 1)
    def _():
        await_greetings()
        rows = [jnp.sum(sums[k], axis=0, keepdims=True) for k in range(2)]
        rows.append(jnp.zeros((6, C_OUT), f32))
        out_ref[...] = sum_all(jnp.concatenate(rows, axis=0), as_buffers(sum_buffers))


def second_moments(stats, conv_stats):
    count_out = stats[5:6]
    mean_conv = conv_stats[0:1] / count_out
    rstd_conv = lax.rsqrt(conv_stats[1:2] / count_out - mean_conv * mean_conv + norm_epsilon)
    mean_short = stats[2:3] / count_out
    rstd_short = lax.rsqrt(stats[3:4] / count_out - mean_short * mean_short + norm_epsilon)
    return mean_conv, rstd_conv, mean_short, rstd_short


def output_part(
    conv_ref, xe_ref, cot_ref, m_ref, st_ref, cs_ref, norm_ref, ws_ref,
    o_ref, up_ref, out_ref,
    cots, outs, sums,
):
    step = pl.program_id(0)

    @pl.when(step == 0)
    def _():
        sums[...] = jnp.zeros_like(sums)

    norm = norm_ref[...]
    mean_conv, rstd_conv, mean_short, rstd_short = second_moments(st_ref[...], cs_ref[...])
    scale_conv = 0.5 * norm[2:3] * rstd_conv
    scale_short = 0.5 * norm[4:5] * rstd_short
    shift = 0.5 * (norm[3:4] + norm[5:6]) - scale_conv * mean_conv - scale_short * mean_short
    for side in range(2):
        for joint in range(JOINTS):
            for lane in range(2):
                cots[side, lane, joint] = cot_ref[
                    side, joint, :, lane * HALF : (lane + 1) * HALF
                ].astype(f32)
    for q in range(4):
        mask = m_ref[0, 2 * q]
        mask = jnp.concatenate([mask, mask], axis=1)[None]
        short_all = dot(xe_ref[0, q], ws_ref[...])
        for start in range(0, JOINTS, CUT):
            rows = slice(start * 2 * GROUP, (start + CUT) * 2 * GROUP)
            conv = conv_ref[0, q, rows, :]
            short = short_all[rows]
            half = conv * scale_conv + short * scale_short + shift
            turn = jnp.tanh(half)
            grow = (0.5 + 0.5 * turn).reshape(CUT, 2 * GROUP, C_OUT) * mask
            half = half.reshape(CUT, 2 * GROUP, C_OUT)
            turn = turn.reshape(CUT, 2 * GROUP, C_OUT)
            result = (half + half) * grow
            slope = grow + grow * (half - half * turn)
            cot = jnp.concatenate(
                [
                    jnp.concatenate(
                        [
                            cots[side, lane, start : start + CUT, pl.ds(q, GROUP, stride=4), :]
                            for lane in range(2)
                        ],
                        axis=2,
                    )
                    for side in range(2)
                ],
                axis=1,
            )
            for side in range(2):
                for lane in range(2):
                    outs[side, lane, start : start + CUT, pl.ds(q, GROUP, stride=4), :] = result[
                        :, side * GROUP : (side + 1) * GROUP, lane * HALF : (lane + 1) * HALF
                    ]
            up = (cot * slope).reshape(-1, C_OUT)
            up_ref[0, q, rows, :] = up
            sums[0] += fold(up)
            sums[1] += fold(up * conv)
            sums[2] += fold(up * short)
    for side in range(2):
        for joint in range(JOINTS):
            for lane in range(2):
                o_ref[side, joint, :, lane * HALF : (lane + 1) * HALF] = outs[
                    side, lane, joint
                ].astype(bf16)

    @pl.when(step == pl.num_programs(0) - 1)
    def _():
        rows = [jnp.sum(sums[k], axis=0, keepdims=True) for k in range(3)]
        rows.append(jnp.zeros((5, C_OUT), f32))
        out_ref[...] = jnp.concatenate(rows, axis=0)


def back_totals(back, moments):
    mean_conv, rstd_conv, mean_short, rstd_short = moments
    back_sum = back[0:1]
    back_conv = rstd_conv * (back[1:2] - mean_conv * back_sum)
    back_short = rstd_short * (back[2:3] - mean_short * back_sum)
    return back_sum, back_conv, back_short


def weight_part(
    conv_ref, up_ref, xe_ref, a_ref, m_ref, st_ref, cs_ref, bk_ref, norm_ref, ws_ref,
    cg_ref, sg_ref, left_ref, right_ref, grad_ref, total_ref,
    turned, edges, tg, shg, low_rims, high_rims, lefts, rights,
    sent_right, got_left, sent_left, got_right, *sum_buffers,
):
    step = pl.program_id(0)
    last = pl.num_programs(0) - 1
    sems = (sent_right, got_left, sent_left, got_right)

    def rims(at, act):
        with_neighbours(
            at, low_rims.at[at], high_rims.at[at], lefts.at[at], rights.at[at], sems, act
        )

    @pl.when(step == 0)
    def _():
        lefts[...] = jnp.zeros_like(lefts)
        rights[...] = jnp.zeros_like(rights)
        greet()
        tg[...] = jnp.zeros_like(tg)
        shg[...] = jnp.zeros_like(shg)
        low_rims[...] = jnp.zeros_like(low_rims)
        high_rims[...] = jnp.zeros_like(high_rims)
        await_greetings()
        total_ref[...] = sum_all(bk_ref[...], as_buffers(sum_buffers))

    norm = norm_ref[...]
    stats = st_ref[...]
    moments = second_moments(stats, cs_ref[...])
    mean_conv, rstd_conv, mean_short, rstd_short = moments
    back_sum, back_conv, back_short = back_totals(total_ref[...], moments)
    count_out = stats[5:6]

    def terms(gain, mean, rstd, back):
        lead = gain * rstd
        slope = lead * rstd * back / count_out
        return lead, slope, lead * back_sum / count_out - slope * mean

    lead_c, slope_c, shift_c = terms(norm[2:3], mean_conv, rstd_conv, back_conv)
    lead_s, slope_s, shift_s = terms(norm[4:5], mean_short, rstd_short, back_short)
    for q in range(4):
        mask = m_ref[0, 2 * q]
        mask = jnp.concatenate([mask, mask], axis=1)[None]
        short_all = dot(xe_ref[0, q], ws_ref[...])
        for start in range(0, JOINTS, CUT):
            rows = slice(start * 2 * GROUP, (start + CUT) * 2 * GROUP)
            up = up_ref[0, q, rows, :]

            def masked(values):
                return (values.reshape(CUT, 2 * GROUP, C_OUT) * mask).reshape(-1, C_OUT)

            cg = up * lead_c - masked(conv_ref[0, q, rows, :] * slope_c + shift_c)
            cg_ref[0, q, rows, :] = cg.astype(bf16)
            for lane in range(2):
                edges[lane, rows, :] = cg[:, lane * HALF : (lane + 1) * HALF]
            sg = up * lead_s - masked(short_all[rows] * slope_s + shift_s)
            sg_ref[0, q, rows, :] = sg.astype(bf16)
        for lane in range(2):
            at = slice(lane * HALF, (lane + 1) * HALF)
            target = low_rims if q < 2 else high_rims
            outer = edges[lane, pl.ds(0 if q < 2 else 7, UNITS, stride=GROUP), :]
            target[step, q % 2, 0:UNITS, at] = outer.astype(bf16)
    rims(step, "start")
    turned[...] = cg_ref[0].reshape(4 * ROWS, C_OUT).T
    for j in range(TAPS):
        window = a_ref[0, j % 2, j // 2 : j // 2 + 4].reshape(4 * ROWS, C_OUT)
        tg[j] += dot(turned[...], window)
    shg[...] += dot_tn(
        xe_ref[0].reshape(4 * ROWS, C_IN), sg_ref[0].reshape(4 * ROWS, C_OUT)
    )

    @pl.when(step == last)
    def _():
        for j in range(TAPS):
            grad_ref[j * C_OUT : (j + 1) * C_OUT, :] = tg[j].astype(bf16)
        grad_ref[TAPS * C_OUT : TAPS * C_OUT + C_IN, :] = shg[...].astype(bf16)
        rest = grad_ref.shape[0] - TAPS * C_OUT - C_IN
        if rest:
            grad_ref[TAPS * C_OUT + C_IN :, :] = jnp.zeros((rest, C_OUT), bf16)
        for pair in range(lefts.shape[0]):
            rims(pair, "wait")
        left_ref[...] = lefts[...]
        right_ref[...] = rights[...]


class Sharing:
    def __init__(self, source, refs):
        self.source = source
        self.here, self.up, self.out = refs[0:3]
        self.firsts, self.seconds, self.thirds, self.gathered, self.joined, self.full = refs[3:9]
        self.sems = refs[9:21]
        tm = lax.axis_index("tm")
        self.core = tm % 2
        self.line = tm // 2
        self.lines = lax.axis_size("tm") // 2
        self.batch = lax.axis_index("batch")
        self.batches = lax.axis_size("batch")
        self.half = source.shape[0] // 2
        self.part = self.half // self.lines
        self.piece = self.part // self.batches

    @staticmethod
    def padded(rows):
        unit = 16 * lax.axis_size("tm") * lax.axis_size("batch")
        return (rows + unit - 1) // unit * unit

    @staticmethod
    def scratch(rows):
        lines, batches = lax.axis_size("tm") // 2, lax.axis_size("batch")
        half = rows // 2
        part = half // lines
        piece = part // batches
        found = [
            pltpu.VMEM(shape, bf16)
            for shape in (
                (half, C_OUT),
                (part, C_OUT),
                (piece, C_OUT),
                (half, C_OUT),
                (lines, part, C_OUT),
                (batches, piece, C_OUT),
                (batches, piece, C_OUT),
                (lines, part, C_OUT),
                (2, half, C_OUT),
            )
        ]
        for count in (1, lines, batches, batches, lines, 1):
            found += [pltpu.SemaphoreType.DMA((count,))] * 2
        return found

    def core_peer(self):
        return {"tm": 2 * self.line + 1 - self.core}

    def line_peers(self):
        for d in range(1, self.lines):
            to = lax.rem(self.line + d, self.lines)
            yield d, to, {"tm": 2 * to + self.core}

    def batch_peers(self):
        for d in range(1, self.batches):
            to = lax.rem(self.batch + d, self.batches)
            yield d, to, {"batch": to}

    def rows(self, index, count):
        return pl.ds(pl.multiple_of(index * count, 16), count)

    def copies(self, level):
        sent, got = self.sems[2 * level], self.sems[2 * level + 1]
        if level == 0:
            source = self.source.at[self.rows(1 - self.core, self.half)]
            return [remote(source, self.firsts, sent.at[0], got.at[0], self.core_peer())]
        if level == 1:
            return [
                remote(
                    self.here.at[self.rows(to, self.part)], self.seconds.at[self.line],
                    sent.at[d], got.at[d], device,
                )
                for d, to, device in self.line_peers()
            ]
        if level == 2:
            return [
                remote(
                    self.up.at[self.rows(to, self.piece)], self.thirds.at[self.batch],
                    sent.at[d], got.at[d], device,
                )
                for d, to, device in self.batch_peers()
            ]
        if level == 3:
            slot = self.gathered.at[self.batch]
            return [
                remote(slot, slot, sent.at[d], got.at[d], device)
                for d, _, device in self.batch_peers()
            ]
        if level == 4:
            slot = self.joined.at[self.line]
            return [
                remote(slot, slot, sent.at[d], got.at[d], device)
                for d, _, device in self.line_peers()
            ]
        slot = self.full.at[self.core]
        return [remote(slot, slot, sent.at[0], got.at[0], self.core_peer())]

    def start(self, level):
        if level == 3:
            self.gathered[self.batch] = self.out[...]
        if level == 4:
            self.joined[self.line] = self.gathered[...].reshape(self.part, C_OUT)
        if level == 5:
            self.full[self.core] = self.joined[...].reshape(self.half, C_OUT)
        for copy in self.copies(level):
            copy.start()

    def end(self, level):
        for copy in self.copies(level):
            copy.wait()
        if level == 0:
            own = self.source[self.rows(self.core, self.half), :].astype(f32)
            self.here[...] = (own + self.firsts[...].astype(f32)).astype(bf16)
        if level == 1:
            own = self.here[self.rows(self.line, self.part), :].astype(f32)
            for d in range(1, self.lines):
                own = own + self.seconds[lax.rem(self.line + d, self.lines)].astype(f32)
            self.up[...] = own.astype(bf16)
        if level == 2:
            own = self.up[self.rows(self.batch, self.piece), :].astype(f32)
            for d in range(1, self.batches):
                own = own + self.thirds[lax.rem(self.batch + d, self.batches)].astype(f32)
            self.out[...] = own.astype(bf16)

    def next(self, level):
        self.end(level)
        if level < 5:
            self.start(level + 1)


def conv_back(
    cg_ref, left_ref, right_ref, taps_ref, h_ref, m_ref, st_ref, norm_ref, xg_ref, grad_ref,
    hg_ref, out_ref, sum_ref, gg_ref,
    fills, ext, sums, fg, gg, *buffers,
):
    step = pl.program_id(0)
    pairs = pl.num_programs(0) // 2
    sharing = Sharing(grad_ref, buffers[6:])
    stats = st_ref[...]
    norm = norm_ref[...]
    mean, rstd, scale, shift = first_moments(stats, norm)

    @pl.when(step == 0)
    def _():
        greet()
        sums[...] = jnp.zeros_like(sums)
        gg[...] = jnp.zeros_like(gg)

    @pl.when(step < pairs)
    def _():
        half_scale, half_shift = 0.5 * scale, 0.5 * shift
        for q in range(2):
            for lane in range(2):
                at = slice(lane * HALF, (lane + 1) * HALF)
                fills[q, lane, pl.ds(7, UNITS, stride=GROUP), :] = left_ref[
                    0, q, 0:UNITS, at
                ].astype(f32)
                fills[q, lane, pl.ds(0, UNITS, stride=GROUP), :] = right_ref[
                    0, q, 0:UNITS, at
                ].astype(f32)
        for q in range(4):
            ext[q + 2] = cg_ref[0, q]
            for start in range(0, JOINTS, CUT):
                rows = slice(start * 2 * GROUP, (start + CUT) * 2 * GROUP)
                tiles = cg_ref[0, q, rows, :].astype(f32).reshape(-1, GROUP, C_OUT)
                fill = jnp.concatenate([fills[q % 2, lane, rows, :] for lane in range(2)], axis=1)
                fill = fill.reshape(-1, GROUP, C_OUT)
                moved = insert_and_roll(tiles, fill, 7 if q >= 2 else 0)
                at = q - 2 if q >= 2 else q + 6
                ext[at, rows, :] = moved.reshape(-1, C_OUT).astype(bf16)
        for p in range(2):
            total = None
            for i in range(5 - p):
                window = ext[4 - i : 8 - i].reshape(4 * ROWS, C_OUT)
                part = dot_nt(window, taps_ref[2 * i + p])
                total = part if total is None else total + part
            for q in range(4):
                c = 2 * q + p
                mask = 0.5 * m_ref[0, c]
                mask = jnp.concatenate([mask, mask], axis=1)[None]
                for start in range(0, JOINTS, CUT):
                    rows = slice(start * 2 * GROUP, (start + CUT) * 2 * GROUP)
                    hidden = h_ref[0, c, rows, :].astype(f32)
                    half = hidden * half_scale + half_shift
                    turn = jnp.tanh(half)
                    slope = (1.0 + turn) * (1.0 + (half - half * turn))
                    slope = (slope.reshape(CUT, 2 * GROUP, C_OUT) * mask).reshape(-1, C_OUT)
                    grad = total[q * ROWS + rows.start : q * ROWS + rows.stop] * slope
                    fg[step, c, rows, :] = grad
                    sums[0] += fold(grad)
                    sums[1] += fold(grad * hidden)

    @pl.when(step >= pairs)
    def _():
        pair = step - pairs
        count_in = stats[4:5]
        back_sum = out_ref[0:1]
        back_norm = rstd * (out_ref[1:2] - mean * back_sum)
        lead = norm[0:1] * rstd
        slope = lead * rstd * back_norm / count_in
        offset = lead * back_sum / count_in - slope * mean
        for c in range(PHASES):
            mask = m_ref[0, c]
            mask = jnp.concatenate([mask, mask], axis=1)[None]
            for start in range(0, JOINTS, CUT):
                rows = slice(start * 2 * GROUP, (start + CUT) * 2 * GROUP)
                hidden = h_ref[0, c, rows, :].astype(f32)
                taken = (hidden * slope + offset).reshape(CUT, 2 * GROUP, C_OUT) * mask
                taken = taken.reshape(-1, C_OUT)
                hg_ref[0, c, rows, :] = (fg[pair, c, rows, :] * lead - taken).astype(bf16)
        gg[...] += dot_tn(
            xg_ref[0].reshape(PHASES * ROWS, SUBSETS * C_IN),
            hg_ref[0].reshape(PHASES * ROWS, C_OUT),
        )

    @pl.when(step == 0)
    def _():
        await_greetings()
        sharing.start(0)

    for level, at in ((0, 1), (1, 3)):

        @pl.when(step == at)
        def _(level=level):
            sharing.next(level)

    @pl.when(step == pairs - 1)
    def _():
        rows = [jnp.sum(sums[k], axis=0, keepdims=True) for k in range(2)]
        rows.append(jnp.zeros((6, C_OUT), f32))
        sharing.end(2)
        out_ref[...] = sum_all(jnp.concatenate(rows, axis=0), as_buffers(buffers[0:6]))
        sharing.start(3)

    for level, at in ((3, pairs + 1), (4, pairs + 3)):

        @pl.when(step == at)
        def _(level=level):
            sharing.next(level)

    @pl.when(step == 2 * pairs - 1)
    def _():
        gg_ref[0 : SUBSETS * C_IN, :] = gg[...].astype(bf16)
        rest = gg_ref.shape[0] - SUBSETS * C_IN
        if rest:
            gg_ref[SUBSETS * C_IN :, :] = jnp.zeros((rest, C_OUT), bf16)
        sharing.end(5)
        sum_ref[...] = sharing.full[...].reshape(sum_ref.shape)


def graph_back(
    hg_ref, xq_ref, sg_ref, wgt_ref, wst_ref, kront_ref, own_ref, grad_ref,
    ig_ref, sum_ref, edge_ref,
    spread, natural, eg, own_grad, *buffers,
):
    step = pl.program_id(0)
    last = pl.num_programs(0) - 1
    sharing = Sharing(grad_ref, buffers[6:])

    @pl.when(step == 0)
    def _():
        greet()
        eg[...] = jnp.zeros_like(eg)
        own_grad[...] = jnp.zeros_like(own_grad)
        spread[...] = jnp.zeros_like(spread)
        await_greetings()
        sharing.start(0)

    own = own_ref[...]
    own = jnp.concatenate([own, own], axis=2)

    def side_by_side(values):
        return jnp.concatenate([values[:, 0:GROUP], values[:, GROUP : 2 * GROUP]], axis=2)

    for c in range(PHASES):
        back = dot(hg_ref[0, c], wgt_ref[...]).reshape(JOINTS, 2 * GROUP, SUBSETS * C_IN)
        for k in range(2):
            lanes = slice((k + 1) * C_IN, (k + 2) * C_IN)
            spread[c % 2, k, 0:HALF_ROWS, :] = (
                side_by_side(back[:, :, lanes]).reshape(HALF_ROWS, 2 * C_IN).astype(bf16)
            )
        direct = side_by_side(back[:, :, 0:C_IN])
        both = spread[c % 2].reshape(2 * C_OUT, C_OUT)
        result = dot(kront_ref[...], both).reshape(JOINTS, GROUP, 2 * C_IN) + direct * own
        if c % 2 == 0:
            short = dot(sg_ref[0, c // 2], wst_ref[...]).reshape(JOINTS, 2 * GROUP, C_IN)
            result = result + side_by_side(short)
        for side in range(2):
            natural[side, :, pl.ds(c, GROUP, stride=PHASES), :] = result[
                :, :, side * C_IN : (side + 1) * C_IN
            ]
        eg[...] += dot_nt(both, xq_ref[0, c])
        seen = xq_ref[0, c, 0:HALF_ROWS, :].astype(f32).reshape(JOINTS, GROUP, 2 * C_IN)
        own_grad[...] += seen * direct
    for side in range(2):
        for joint in range(JOINTS):
            ig_ref[side, joint] = natural[side, joint].astype(bf16)

    for level in range(5):

        @pl.when(step == min(level + 1, 5))
        def _(level=level):
            sharing.next(level)

    @pl.when(step == last)
    def _():
        lines = lax.broadcasted_iota(jnp.int32, (C_OUT, C_OUT), 0)
        spots = lax.broadcasted_iota(jnp.int32, (C_OUT, C_OUT), 1)
        same = lines % GROUP == spots % GROUP
        down = (lax.broadcasted_iota(jnp.int32, (32, C_OUT), 0) == lax.broadcasted_iota(
            jnp.int32, (32, C_OUT), 1
        ) // GROUP).astype(f32)
        sums = jnp.sum(own_grad[...], axis=1)
        sums = jnp.sum(sums, axis=1, keepdims=True)
        row = lax.broadcasted_iota(jnp.int32, (JOINTS, 128), 0)
        col = lax.broadcasted_iota(jnp.int32, (JOINTS, 128), 1)
        packed = jnp.where(row == col, jnp.broadcast_to(sums, (JOINTS, 128)), 0.0)
        packed = jnp.concatenate([packed, jnp.zeros((32 - JOINTS, 128), f32)], axis=0)
        for k in range(2):
            kept = jnp.where(same, eg[k * C_OUT : (k + 1) * C_OUT, :], 0.0)
            narrow = lax.dot_general(
                down, kept, (((1,), (1,)), ((), ())),
                preferred_element_type=f32, precision=lax.Precision.HIGHEST,
            )
            row = lax.broadcasted_iota(jnp.int32, (C_OUT, 128), 0)
            col = lax.broadcasted_iota(jnp.int32, (C_OUT, 128), 1)
            place = (row // GROUP + 32 * (k + 1) == col).astype(f32)
            packed = packed + jnp.dot(
                narrow, place, preferred_element_type=f32, precision=lax.Precision.HIGHEST
            )
        edge_ref[...] = sum_all(packed, as_buffers(buffers[0:6]))
        sharing.end(5)
        sum_ref[...] = sharing.full[...].reshape(sum_ref.shape)


def update(
    grads_ref, graph_grad_ref, edge_grad_ref, gm_ref, st_ref, cs_ref, bk_ref, fs_ref, ig_ref,
    *refs,
):
    groups = [refs[4 * k : 4 * k + 4] for k in range(5)]
    out_ig, out_norm = refs[20:22]
    outs = [refs[22 + 4 * k : 26 + 4 * k] for k in range(5)]
    squares, norm_grad = refs[42:44]
    step = pl.program_id(0)
    taps_rows = TAPS * C_OUT

    def edge_grad(k):
        values = edge_grad_ref[...]
        if k:
            values = pltpu.roll(values, 128 - 32 * k, 1)
        return values[0:JOINTS, 0:JOINTS] * gm_ref[k]

    def apply(group, out, at, gradient, rate, decay):
        factor = squares[0:1, 0:1]
        new = adam_update(*[ref[at] for ref in group], gradient, factor, rate, decay)
        for ref, value in zip(out, new):
            ref[at] = value

    @pl.when(step == 0)
    def _():
        stats = st_ref[...]
        norm = groups[4][0][...]
        mean, rstd, _, _ = first_moments(stats, norm)
        first_sum = fs_ref[0:1]
        first_norm = rstd * (fs_ref[1:2] - mean * first_sum)
        back_sum, back_conv, back_short = back_totals(
            bk_ref[...], second_moments(stats, cs_ref[...])
        )
        norm_grad[...] = jnp.concatenate(
            [first_norm, first_sum, back_conv, back_sum, back_short, back_sum], axis=0
        )
        total = jnp.zeros((GROUP, C_OUT), f32)
        for start in range(0, taps_rows + C_IN, C_IN):
            rows = grads_ref[start : start + C_IN, :].astype(f32)
            total = total + fold(rows * rows)
        for start in range(0, SUBSETS * C_IN, C_IN):
            rows = graph_grad_ref[start : start + C_IN, :].astype(f32)
            total = total + fold(rows * rows)
        whole = jnp.sum(total) + jnp.sum(norm_grad[...] * norm_grad[...])
        for k in range(SUBSETS):
            values = edge_grad(k)
            whole = whole + jnp.sum(values * values)
        size = jnp.sqrt(jnp.full((GROUP, 128), whole, f32))
        squares[...] = jnp.minimum(1.0, clip_limit / (size + 1e-06))
        out_norm[...] = size
        every = (slice(None), slice(None))
        apply(groups[4], outs[4], every, norm_grad[...], rate_small, 0.0)
        for k in range(SUBSETS):
            apply(groups[3], outs[3], k, edge_grad(k), rate_small, 0.0)

    @pl.when(step < TAPS)
    def _():
        rows = grads_ref[pl.ds(pl.multiple_of(step * C_OUT, C_OUT), C_OUT), :].astype(f32)
        apply(groups[1], outs[1], 0, rows.T, rate_matrix, decay_matrix)

    @pl.when(step >= TAPS)
    def _():
        k = step - TAPS
        rows = graph_grad_ref[pl.ds(pl.multiple_of(k * C_IN, C_IN), C_IN), :].astype(f32)
        every = (slice(None), slice(None))
        apply(groups[0], outs[0], every, rows, rate_matrix, decay_matrix)

    @pl.when(step == TAPS)
    def _():
        rows = grads_ref[taps_rows : taps_rows + C_IN, :].astype(f32)
        every = (slice(None), slice(None))
        apply(groups[2], outs[2], every, rows, rate_matrix, decay_matrix)

    out_ig[...] = ig_ref[...]


def whole_spec(shape):
    return pl.BlockSpec(shape, lambda i: (0,) * len(shape))


def lead_spec(shape):
    return pl.BlockSpec(shape, lambda i: (i,) + (0,) * (len(shape) - 1))


def spec(block, index):
    return pl.BlockSpec(block, index)


def by_step(block):
    return spec(block, lambda i: (i,) + (0,) * (len(block) - 1))


def call(body, steps, ins, outs, scratch, name, **more):
    def to_spec(where, shape):
        if where is None:
            return whole_spec(shape)
        return where if isinstance(where, pl.BlockSpec) else by_step(where)

    return pl.pallas_call(
        body,
        grid=(steps,),
        in_specs=[to_spec(where, array.shape) for array, where in ins],
        out_specs=[to_spec(where, shape) for shape, _, where in outs],
        out_shape=[jax.ShapeDtypeStruct(shape, kind) for shape, kind, _ in outs],
        scratch_shapes=scratch,
        compiler_params=params(**more),
        name=name,
    )(*[array for array, _ in ins])


def shards(
    inputs, cotangent, lengths, frame_mask, subsets,
    graph_weight, graph_moment, graph_square, graph_average,
    temporal_weight, temporal_moment, temporal_square, temporal_average,
    shortcut_weight, shortcut_moment, shortcut_square, shortcut_average,
    edge_weight, edge_moment, edge_square, edge_average,
    norm_params, norm_moment, norm_square, norm_average,
):
    clips = inputs.shape[0]
    frames = inputs.shape[1]
    pairs = clips // 2
    natural = jnp.transpose(inputs, (0, 2, 1, 3))
    cot = jnp.transpose(cotangent, (0, 2, 1, 3))

    x_block = (2, JOINTS, frames, C_IN)
    mask_block = (1, PHASES, 2 * GROUP, 128)
    wide_block = (1, PHASES, ROWS, C_OUT)
    out_block = (1, 4, ROWS, C_OUT)
    xe_block = (1, 4, ROWS, C_IN)
    a_block = (1, 2, 8, ROWS, C_OUT)
    rim_block = (1, 2, 64, C_OUT)
    xg_block = (1, PHASES, ROWS, SUBSETS * C_IN)
    xq_block = (1, PHASES, C_OUT, C_OUT)
    cot_block = (2, JOINTS, frames // 2, C_OUT)
    edge_block = (1, JOINTS, 2 * GROUP, C_IN)
    small = (8, C_OUT)
    dma = pltpu.SemaphoreType.DMA

    def full(block):
        return (pairs,) + block[1:]

    vmem = pl.BlockSpec(memory_space=pltpu.VMEM)
    shapes = [
        ((clips * frames, 128), f32),
        ((clips * GROUP, 128), f32),
        ((2 * HALF_ROWS, C_OUT), bf16),
        ((HALF_ROWS, 2 * C_OUT), bf16),
        ((JOINTS, GROUP, C_IN), f32),
        ((SUBSETS, JOINTS, JOINTS), f32),
        ((SUBSETS * C_IN, C_OUT), bf16),
        ((C_OUT, SUBSETS * C_IN), bf16),
        ((C_IN, C_OUT), bf16),
        ((C_OUT, C_IN), bf16),
        ((TAPS, C_OUT, C_OUT), bf16),
    ]
    masks, edge_masks, kron, kront, own, graph_mask, wg, wgt, ws, wst, taps = pl.pallas_call(
        prepare,
        in_specs=[pl.BlockSpec(memory_space=pltpu.SMEM)] + [vmem] * 6,
        out_specs=[vmem] * 11,
        out_shape=[jax.ShapeDtypeStruct(shape, kind) for shape, kind in shapes],
        compiler_params=pltpu.CompilerParams(vmem_limit_bytes=60 * 2**20),
        name="prepare",
    )(lengths, frame_mask, subsets, edge_weight, graph_weight, shortcut_weight, temporal_weight)
    masks = masks.reshape(pairs, PHASES, 2 * GROUP, 128)

    xg, xq, xe, hidden, stats, rims, rim_mask = call(
        graph_forward,
        pairs,
        [
            (natural, x_block),
            (masks, mask_block),
            (edge_masks, None),
            (kron, None),
            (own, None),
            (wg, None),
            (ws, None),
        ],
        [
            (full(xg_block), bf16, xg_block),
            (full(xq_block), bf16, xq_block),
            (full(xe_block), bf16, xe_block),
            (full(wide_block), bf16, wide_block),
            (small, f32, None),
            (full(edge_block), bf16, None),
            (edge_masks.shape, f32, None),
        ],
        [
            pltpu.VMEM((2, JOINTS, frames, C_IN), f32),
            pltpu.VMEM((4, GROUP, C_OUT), f32),
            pltpu.VMEM((2, 2 * GROUP, 128), f32),
            pltpu.VMEM(full(edge_block), bf16),
            pltpu.VMEM(full(edge_block), bf16),
            pltpu.VMEM(full(edge_block), bf16),
            pltpu.VMEM(edge_masks.shape, f32),
            pltpu.VMEM(edge_masks.shape, f32),
        ]
        + [dma((pairs + 1,))] * 4
        + sum_scratch(),
        "graph_forward",
        collective_id=1,
        has_side_effects=True,
    )

    active, conv, conv_stats = call(
        conv_forward,
        pairs,
        [
            (hidden, wide_block),
            (rims, edge_block),
            (masks, mask_block),
            (rim_mask, (2 * GROUP, 128)),
            (stats, None),
            (norm_params, None),
            (kron, None),
            (own, None),
            (wg, None),
            (taps, None),
        ],
        [
            (full(a_block), bf16, a_block),
            (full(out_block), f32, out_block),
            (small, f32, None),
        ],
        [
            pltpu.VMEM((C_OUT, C_OUT), bf16),
            pltpu.VMEM((2, ROWS, HALF), f32),
            pltpu.VMEM((4, 2, ROWS, HALF), f32),
            pltpu.VMEM((2, GROUP, C_OUT), f32),
        ]
        + sum_scratch(),
        "conv_forward",
        collective_id=2,
        has_side_effects=True,
    )

    outputs, upstream, back = call(
        output_part,
        pairs,
        [
            (conv, out_block),
            (xe, xe_block),
            (cot, cot_block),
            (masks, mask_block),
            (stats, None),
            (conv_stats, None),
            (norm_params, None),
            (ws, None),
        ],
        [
            (cot.shape, bf16, cot_block),
            (full(out_block), f32, out_block),
            (small, f32, None),
        ],
        [
            pltpu.VMEM((2, 2, JOINTS, frames // 2, HALF), f32),
            pltpu.VMEM((2, 2, JOINTS, frames // 2, HALF), f32),
            pltpu.VMEM((3, GROUP, C_OUT), f32),
        ],
        "output_part",
    )

    grad_rows = Sharing.padded(TAPS * C_OUT + C_IN)
    conv_grad, short_grad, left_rim, right_rim, grads, back = call(
        weight_part,
        pairs,
        [
            (conv, out_block),
            (upstream, out_block),
            (xe, xe_block),
            (active, a_block),
            (masks, mask_block),
            (stats, None),
            (conv_stats, None),
            (back, None),
            (norm_params, None),
            (ws, None),
        ],
        [
            (full(out_block), bf16, out_block),
            (full(out_block), bf16, out_block),
            (full(rim_block), bf16, None),
            (full(rim_block), bf16, None),
            ((grad_rows, C_OUT), bf16, None),
            (small, f32, None),
        ],
        [
            pltpu.VMEM((C_OUT, 4 * ROWS), bf16),
            pltpu.VMEM((2, ROWS, HALF), f32),
            pltpu.VMEM((TAPS, C_OUT, C_OUT), f32),
            pltpu.VMEM((C_IN, C_OUT), f32),
        ]
        + [pltpu.VMEM(full(rim_block), bf16)] * 4
        + [dma((pairs,))] * 4
        + sum_scratch(),
        "weight_part",
        collective_id=3,
        has_side_effects=True,
    )

    def early(block):
        return spec(block, lambda i: (jnp.minimum(i, pairs - 1),) + (0,) * (len(block) - 1))

    def late(block):
        return spec(block, lambda i: (jnp.maximum(i - pairs, 0),) + (0,) * (len(block) - 1))

    def twice(block):
        return spec(block, lambda i: (lax.rem(i, pairs),) + (0,) * (len(block) - 1))

    graph_rows = Sharing.padded(SUBSETS * C_IN)
    hidden_grad, first_sums, grad_sums, graph_grad = call(
        conv_back,
        2 * pairs,
        [
            (conv_grad, early(out_block)),
            (left_rim, early(rim_block)),
            (right_rim, early(rim_block)),
            (taps, None),
            (hidden, twice(wide_block)),
            (masks, twice(mask_block)),
            (stats, None),
            (norm_params, None),
            (xg, late(xg_block)),
            (grads, None),
        ],
        [
            (full(wide_block), bf16, late(wide_block)),
            (small, f32, None),
            ((grad_rows, C_OUT), bf16, None),
            ((graph_rows, C_OUT), bf16, None),
        ],
        [
            pltpu.VMEM((2, 2, ROWS, HALF), f32),
            pltpu.VMEM((8, ROWS, C_OUT), bf16),
            pltpu.VMEM((2, GROUP, C_OUT), f32),
            pltpu.VMEM(full(wide_block), f32),
            pltpu.VMEM((SUBSETS * C_IN, C_OUT), f32),
        ]
        + sum_scratch()
        + Sharing.scratch(grad_rows),
        "conv_back",
        collective_id=4,
        has_side_effects=True,
    )

    input_grad, graph_sum, edge_sum = call(
        graph_back,
        pairs,
        [
            (hidden_grad, wide_block),
            (xq, xq_block),
            (short_grad, out_block),
            (wgt, None),
            (wst, None),
            (kront, None),
            (own, None),
            (graph_grad, None),
        ],
        [
            (natural.shape, bf16, x_block),
            ((graph_rows, C_OUT), bf16, None),
            ((32, 128), f32, None),
        ],
        [
            pltpu.VMEM((2, 2, C_OUT, C_OUT), bf16),
            pltpu.VMEM((2, JOINTS, frames, C_IN), f32),
            pltpu.VMEM((2 * C_OUT, C_OUT), f32),
            pltpu.VMEM((JOINTS, GROUP, 2 * C_IN), f32),
        ]
        + sum_scratch((32, 128))
        + Sharing.scratch(graph_rows),
        "graph_back",
        collective_id=5,
        has_side_effects=True,
    )

    tap_spec = spec((1, C_OUT, C_OUT), lambda i: (jnp.minimum(i, TAPS - 1), 0, 0))
    graph_spec = spec((C_IN, C_OUT), lambda i: (0, jnp.maximum(i - TAPS, 0)))
    states = [
        (graph_weight, graph_moment, graph_square, graph_average),
        (temporal_weight, temporal_moment, temporal_square, temporal_average),
        (shortcut_weight, shortcut_moment, shortcut_square, shortcut_average),
        (edge_weight, edge_moment, edge_square, edge_average),
        (norm_params, norm_moment, norm_square, norm_average),
    ]
    places = [graph_spec, tap_spec, None, None, None]
    state_ins = [(array, place) for group, place in zip(states, places) for array in group]
    clip_block = (1, JOINTS, frames, C_IN)
    clip_spec = spec(clip_block, lambda i: (jnp.minimum(i, clips - 1), 0, 0, 0))
    new = call(
        update,
        max(clips, TAPS + SUBSETS),
        [
            (grad_sums, None),
            (graph_sum, None),
            (edge_sum, None),
            (graph_mask, None),
            (stats, None),
            (conv_stats, None),
            (back, None),
            (first_sums, None),
            (input_grad, clip_spec),
        ]
        + state_ins,
        [(natural.shape, bf16, clip_spec), ((GROUP, 128), f32, None)]
        + [(array.shape, f32, place) for array, place in state_ins],
        [pltpu.VMEM((GROUP, 128), f32), pltpu.VMEM((6, C_OUT), f32)],
        "update",
    )
    return (
        jnp.transpose(outputs, (0, 2, 1, 3)),
        jnp.transpose(new[0], (0, 2, 1, 3)),
        new[1][0, 0:1],
        *new[2:],
    )


def solution(mesh):
    rows = P("batch", "tm", None, None)
    in_specs = (rows, rows, P("batch"), P("batch", "tm")) + (P(),) * 21
    out_specs = (rows, rows) + (P(),) * 21
    return jax.shard_map(shards, mesh=mesh, in_specs=in_specs, out_specs=out_specs, check_vma=False)
```

time: 559 us -> 233 us (0.42); the launches traced: 550 us -> 233 us
  blocking collectives: 207 us -> 0 us
  Pallas kernels: 139 us -> 231 us
  waiting for transfers between devices: 74.5 us -> 0 us
  local copies, waits for them, and re-layouts: 64.2 us -> 1.19 us
  other arithmetic: 31.1 us -> 0 us
  between operations: 19.3 us -> 0.71 us
  starting transfers between devices: 14.9 us -> 0 us
    psum x5 -> x0, blocking collectives: 207 us -> none  [the longest x1 43.1 us: shards(): first_sums = lax.psum(first_sums, ('batch', 'tm'))]
    pallas_call x6 -> x8, Pallas kernels: 139 us -> 231 us  [the longest x7 227 us: call(): pl.pallas_call(body, grid=(steps,), in_specs=[to_spec(where, array.shape)...]
    psum x1 -> x0, waiting for transfers between devices: 74.5 us -> none  [shards(): lax.psum((graph_grad, temporal_grad, shortcut_grad, edge_grad), ('batch',...]
    unnamed x99 -> x0, local copies, waits for them, and re-layouts: 33.6 us -> none
    ppermute x6 -> x0, starting transfers between devices: 14.8 us -> none  [the longest x1 5.02 us: shards(): mask_before = lax.ppermute(mask_in[:, -4:], 'tm', forward)]
    add x7 -> x0, other arithmetic: 12.5 us -> none  [the longest x5 12.5 us: adam_update(): average_new = average_decay * average + (1.0 - average_decay) * weight_new]
    reduce_sum x8 -> x0, other arithmetic: 11.3 us -> none  [the longest x1 3.8 us: shards(): edge_off = jnp.einsum('kwrvr->kvw', edge_wide)]
    mul x5 -> x0, local copies, waits for them, and re-layouts: 11.3 us -> none  [the longest x4 7.11 us: shards(): graph_low[1:].transpose(1, 0, 2)[:, None, :, :, None]]
  transfers between devices with their start and end apart: 7 -> 0, of which waited for: 1 -> 0; matrix products, arithmetic and copies ran while one was open for 9% -> 0% of each run, Pallas kernels for 3% -> 0%
where the time goes in v2:
time: 233 us
  Pallas kernels  231 us (99%)
    pallas_call x7, Pallas kernels, call(): pl.pallas_call(body, grid=(steps,), in_specs=[to_spec(where, array.shape)...  227 us

profile of v2, /device:TPU:0, one launch (start us, length us, event | category | flops | bytes accessed | tf_op | source)
XLA Modules:
  0.0 232.8 jit_solution(2749812565933452375)
XLA Ops:
  0.7 4.0 %prepare.1 = (f32[768,128]{1,0:T(8,128)}, f32[96,128]{1,0:T(8,128)}, bf16[400,256]{1,0:T(8,128)(2,1)}, bf16[200,512]{1,0:T(8,128)(2,1)}, f32[25,8,128]{2,1,0:T(8...) custom-call(s32[12]{0:T(128)} %length_ref.1, ...), custom_call_target="tpu_custom_call" | custom-call | tf_op jit(solution)/shard_map/prepare/pallas_call | solution.py:1117
  4.6 30.9 %graph_forward.1 = (bf16[6,8,400,384]{3,2,1,0:T(8,128)(2,1)}, bf16[6,8,256,256]{3,2,1,0:T(8,128)(2,1)}, bf16[6,4,400,128]{3,2,1,0:T(8,128)(2,1)}, bf16[6,8,400,2...) custom-call(bf16[12,25,64,128]{3,2,1,0:T(8,128)(2,1)} %bitcast.11, ...), custom_call_target="tpu_custom_call" | custom-call | tf_op jit(solution)/shard_map/graph_forward/pallas_call | solution.py:1060
  35.5 30.0 %conv_forward.1 = (bf16[6,2,8,400,256]{4,3,2,1,0:T(8,128)(2,1)}, f32[6,4,400,256]{3,2,1,0:T(8,128)}, f32[8,256]{1,0:T(8,128)}) custom-call(bf16[6,8,400,256]{3,2,1,0:T(8,128)(2,1)} %get-tuple-element.88.h_ref, bf16[6,25,16,128]{3,2,1,0:T(8,128)(2,1)} %get-tuple-element.89.xh_ref, f32[6,8,16,128]{3,2,1,0:T(8,128)} %bitcast.7, ...), custom_call_target="tpu_custom_call" | custom-call | tf_op jit(solution)/shard_map/conv_forward/pallas_call | solution.py:1060
  65.6 15.8 %output_part.1 = (bf16[12,25,32,256]{3,2,1,0:T(8,128)(2,1)}, f32[6,4,400,256]{3,2,1,0:T(8,128)}, f32[8,256]{1,0:T(8,128)}) custom-call(f32[6,4,400,256]{3,2,1,0:T(8,128)} %get-tuple-element.93.conv_ref, bf16[6,4,400,128]{3,2,1,0:T(8,128)(2,1)} %get-tuple-element.94.xe_ref, bf16[12,25,32,256]{3,2,1,0:T(8,128)(2,1)} %bitcast.12, f32[6,8,16,128]{3,2,1,0:T(8,128)} %bitcast.8, ...), custom_call_target="tpu_custom_call" | custom-call | tf_op jit(solution)/shard_map/output_part/pallas_call | solution.py:1060
  81.3 37.1 %weight_part.1 = (bf16[6,4,400,256]{3,2,1,0:T(8,128)(2,1)}, bf16[6,4,400,256]{3,2,1,0:T(8,128)(2,1)}, bf16[6,2,64,256]{3,2,1,0:T(8,128)(2,1)}, bf16[6,2,64,256]{...) custom-call(f32[6,4,400,256]{3,2,1,0:T(8,128)} %get-tuple-element.93.conv_ref, ...), custom_call_target="tpu_custom_call" | custom-call | tf_op jit(solution)/shard_map/weight_part/pallas_call | solution.py:1060
  118.5 55.3 %conv_back.1 = (bf16[6,8,400,256]{3,2,1,0:T(8,128)(2,1)}, f32[8,256]{1,0:T(8,128)}, bf16[2560,256]{1,0:T(8,128)(2,1)}, bf16[512,256]{1,0:T(8,128)(2,1)}) custom-call(bf16[6,4,400,256]{3,2,1,0:T(8,128)(2,1)} %get-tuple-element.100.cg_ref, bf16[6,2,64,256]{3,2,1,0:T(8,128)(2,1)} %get-tuple-element.101.left_ref, ...), custom_call_target="tpu_custom_call" | custom-call | tf_op jit(solution)/shard_map/conv_back/pallas_call | solution.py:1060
  173.8 39.5 %graph_back.1 = (bf16[12,25,64,128]{3,2,1,0:T(8,128)(2,1)}, bf16[512,256]{1,0:T(8,128)(2,1)}, f32[32,128]{1,0:T(8,128)}) custom-call(bf16[6,8,400,256]{3,2,1,0:T(8,128)(2,1)} %get-tuple-element.106.hg_ref, bf16[6,8,256,256]{3,2,1,0:T(8,128)(2,1)} %get-tuple-element.107.xq_ref, bf16[6,4,400,256]{3,2,1,0:T(8,128)(2,1)} %get-tuple-element.108.sg_ref, ...), custom_call_target="tpu_custom_call" | custom-call | tf_op jit(solution)/shard_map/graph_back/pallas_call | solution.py:1060
  213.2 18.4 %update.1 = (bf16[12,25,64,128]{3,2,1,0:T(8,128)(2,1)}, f32[8,128]{1,0:T(8,128)}, f32[128,768]{1,0:T(8,128)}, f32[128,768]{1,0:T(8,128)}, f32[128,768]{1,0:T(8,1...) custom-call(bf16[2560,256]{1,0:T(8,128)(2,1)} %get-tuple-element.105, ...), custom_call_target="tpu_custom_call" | custom-call | tf_op jit(solution)/shard_map/update/pallas_call | solution.py:1060
  231.6 1.2 slice.3

commit v3 on v2

v3 whole, which is shorter than its diff:
```python
import functools

import jax
import jax.numpy as jnp
from jax import lax
from jax.experimental import pallas as pl
from jax.experimental.pallas import tpu as pltpu
from jax.sharding import PartitionSpec as P

C_IN = 128
C_OUT = 256
JOINTS = 25
SUBSETS = 3
TAPS = 9
GROUP = 8
PHASES = 8
UNITS = 2 * JOINTS
ROWS = UNITS * GROUP
HALF_ROWS = JOINTS * GROUP
HALF = C_IN
CUT = 5
DEPTH = 4 * ROWS + 64

f32 = jnp.float32
bf16 = jnp.bfloat16

norm_epsilon = 1e-05
beta_first = 0.9
beta_second = 0.999
adam_epsilon = 1e-08
clip_limit = 1.0
average_decay = 0.9
rate_matrix = 0.05
rate_small = 0.3
decay_matrix = 0.01
steps_taken = 3.0


def params(**more):
    return pltpu.CompilerParams(
        vmem_limit_bytes=60 * 2**20, dimension_semantics=("arbitrary",), **more
    )


def adjacency(subsets):
    linked = (subsets > 0).astype(f32)
    degree = jnp.sum(linked, axis=0)
    labels = jnp.arange(SUBSETS, dtype=jnp.int32) + 1
    chosen = (subsets[None, :, :] == labels[:, None, None]).astype(f32)
    return chosen / degree[None, None, :]


def adam_update(weight, moment, square, average, gradient, factor, rate, decay):
    fix_first = 1.0 - beta_first**steps_taken
    fix_second = 1.0 - beta_second**steps_taken
    clipped = gradient * factor
    moment_new = beta_first * moment + (1.0 - beta_first) * clipped
    square_new = beta_second * square + (1.0 - beta_second) * clipped * clipped
    scaled = square_new * (1.0 / fix_second)
    below = scaled * lax.rsqrt(scaled) + adam_epsilon
    guess = pl.reciprocal(below, approx=True)
    guess = guess * (2.0 - below * guess)
    stepped = moment_new * (1.0 / fix_first) * guess
    weight_new = weight - rate * (stepped + decay * weight)
    average_new = average_decay * average + (1.0 - average_decay) * weight_new
    return (weight_new, moment_new, square_new, average_new)


def dot(a, b):
    return jnp.dot(a, b, preferred_element_type=f32)


def dot_nt(a, b):
    return lax.dot_general(a, b, (((1,), (1,)), ((), ())), preferred_element_type=f32)


def dot_tn(a, b):
    return lax.dot_general(a, b, (((0,), (0,)), ((), ())), preferred_element_type=f32)


def fold(values):
    return jnp.sum(values.reshape(-1, GROUP, values.shape[-1]), axis=0)


MESH = pl.DeviceIdType.MESH


def peers(axis):
    count = lax.axis_size(axis)
    here = lax.axis_index(axis)
    return [(d, {axis: lax.rem(here + d, count)}) for d in range(1, count)]


def greet():
    barrier = pltpu.get_barrier_semaphore()
    for axis in ("tm", "batch"):
        for _, device in peers(axis):
            pl.semaphore_signal(barrier, inc=1, device_id=device, device_id_type=MESH)


def await_greetings():
    count = lax.axis_size("tm") + lax.axis_size("batch") - 2
    pl.semaphore_wait(pltpu.get_barrier_semaphore(), count)


class Total:
    def __init__(self, buffers):
        self.levels = list(zip(("tm", "batch"), (buffers[0:3], buffers[3:6])))

    def copies(self, level):
        axis, (slots, sent, received) = self.levels[level]
        here = lax.axis_index(axis)
        return [
            remote(slots.at[here], slots.at[here], sent.at[d], received.at[d], device)
            for d, device in peers(axis)
        ]

    def start(self, level, values):
        axis, (slots, _, _) = self.levels[level]
        slots[lax.axis_index(axis)] = values
        for copy in self.copies(level):
            copy.start()

    def end(self, level):
        axis, (slots, _, _) = self.levels[level]
        for copy in self.copies(level):
            copy.wait()
        values = slots[0]
        for k in range(1, lax.axis_size(axis)):
            values = values + slots[k]
        return values


def sum_all(values, buffers):
    total = Total(buffers)
    total.start(0, values)
    total.start(1, total.end(0))
    return total.end(1)


def sum_scratch(shape=(8, C_OUT)):
    found = []
    for axis in ("tm", "batch"):
        count = lax.axis_size(axis)
        found += [
            pltpu.VMEM((count, *shape), f32),
            pltpu.SemaphoreType.DMA((count,)),
            pltpu.SemaphoreType.DMA((count,)),
        ]
    return found


def remote(source, target, sent, received, device):
    return pltpu.make_async_remote_copy(
        src_ref=source,
        dst_ref=target,
        send_sem=sent,
        recv_sem=received,
        device_id=device,
        device_id_type=MESH,
    )


def with_neighbours(step, low, high, from_left, from_right, sems, act):
    here = lax.axis_index("tm")
    last = lax.axis_size("tm") - 1
    sent_right, got_left, sent_left, got_right = sems

    def rightward():
        return remote(high, from_left, sent_right.at[step], got_left.at[step], {"tm": here + 1})

    def leftward():
        return remote(low, from_right, sent_left.at[step], got_right.at[step], {"tm": here - 1})

    if act == "start":

        @pl.when(here < last)
        def _():
            rightward().start()

        @pl.when(here > 0)
        def _():
            leftward().start()

    else:

        @pl.when(here < last)
        def _():
            rightward().wait_send()
            leftward().wait_recv()

        @pl.when(here > 0)
        def _():
            leftward().wait_send()
            rightward().wait_recv()


def first_moments(stats, norm):
    count_in = stats[4:5]
    mean = stats[0:1] / count_in
    rstd = lax.rsqrt(stats[1:2] / count_in - mean * mean + norm_epsilon)
    return mean, rstd, norm[0:1] * rstd, norm[1:2] - norm[0:1] * rstd * mean


def one_hot_rows(rows, columns):
    row = lax.broadcasted_iota(jnp.int32, (rows, columns), 0)
    col = lax.broadcasted_iota(jnp.int32, (rows, columns), 1)
    return (row // GROUP == col).astype(bf16)


def prepare(
    length_ref, frame_ref, subset_ref, edge_ref, graph_ref, short_ref, taps_ref,
    m_ref, em_ref, kron_ref, kront_ref, own_ref, gm_ref, wg_ref, wgt_ref, ws_ref, wst_ref, low_ref,
):
    clips, frames = frame_ref.shape
    first = lax.axis_index("tm") * frames
    row = lax.broadcasted_iota(jnp.int32, (clips, frames), 0)
    ids = lax.broadcasted_iota(jnp.int32, (clips, frames), 1) + first
    ends = jnp.zeros((clips, frames), jnp.int32)
    for clip in range(clips):
        ends = jnp.where(row == clip, length_ref[clip], ends)
    mask = ((ids < ends) & (frame_ref[...] > 0)).astype(bf16)
    every = jnp.ones((frames, 128), bf16)

    def spread(rows, clip_of, frame_of):
        at = lax.broadcasted_iota(jnp.int32, (rows, clips), 0)
        chosen = (clip_of(at) == lax.broadcasted_iota(jnp.int32, (rows, clips), 1)).astype(bf16)
        lines = dot(chosen, mask)
        at = lax.broadcasted_iota(jnp.int32, (rows, frames), 0)
        kept = frame_of(at) == lax.broadcasted_iota(jnp.int32, (rows, frames), 1)
        return dot(jnp.where(kept, lines, 0.0).astype(bf16), every)

    side = 2 * GROUP
    m_ref[...] = spread(
        clips * frames,
        lambda at: 2 * (at // (PHASES * side)) + at // GROUP % 2,
        lambda at: PHASES * (at % GROUP) + at // side % PHASES,
    )
    em_ref[...] = spread(
        clips * GROUP, lambda at: at // GROUP, lambda at: (at % GROUP + frames - 4) % frames
    )
    subsets = subset_ref[...]
    degree = jnp.sum((subsets > 0).astype(f32), axis=0, keepdims=True)
    lift = one_hot_rows(HALF_ROWS, JOINTS)
    row = lax.broadcasted_iota(jnp.int32, (JOINTS, C_OUT), 0)
    drop = (row == lax.broadcasted_iota(jnp.int32, (JOINTS, C_OUT), 1) // GROUP).astype(bf16)
    row = lax.broadcasted_iota(jnp.int32, (HALF_ROWS, C_OUT), 0)
    same = row % GROUP == lax.broadcasted_iota(jnp.int32, (HALF_ROWS, C_OUT), 1) % GROUP
    for k in range(SUBSETS):
        share = (subsets == k + 1).astype(f32) / degree
        gm_ref[k] = share
        low = (share * edge_ref[k]).astype(bf16)
        if k == 0:
            row = lax.broadcasted_iota(jnp.int32, (JOINTS, JOINTS), 0)
            col = lax.broadcasted_iota(jnp.int32, (JOINTS, JOINTS), 1)
            diagonal = jnp.sum(jnp.where(row == col, low.astype(f32), 0.0), axis=1, keepdims=True)
            wide = jnp.broadcast_to(diagonal, (JOINTS, C_IN)).astype(bf16)
            own_ref[...] = dot(lift, wide).reshape(JOINTS, GROUP, C_IN)
        else:
            ahead = dot(lift, dot_tn(low, drop).astype(bf16))
            rows = slice((k - 1) * HALF_ROWS, k * HALF_ROWS)
            kron_ref[rows, :] = jnp.where(same, ahead, 0.0).astype(bf16)
            behind = dot(lift, dot(low, drop).astype(bf16))
            lanes = slice((k - 1) * C_OUT, k * C_OUT)
            kront_ref[:, lanes] = jnp.where(same, behind, 0.0).astype(bf16)
        block = graph_ref[:, k * C_OUT : (k + 1) * C_OUT]
        wg_ref[k * C_IN : (k + 1) * C_IN, :] = block.astype(bf16)
        wgt_ref[:, k * C_IN : (k + 1) * C_IN] = block.T.astype(bf16)
    ws_ref[...] = short_ref[...].astype(bf16)
    wst_ref[...] = short_ref[...].T.astype(bf16)
    low_ref[...] = taps_ref[...].astype(bf16)


def mix_rows(parts, scales, kron_ref, wide_ref):
    mixed = dot(kron_ref[...], wide_ref[...])
    sides = []
    for side in range(2):
        lanes = slice(side * HALF, (side + 1) * HALF)
        sides.append(
            jnp.concatenate(
                [
                    parts[side] * scales,
                    mixed[0:HALF_ROWS, lanes].reshape(JOINTS, GROUP, C_IN),
                    mixed[HALF_ROWS : 2 * HALF_ROWS, lanes].reshape(JOINTS, GROUP, C_IN),
                ],
                axis=2,
            )
        )
    return jnp.concatenate(sides, axis=1).reshape(ROWS, SUBSETS * C_IN).astype(bf16)


def put_wide(parts, wide_ref):
    wide = jnp.concatenate([part.reshape(HALF_ROWS, C_IN) for part in parts], axis=1)
    wide_ref[0:HALF_ROWS, :] = wide.astype(bf16)


def graph_forward(
    x_ref, head_ref, tail_ref, m_ref, em_ref, kron_ref, own_ref, wg_ref, ws_ref,
    xq_ref, xe_ref, h_ref, st_ref, rim_ref, rim_mask_ref,
    xs, xg, xe, sums, counts, mine, lefts, rights, mask_lefts, mask_rights,
    sent_right, got_left, sent_left, got_right, *sum_buffers,
):
    step = pl.program_id(0)
    last = pl.num_programs(0) - 1
    sems = (sent_right, got_left, sent_left, got_right)

    def rims(act):
        with_neighbours(0, mine, mine, lefts, rights, sems, act)
        with_neighbours(1, em_ref, em_ref, mask_lefts, mask_rights, sems, act)

    @pl.when(step == 0)
    def _():
        for ref in (lefts, rights, mask_lefts, mask_rights):
            ref[...] = jnp.zeros_like(ref)
        greet()
        for pair in range(mine.shape[0]):
            ends = []
            for clip in (2 * pair, 2 * pair + 1):
                above = pltpu.roll(tail_ref[clip].astype(f32)[:, GROUP:], 4, 1)
                below = pltpu.roll(head_ref[clip].astype(f32)[:, :GROUP], 4, 1)
                sub = lax.broadcasted_iota(jnp.int32, above.shape, 1)
                ends.append(jnp.where(sub < 4, above, below))
            mine[pair] = jnp.concatenate(ends, axis=1).astype(bf16)
        sums[...] = jnp.zeros_like(sums)
        counts[...] = jnp.zeros_like(counts)

    def permute():
        for side in range(2):
            for start in range(0, JOINTS, CUT):
                rows = x_ref[side, start : start + CUT].astype(f32)
                rows = jnp.swapaxes(rows.reshape(CUT, GROUP, PHASES, C_IN), 1, 2)
                for c in range(PHASES):
                    mask = m_ref[0, c, side * GROUP : (side + 1) * GROUP]
                    xs[c, side, start : start + CUT] = rows[:, c] * mask[None]

    def mix(c):
        xq_ref[0, c, HALF_ROWS:, :] = jnp.zeros((C_OUT - HALF_ROWS, C_OUT), bf16)
        parts = [xs[c, 0], xs[c, 1]]
        put_wide(parts, xq_ref.at[0, c])
        xg[c] = mix_rows(parts, own_ref[...], kron_ref, xq_ref.at[0, c])
        counts[0] += m_ref[0, c]
        if c % 2 == 0:
            counts[1] += m_ref[0, c]
            even = jnp.concatenate(parts, axis=1).reshape(ROWS, C_IN).astype(bf16)
            xe_ref[0, c // 2] = even
            xe[c // 2] = even

    def project(c):
        hidden = dot(xg[c : c + 2].reshape(2 * ROWS, SUBSETS * C_IN), wg_ref[...])
        h_ref[0, c : c + 2] = hidden.reshape(2, ROWS, C_OUT).astype(bf16)
        sums[0] += fold(hidden)
        sums[1] += fold(hidden * hidden)
        short = dot(xe[c // 2], ws_ref[...])
        sums[2] += fold(short)
        sums[3] += fold(short * short)

    @pl.when(step == 0)
    def _():
        permute()
        for c in range(PHASES):
            mix(c)

    @pl.when((step > 0) & (step < last))
    def _():
        permute()
        for c in range(0, PHASES, 2):
            project(c)
            mix(c)
            mix(c + 1)

    @pl.when(step == last)
    def _():
        for c in range(0, PHASES, 2):
            project(c)

    @pl.when(step == 1)
    def _():
        await_greetings()
        rims("start")

    @pl.when(step == last)
    def _():
        rows = [jnp.sum(sums[k], axis=0, keepdims=True) for k in range(4)]
        for k in range(2):
            total = JOINTS * jnp.sum(counts[k], axis=0, keepdims=True)
            rows.append(jnp.concatenate([total, total], axis=1))
        rows.append(jnp.zeros((2, C_OUT), f32))
        st_ref[...] = sum_all(jnp.concatenate(rows, axis=0), sum_buffers)
        rims("wait")
        sub = lax.broadcasted_iota(jnp.int32, mask_lefts.shape, 0) % GROUP
        rim_mask_ref[...] = jnp.where(sub < 4, mask_lefts[...], mask_rights[...])
        for pair in range(lefts.shape[0]):
            sub = lax.broadcasted_iota(jnp.int32, lefts.shape[1:], 1) % GROUP
            both = jnp.where(sub < 4, lefts[pair].astype(f32), rights[pair].astype(f32))
            rim_ref[pair] = both.astype(bf16)


def insert_and_roll(tiles, fill, side):
    sub = lax.broadcasted_iota(jnp.int32, tiles.shape, 1)
    joined = jnp.where(sub == side, fill, tiles)
    return pltpu.roll(joined, 1 if side == 7 else GROUP - 1, 1)


def conv_forward(
    h_ref, xh_ref, m_ref, mh_ref, st_ref, norm_ref, kron_ref, own_ref, wg_ref, taps_ref,
    a_ref, conv_ref, out_ref,
    pad, rims, fills, sums, *sum_buffers,
):
    step = pl.program_id(0)

    @pl.when(step == 0)
    def _():
        greet()
        sums[...] = jnp.zeros_like(sums)
        pad[...] = jnp.zeros_like(pad)

    _, _, scale, shift = first_moments(st_ref[...], norm_ref[...])
    scale, shift = 0.5 * scale, 0.5 * shift

    def activate(values, mask):
        half = values * scale + shift
        return (half + half * jnp.tanh(half)).reshape(-1, 2 * GROUP, C_OUT) * mask

    def wide(mask):
        return jnp.concatenate([mask, mask], axis=1)[None]

    rim_mask = mh_ref[...]
    rim_rows = xh_ref[0].astype(f32) * rim_mask[None]
    parts = [rim_rows[:, side * GROUP : (side + 1) * GROUP] for side in range(2)]
    put_wide(parts, pad)
    rim_hidden = dot(mix_rows(parts, own_ref[...], kron_ref, pad), wg_ref[...])
    rim_active = activate(rim_hidden, wide(rim_mask)).reshape(ROWS, C_OUT)
    for lane in range(2):
        rims[lane] = rim_active[:, lane * HALF : (lane + 1) * HALF]
    for p in range(2):
        for q in range(2):
            for lane in range(2):
                fills[2 * p + q, lane, pl.ds(7, UNITS, stride=GROUP), :] = rims[
                    lane, pl.ds(2 * q + p, UNITS, stride=GROUP), :
                ]
                fills[2 * p + q, lane, pl.ds(0, UNITS, stride=GROUP), :] = rims[
                    lane, pl.ds(4 + 2 * q + p, UNITS, stride=GROUP), :
                ]

    a_ref[0, 1, 7, 0:64, :] = jnp.zeros((64, C_OUT), bf16)
    for c in range(PHASES):
        p, q = c % 2, c // 2
        mask = wide(m_ref[0, c])
        for start in range(0, JOINTS, CUT):
            rows = slice(start * 2 * GROUP, (start + CUT) * 2 * GROUP)
            active = activate(h_ref[0, c, rows, :].astype(f32), mask)
            a_ref[0, p, q + 2, rows, :] = active.reshape(-1, C_OUT).astype(bf16)
            if p == 1 and q == 1:
                continue
            tiles = active.reshape(-1, GROUP, C_OUT)
            fill = jnp.concatenate(
                [fills[2 * p + q % 2, lane, rows, :] for lane in range(2)], axis=1
            ).reshape(-1, GROUP, C_OUT)
            moved = insert_and_roll(tiles, fill, 7 if q >= 2 else 0)
            at = q - 2 if q >= 2 else q + 6
            a_ref[0, p, at, rows, :] = moved.reshape(-1, C_OUT).astype(bf16)

    total = None
    for j in range(TAPS):
        window = a_ref[0, j % 2, j // 2 : j // 2 + 4].reshape(4 * ROWS, C_OUT)
        part = dot(window, taps_ref[j])
        total = part if total is None else total + part
    conv_ref[0] = total.reshape(4, ROWS, C_OUT)
    for q in range(4):
        block = total[q * ROWS : (q + 1) * ROWS].reshape(JOINTS, 2 * GROUP, C_OUT)
        live = block * wide(m_ref[0, 2 * q])
        sums[0] += fold(live)
        sums[1] += fold(live * block)

    @pl.when(step == pl.num_programs(0) - 1)
    def _():
        await_greetings()
        rows = [jnp.sum(sums[k], axis=0, keepdims=True) for k in range(2)]
        rows.append(jnp.zeros((6, C_OUT), f32))
        out_ref[...] = sum_all(jnp.concatenate(rows, axis=0), sum_buffers)


def second_moments(stats, conv_stats):
    count_out = stats[5:6]
    mean_conv = conv_stats[0:1] / count_out
    rstd_conv = lax.rsqrt(conv_stats[1:2] / count_out - mean_conv * mean_conv + norm_epsilon)
    mean_short = stats[2:3] / count_out
    rstd_short = lax.rsqrt(stats[3:4] / count_out - mean_short * mean_short + norm_epsilon)
    return mean_conv, rstd_conv, mean_short, rstd_short


def back_totals(back, moments):
    mean_conv, rstd_conv, mean_short, rstd_short = moments
    back_sum = back[0:1]
    back_conv = rstd_conv * (back[1:2] - mean_conv * back_sum)
    back_short = rstd_short * (back[2:3] - mean_short * back_sum)
    return back_sum, back_conv, back_short


def middle(
    conv_ref, xe_ref, cot_ref, a_ref, m_ref, st_ref, cs_ref, norm_ref, ws_ref,
    o_ref, cg_ref, sg_ref, left_ref, right_ref, grad_ref, total_ref,
    cots, outs, sums, conv_kept, up_kept, turned, edges, tg, shg, low_rims, high_rims, lefts, rights,
    sent_right, got_left, sent_left, got_right, *sum_buffers,
):
    step = pl.program_id(0)
    pairs = low_rims.shape[0]
    sems = (sent_right, got_left, sent_left, got_right)

    def rims(at, act):
        with_neighbours(
            at, low_rims.at[at], high_rims.at[at], lefts.at[at], rights.at[at], sems, act
        )

    norm = norm_ref[...]
    stats = st_ref[...]
    moments = second_moments(stats, cs_ref[...])
    mean_conv, rstd_conv, mean_short, rstd_short = moments

    @pl.when(step == 0)
    def _():
        for ref in (sums, lefts, rights, tg, shg, turned, low_rims, high_rims):
            ref[...] = jnp.zeros_like(ref)
        greet()

    @pl.when(step < pairs)
    def _():
        scale_conv = 0.5 * norm[2:3] * rstd_conv
        scale_short = 0.5 * norm[4:5] * rstd_short
        shift = 0.5 * (norm[3:4] + norm[5:6]) - scale_conv * mean_conv - scale_short * mean_short
        for side in range(2):
            for joint in range(JOINTS):
                for lane in range(2):
                    cots[side, lane, joint] = cot_ref[
                        side, joint, :, lane * HALF : (lane + 1) * HALF
                    ].astype(f32)
        for q in range(4):
            mask = m_ref[0, 2 * q]
            mask = jnp.concatenate([mask, mask], axis=1)[None]
            short_all = dot(xe_ref[0, q], ws_ref[...])
            for start in range(0, JOINTS, CUT):
                rows = slice(start * 2 * GROUP, (start + CUT) * 2 * GROUP)
                conv = conv_ref[0, q, rows, :]
                conv_kept[step, q, rows, :] = conv
                short = short_all[rows]
                half = conv * scale_conv + short * scale_short + shift
                turn = jnp.tanh(half)
                grow = (0.5 + 0.5 * turn).reshape(CUT, 2 * GROUP, C_OUT) * mask
                half = half.reshape(CUT, 2 * GROUP, C_OUT)
                turn = turn.reshape(CUT, 2 * GROUP, C_OUT)
                result = (half + half) * grow
                slope = grow + grow * (half - half * turn)
                cot = jnp.concatenate(
                    [
                        jnp.concatenate(
                            [
                                cots[side, lane, start : start + CUT, pl.ds(q, GROUP, stride=4), :]
                                for lane in range(2)
                            ],
                            axis=2,
                        )
                        for side in range(2)
                    ],
                    axis=1,
                )
                for side in range(2):
                    for lane in range(2):
                        outs[
                            side, lane, start : start + CUT, pl.ds(q, GROUP, stride=4), :
                        ] = result[
                            :, side * GROUP : (side + 1) * GROUP, lane * HALF : (lane + 1) * HALF
                        ]
                up = (cot * slope).reshape(-1, C_OUT)
                up_kept[step, q, rows, :] = up
                sums[0] += fold(up)
                sums[1] += fold(up * conv)
                sums[2] += fold(up * short)
        for side in range(2):
            for joint in range(JOINTS):
                for lane in range(2):
                    o_ref[side, joint, :, lane * HALF : (lane + 1) * HALF] = outs[
                        side, lane, joint
                    ].astype(bf16)

    @pl.when(step == pairs - 1)
    def _():
        rows = [jnp.sum(sums[k], axis=0, keepdims=True) for k in range(3)]
        rows.append(jnp.zeros((5, C_OUT), f32))
        await_greetings()
        total_ref[...] = sum_all(jnp.concatenate(rows, axis=0), sum_buffers)

    def gradients(pair, q):
        back_sum, back_conv, back_short = back_totals(total_ref[...], moments)
        count_out = stats[5:6]

        def terms(gain, mean, rstd, back):
            lead = gain * rstd
            slope = lead * rstd * back / count_out
            return lead, slope, lead * back_sum / count_out - slope * mean

        lead_c, slope_c, shift_c = terms(norm[2:3], mean_conv, rstd_conv, back_conv)
        lead_s, slope_s, shift_s = terms(norm[4:5], mean_short, rstd_short, back_short)
        mask = m_ref[0, 2 * q]
        mask = jnp.concatenate([mask, mask], axis=1)[None]
        short_all = dot(xe_ref[0, q], ws_ref[...])
        for start in range(0, JOINTS, CUT):
            rows = slice(start * 2 * GROUP, (start + CUT) * 2 * GROUP)
            up = up_kept[pair, q, rows, :]

            def masked(values):
                return (values.reshape(CUT, 2 * GROUP, C_OUT) * mask).reshape(-1, C_OUT)

            cg = up * lead_c - masked(conv_kept[pair, q, rows, :] * slope_c + shift_c)
            cg_ref[0, q, rows, :] = cg.astype(bf16)
            for lane in range(2):
                edges[lane, rows, :] = cg[:, lane * HALF : (lane + 1) * HALF]
            sg = up * lead_s - masked(short_all[rows] * slope_s + shift_s)
            sg_ref[0, q, rows, :] = sg.astype(bf16)
        for lane in range(2):
            at = slice(lane * HALF, (lane + 1) * HALF)
            target = low_rims if q < 2 else high_rims
            outer = edges[lane, pl.ds(0 if q < 2 else 7, UNITS, stride=GROUP), :]
            target[pair, q % 2, 0:UNITS, at] = outer.astype(bf16)

    def turn_over():
        turned[:, 0 : 4 * ROWS] = cg_ref[0].reshape(4 * ROWS, C_OUT).T
        shg[...] += dot_tn(
            xe_ref[0].reshape(4 * ROWS, C_IN), sg_ref[0].reshape(4 * ROWS, C_OUT)
        )

    def taps_of(first, end):
        every = a_ref[0].reshape(16 * ROWS, C_OUT)
        for j in range(first, end):
            at = (8 * (j % 2) + j // 2) * ROWS
            tg[j] += dot(turned[...], every[at : at + DEPTH])

    @pl.when(step == pairs)
    def _():
        for q in range(4):
            gradients(0, q)
        turn_over()

    @pl.when((step > pairs) & (step < 2 * pairs))
    def _():
        for q in range(4):
            taps_of(2 * q, 2 * q + 2)
            gradients(step - pairs, q)
        taps_of(8, 9)
        turn_over()

    @pl.when((step >= pairs) & (step < 2 * pairs))
    def _():
        rims(step - pairs, "start")

    @pl.when(step == 2 * pairs)
    def _():
        taps_of(0, 9)
        for j in range(TAPS):
            grad_ref[j * C_OUT : (j + 1) * C_OUT, :] = tg[j].astype(bf16)
        grad_ref[TAPS * C_OUT : TAPS * C_OUT + C_IN, :] = shg[...].astype(bf16)
        rest = grad_ref.shape[0] - TAPS * C_OUT - C_IN
        if rest:
            grad_ref[TAPS * C_OUT + C_IN :, :] = jnp.zeros((rest, C_OUT), bf16)
        for pair in range(pairs):
            rims(pair, "wait")
        left_ref[...] = lefts[...]
        right_ref[...] = rights[...]


def padded(rows):
    unit = 16 * lax.axis_size("tm") * lax.axis_size("batch")
    return (rows + unit - 1) // unit * unit


class Places:
    def __init__(self, rows):
        tm = lax.axis_index("tm")
        self.core = tm % 2
        self.line = tm // 2
        self.lines = lax.axis_size("tm") // 2
        self.batch = lax.axis_index("batch")
        self.batches = lax.axis_size("batch")
        self.half = rows // 2
        self.part = self.half // self.lines
        self.piece = self.part // self.batches

    def core_peer(self):
        return {"tm": 2 * self.line + 1 - self.core}

    def line_peers(self):
        for d in range(1, self.lines):
            to = lax.rem(self.line + d, self.lines)
            yield d, to, {"tm": 2 * to + self.core}

    def batch_peers(self):
        for d in range(1, self.batches):
            to = lax.rem(self.batch + d, self.batches)
            yield d, to, {"batch": to}

    def rows(self, index, count):
        return pl.ds(pl.multiple_of(index * count, 16), count)


def three_levels(rows):
    lines, batches = lax.axis_size("tm") // 2, lax.axis_size("batch")
    half = rows // 2
    return lines, batches, half, half // lines, half // lines // batches


class Scatter(Places):
    def __init__(self, source, refs):
        super().__init__(source.shape[0])
        self.source = source
        self.here, self.up, self.out, self.firsts, self.seconds, self.thirds = refs[0:6]
        self.sems = refs[6:12]

    @staticmethod
    def scratch(rows):
        lines, batches, half, part, piece = three_levels(rows)
        shapes = ((half,), (part,), (piece,), (half,), (lines, part), (batches, piece))
        found = [pltpu.VMEM((*shape, C_OUT), bf16) for shape in shapes]
        for count in (1, lines, batches):
            found += [pltpu.SemaphoreType.DMA((count,))] * 2
        return found

    def copies(self, level):
        sent, got = self.sems[2 * level], self.sems[2 * level + 1]
        if level == 0:
            source = self.source.at[self.rows(1 - self.core, self.half)]
            return [remote(source, self.firsts, sent.at[0], got.at[0], self.core_peer())]
        if level == 1:
            return [
                remote(
                    self.here.at[self.rows(to, self.part)], self.seconds.at[self.line],
                    sent.at[d], got.at[d], device,
                )
                for d, to, device in self.line_peers()
            ]
        return [
            remote(
                self.up.at[self.rows(to, self.piece)], self.thirds.at[self.batch],
                sent.at[d], got.at[d], device,
            )
            for d, to, device in self.batch_peers()
        ]

    def start(self, level):
        for copy in self.copies(level):
            copy.start()

    def end(self, level):
        for copy in self.copies(level):
            copy.wait()
        if level == 0:
            own = self.source[self.rows(self.core, self.half), :].astype(f32)
            self.here[...] = (own + self.firsts[...].astype(f32)).astype(bf16)
        if level == 1:
            own = self.here[self.rows(self.line, self.part), :].astype(f32)
            for d in range(1, self.lines):
                own = own + self.seconds[lax.rem(self.line + d, self.lines)].astype(f32)
            self.up[...] = own.astype(bf16)
        if level == 2:
            own = self.up[self.rows(self.batch, self.piece), :].astype(f32)
            for d in range(1, self.batches):
                own = own + self.thirds[lax.rem(self.batch + d, self.batches)].astype(f32)
            self.out[...] = own.astype(bf16)


class Gather(Places):
    def __init__(self, rows, refs):
        super().__init__(rows)
        self.gathered, self.joined, self.full = refs[0:3]
        self.sems = refs[3:9]

    @staticmethod
    def scratch(rows):
        lines, batches, half, part, piece = three_levels(rows)
        shapes = ((batches, piece), (lines, part), (2, half))
        found = [pltpu.VMEM((*shape, C_OUT), bf16) for shape in shapes]
        for count in (batches, lines, 1):
            found += [pltpu.SemaphoreType.DMA((count,))] * 2
        return found

    def copies(self, level):
        sent, got = self.sems[2 * level], self.sems[2 * level + 1]
        if level == 0:
            slot = self.gathered.at[self.batch]
            peers_here = self.batch_peers()
        elif level == 1:
            slot = self.joined.at[self.line]
            peers_here = self.line_peers()
        else:
            slot = self.full.at[self.core]
            return [remote(slot, slot, sent.at[0], got.at[0], self.core_peer())]
        return [remote(slot, slot, sent.at[d], got.at[d], device) for d, _, device in peers_here]

    def start(self, level, share=None):
        if level == 0:
            self.gathered[self.batch] = share
        if level == 1:
            self.joined[self.line] = self.gathered[...].reshape(self.part, C_OUT)
        if level == 2:
            self.full[self.core] = self.joined[...].reshape(self.half, C_OUT)
        for copy in self.copies(level):
            copy.start()

    def end(self, level):
        for copy in self.copies(level):
            copy.wait()


def conv_back(
    cg_ref, left_ref, right_ref, taps_ref, h_ref, m_ref, st_ref, norm_ref, xq_ref, kron_ref, own_ref,
    grad_ref,
    hg_ref, out_ref, sum_ref, gg_ref,
    fills, ext, sums, fg, kept, raw, xg, gg, *buffers,
):
    step = pl.program_id(0)
    pairs = pl.num_programs(0) // 2
    scatter = Scatter(grad_ref, buffers[6:])
    stats = st_ref[...]
    norm = norm_ref[...]
    mean, rstd, scale, shift = first_moments(stats, norm)

    @pl.when(step == 0)
    def _():
        greet()
        sums[...] = jnp.zeros_like(sums)
        gg[...] = jnp.zeros_like(gg)

    half_scale, half_shift = 0.5 * scale, 0.5 * shift

    def extend():
        kept[step] = h_ref[0]
        for q in range(2):
            for lane in range(2):
                at = slice(lane * HALF, (lane + 1) * HALF)
                fills[q, lane, pl.ds(7, UNITS, stride=GROUP), :] = left_ref[
                    0, q, 0:UNITS, at
                ].astype(f32)
                fills[q, lane, pl.ds(0, UNITS, stride=GROUP), :] = right_ref[
                    0, q, 0:UNITS, at
                ].astype(f32)
        for q in range(4):
            ext[q + 2] = cg_ref[0, q]
            for start in range(0, JOINTS, CUT):
                rows = slice(start * 2 * GROUP, (start + CUT) * 2 * GROUP)
                tiles = cg_ref[0, q, rows, :].astype(f32).reshape(-1, GROUP, C_OUT)
                fill = jnp.concatenate([fills[q % 2, lane, rows, :] for lane in range(2)], axis=1)
                fill = fill.reshape(-1, GROUP, C_OUT)
                moved = insert_and_roll(tiles, fill, 7 if q >= 2 else 0)
                at = q - 2 if q >= 2 else q + 6
                ext[at, rows, :] = moved.reshape(-1, C_OUT).astype(bf16)

    def convolve(c):
        p, q = c % 2, c // 2
        total = None
        for i in range(5 - p):
            part = dot_nt(ext[4 - i + q], taps_ref[2 * i + p])
            total = part if total is None else total + part
        raw[c] = total

    def activate_back(c):
        mask = 0.5 * m_ref[0, c]
        mask = jnp.concatenate([mask, mask], axis=1)[None]
        for start in range(0, JOINTS, CUT):
            rows = slice(start * 2 * GROUP, (start + CUT) * 2 * GROUP)
            hidden = kept[step - 1, c, rows, :].astype(f32)
            half = hidden * half_scale + half_shift
            turn = jnp.tanh(half)
            slope = (1.0 + turn) * (1.0 + (half - half * turn))
            slope = (slope.reshape(CUT, 2 * GROUP, C_OUT) * mask).reshape(-1, C_OUT)
            grad = raw[c, rows, :] * slope
            fg[step - 1, c, rows, :] = grad
            sums[0] += fold(grad)
            sums[1] += fold(grad * hidden)

    order = (0, 2, 4, 6, 1, 3, 5, 7)

    @pl.when(step == 0)
    def _():
        extend()
        for c in order:
            convolve(c)

    @pl.when((step > 0) & (step < pairs))
    def _():
        extend()
        for c in order:
            activate_back(c)
            convolve(c)

    @pl.when(step == pairs)
    def _():
        for c in order:
            activate_back(c)

    @pl.when(step > pairs)
    def _():
        pair = step - pairs - 1
        count_in = stats[4:5]
        back_sum = out_ref[0:1]
        back_norm = rstd * (out_ref[1:2] - mean * back_sum)
        lead = norm[0:1] * rstd
        slope = lead * rstd * back_norm / count_in
        offset = lead * back_sum / count_in - slope * mean
        for c in range(PHASES):
            mask = m_ref[0, c]
            mask = jnp.concatenate([mask, mask], axis=1)[None]
            for start in range(0, JOINTS, CUT):
                rows = slice(start * 2 * GROUP, (start + CUT) * 2 * GROUP)
                hidden = kept[pair, c, rows, :].astype(f32)
                taken = (hidden * slope + offset).reshape(CUT, 2 * GROUP, C_OUT) * mask
                taken = taken.reshape(-1, C_OUT)
                hg_ref[0, c, rows, :] = (fg[pair, c, rows, :] * lead - taken).astype(bf16)
            seen = xq_ref[0, c, 0:HALF_ROWS, :].astype(f32).reshape(JOINTS, GROUP, 2 * C_IN)
            parts = [seen[:, :, side * C_IN : (side + 1) * C_IN] for side in range(2)]
            xg[c] = mix_rows(parts, own_ref[...], kron_ref, xq_ref.at[0, c])
        gg[...] += dot_tn(
            xg[...].reshape(PHASES * ROWS, SUBSETS * C_IN),
            hg_ref[0].reshape(PHASES * ROWS, C_OUT),
        )

    @pl.when(step == 0)
    def _():
        await_greetings()
        scatter.start(0)

    for level, at in ((0, 1), (1, pairs - 2)):

        @pl.when(step == at)
        def _(level=level):
            scatter.end(level)
            scatter.start(level + 1)

    @pl.when(step == pairs)
    def _():
        rows = [jnp.sum(sums[k], axis=0, keepdims=True) for k in range(2)]
        rows.append(jnp.zeros((6, C_OUT), f32))
        out_ref[...] = sum_all(jnp.concatenate(rows, axis=0), buffers[0:6])

    @pl.when(step == 2 * pairs)
    def _():
        gg_ref[0 : SUBSETS * C_IN, :] = gg[...].astype(bf16)
        rest = gg_ref.shape[0] - SUBSETS * C_IN
        if rest:
            gg_ref[SUBSETS * C_IN :, :] = jnp.zeros((rest, C_OUT), bf16)
        scatter.end(2)
        sum_ref[...] = scatter.out[...]


def graph_back(
    hg_ref, xq_ref, sg_ref, wgt_ref, wst_ref, kront_ref, own_ref, piece_ref, grad_ref,
    ig_ref, taps_sum_ref, sum_ref, edge_ref,
    spread, staged, eg, own_grad, *buffers,
):
    step = pl.program_id(0)
    pairs = pl.num_programs(0) // 2
    total = Total(buffers[0:6])
    gather_taps = Gather(taps_sum_ref.shape[0], buffers[6:15])
    scatter = Scatter(grad_ref, buffers[15:27])
    gather = Gather(grad_ref.shape[0], buffers[27:36])

    @pl.when(step == 0)
    def _():
        greet()
        eg[...] = jnp.zeros_like(eg)
        own_grad[...] = jnp.zeros_like(own_grad)

    def side_by_side(values):
        return jnp.concatenate([values[:, 0:GROUP], values[:, GROUP : 2 * GROUP]], axis=2)

    @pl.when(step < pairs)
    def _():
        rest = jnp.zeros((C_OUT - HALF_ROWS, C_OUT), f32)
        found = None
        owned = None
        for c in range(PHASES):
            if c % 2 == 0:
                pair_back = dot(hg_ref[0, c : c + 2].reshape(2 * ROWS, C_OUT), wgt_ref[...])
                pair_back = pair_back.reshape(2, JOINTS, 2 * GROUP, SUBSETS * C_IN)
            back = pair_back[c % 2]
            for k in range(SUBSETS):
                both = side_by_side(back[:, :, k * C_IN : (k + 1) * C_IN])
                if k == 0:
                    seen = xq_ref[0, c, 0:HALF_ROWS, :].astype(f32)
                    part = seen.reshape(JOINTS, GROUP, 2 * C_IN) * both
                    owned = part if owned is None else owned + part
                both = jnp.concatenate([both.reshape(HALF_ROWS, 2 * C_IN), rest], axis=0)
                spread[step, c, k] = both.astype(bf16)
        for c in range(PHASES):
            both = spread[step, c, 1:3].reshape(2 * C_OUT, C_OUT)
            part = dot_nt(both, xq_ref[0, c])
            found = part if found is None else found + part
        eg[...] += found
        own_grad[...] += owned

    @pl.when(step >= pairs)
    def _():
        pair = step - pairs
        own = own_ref[...]
        own = jnp.concatenate([own, own], axis=2)
        short = dot(sg_ref[0].reshape(4 * ROWS, C_OUT), wst_ref[...])
        short = short.reshape(4, JOINTS, 2 * GROUP, C_IN)
        for c in range(PHASES):
            mixed = dot(kront_ref[...], spread[pair, c, 1:3].reshape(2 * C_OUT, C_OUT))
            direct = spread[pair, c, 0, 0:HALF_ROWS, :].astype(f32)
            result = mixed.reshape(JOINTS, GROUP, 2 * C_IN)
            result = result + direct.reshape(JOINTS, GROUP, 2 * C_IN) * own
            if c % 2 == 0:
                result = result + side_by_side(short[c // 2])
            staged[c] = result
        for side in range(2):
            lanes = slice(side * C_IN, (side + 1) * C_IN)
            for start in range(0, JOINTS, CUT):
                rows = [staged[c, start : start + CUT, :, lanes] for c in range(PHASES)]
                rows = jnp.swapaxes(jnp.stack(rows, axis=1), 1, 2)
                rows = rows.reshape(CUT, GROUP * PHASES, C_IN)
                ig_ref[side, start : start + CUT] = rows.astype(bf16)

    @pl.when(step == 0)
    def _():
        await_greetings()
        scatter.start(0)
        gather_taps.start(0, piece_ref[...])

    for level, at in ((0, 1), (1, 2)):

        @pl.when(step == at)
        def _(level=level):
            scatter.end(level)
            scatter.start(level + 1)

    @pl.when(step == 4)
    def _():
        scatter.end(2)
        gather.start(0, scatter.out[...])
        gather_taps.end(0)
        gather_taps.start(1)

    @pl.when(step == pairs - 1)
    def _():
        lines = lax.broadcasted_iota(jnp.int32, (C_OUT, C_OUT), 0)
        spots = lax.broadcasted_iota(jnp.int32, (C_OUT, C_OUT), 1)
        same = lines % GROUP == spots % GROUP
        row = lax.broadcasted_iota(jnp.int32, (32, C_OUT), 0)
        col = lax.broadcasted_iota(jnp.int32, (32, C_OUT), 1)
        down = (row == col // GROUP).astype(f32)
        sums = jnp.sum(own_grad[...], axis=1)
        sums = jnp.sum(sums, axis=1, keepdims=True)
        row = lax.broadcasted_iota(jnp.int32, (JOINTS, 128), 0)
        col = lax.broadcasted_iota(jnp.int32, (JOINTS, 128), 1)
        packed = jnp.where(row == col, jnp.broadcast_to(sums, (JOINTS, 128)), 0.0)
        packed = jnp.concatenate([packed, jnp.zeros((32 - JOINTS, 128), f32)], axis=0)
        row = lax.broadcasted_iota(jnp.int32, (C_OUT, 128), 0)
        col = lax.broadcasted_iota(jnp.int32, (C_OUT, 128), 1)
        for k in range(2):
            kept = jnp.where(same, eg[k * C_OUT : (k + 1) * C_OUT, :], 0.0)
            narrow = lax.dot_general(
                down, kept, (((1,), (1,)), ((), ())),
                preferred_element_type=f32, precision=lax.Precision.HIGHEST,
            )
            place = (row // GROUP + 32 * (k + 1) == col).astype(f32)
            packed = packed + jnp.dot(
                narrow, place, preferred_element_type=f32, precision=lax.Precision.HIGHEST
            )
        total.start(0, packed)

    @pl.when(step == pairs)
    def _():
        gather.end(0)
        gather.start(1)

    @pl.when(step == pairs + 1)
    def _():
        total.start(1, total.end(0))

    @pl.when(step == pairs + 2)
    def _():
        gather_taps.end(1)
        gather_taps.start(2)

    @pl.when(step == pairs + 3)
    def _():
        gather.end(1)
        gather.start(2)

    @pl.when(step == 2 * pairs - 1)
    def _():
        edge_ref[...] = total.end(1)
        gather_taps.end(2)
        taps_sum_ref[...] = gather_taps.full[...].reshape(taps_sum_ref.shape)
        gather.end(2)
        sum_ref[...] = gather.full[...].reshape(sum_ref.shape)


def update(
    grads_ref, graph_grad_ref, edge_grad_ref, gm_ref, st_ref, cs_ref, bk_ref, fs_ref, ig_ref, o_ref,
    *refs,
):
    groups = [refs[4 * k : 4 * k + 4] for k in range(5)]
    out_ig, out_o, out_norm = refs[20:23]
    outs = [refs[23 + 4 * k : 27 + 4 * k] for k in range(5)]
    squares, norm_grad = refs[43:45]
    step = pl.program_id(0)
    taps_rows = TAPS * C_OUT

    def edge_grad(k):
        values = edge_grad_ref[...]
        if k:
            values = pltpu.roll(values, 128 - 32 * k, 1)
        return values[0:JOINTS, 0:JOINTS] * gm_ref[k]

    def apply(group, out, at, gradient, rate, decay):
        factor = squares[0:1, 0:1]
        new = adam_update(*[ref[at] for ref in group], gradient, factor, rate, decay)
        for ref, value in zip(out, new):
            ref[at] = value

    @pl.when(step == 0)
    def _():
        stats = st_ref[...]
        norm = groups[4][0][...]
        mean, rstd, _, _ = first_moments(stats, norm)
        first_sum = fs_ref[0:1]
        first_norm = rstd * (fs_ref[1:2] - mean * first_sum)
        back_sum, back_conv, back_short = back_totals(
            bk_ref[...], second_moments(stats, cs_ref[...])
        )
        norm_grad[...] = jnp.concatenate(
            [first_norm, first_sum, back_conv, back_sum, back_short, back_sum], axis=0
        )
        total = jnp.zeros((GROUP, C_OUT), f32)
        for start in range(0, taps_rows + C_IN, C_IN):
            rows = grads_ref[start : start + C_IN, :].astype(f32)
            total = total + fold(rows * rows)
        for start in range(0, SUBSETS * C_IN, C_IN):
            rows = graph_grad_ref[start : start + C_IN, :].astype(f32)
            total = total + fold(rows * rows)
        whole = jnp.sum(total) + jnp.sum(norm_grad[...] * norm_grad[...])
        for k in range(SUBSETS):
            values = edge_grad(k)
            whole = whole + jnp.sum(values * values)
        size = jnp.sqrt(jnp.full((GROUP, 128), whole, f32))
        squares[...] = jnp.minimum(1.0, clip_limit / (size + 1e-06))
        out_norm[...] = size
        every = (slice(None), slice(None))
        apply(groups[4], outs[4], every, norm_grad[...], rate_small, 0.0)
        for k in range(SUBSETS):
            apply(groups[3], outs[3], k, edge_grad(k), rate_small, 0.0)

    for k in range(3):
        row = (3 * (step // 2) + k) * C_OUT
        lane = (step % 2) * C_IN
        at = (pl.ds(pl.multiple_of(row, C_OUT), C_OUT), pl.ds(pl.multiple_of(lane, C_IN), C_IN))
        apply(groups[1], outs[1], k, grads_ref[at].astype(f32).T, rate_matrix, decay_matrix)
    rows = graph_grad_ref[pl.ds(pl.multiple_of(step * 64, 64), 64), :].astype(f32)
    every = (slice(None), slice(None))
    apply(groups[0], outs[0], every, rows, rate_matrix, decay_matrix)

    @pl.when(step == 0)
    def _():
        rows = grads_ref[taps_rows : taps_rows + C_IN, :].astype(f32)
        every = (slice(None), slice(None))
        apply(groups[2], outs[2], every, rows, rate_matrix, decay_matrix)

    out_ig[...] = ig_ref[...]
    out_o[...] = o_ref[...]


def whole_spec(shape):
    return pl.BlockSpec(shape, lambda i: (0,) * len(shape))


def lead_spec(shape):
    return pl.BlockSpec(shape, lambda i: (i,) + (0,) * (len(shape) - 1))


def spec(block, index):
    return pl.BlockSpec(block, index)


def by_step(block):
    return spec(block, lambda i: (i,) + (0,) * (len(block) - 1))


def call(body, steps, ins, outs, scratch, name, **more):
    def to_spec(where, shape):
        if where is None:
            return whole_spec(shape)
        return where if isinstance(where, pl.BlockSpec) else by_step(where)

    return pl.pallas_call(
        body,
        grid=(steps,),
        in_specs=[to_spec(where, array.shape) for array, where in ins],
        out_specs=[to_spec(where, shape) for shape, _, where in outs],
        out_shape=[jax.ShapeDtypeStruct(shape, kind) for shape, kind, _ in outs],
        scratch_shapes=scratch,
        compiler_params=params(**more),
        name=name,
    )(*[array for array, _ in ins])


def shards(
    inputs, cotangent, lengths, frame_mask, subsets,
    graph_weight, graph_moment, graph_square, graph_average,
    temporal_weight, temporal_moment, temporal_square, temporal_average,
    shortcut_weight, shortcut_moment, shortcut_square, shortcut_average,
    edge_weight, edge_moment, edge_square, edge_average,
    norm_params, norm_moment, norm_square, norm_average,
):
    clips = inputs.shape[0]
    frames = inputs.shape[1]
    pairs = clips // 2
    natural = jnp.transpose(inputs, (0, 2, 1, 3))
    cot = jnp.transpose(cotangent, (0, 2, 1, 3))

    x_block = (2, JOINTS, frames, C_IN)
    mask_block = (1, PHASES, 2 * GROUP, 128)
    wide_block = (1, PHASES, ROWS, C_OUT)
    out_block = (1, 4, ROWS, C_OUT)
    xe_block = (1, 4, ROWS, C_IN)
    a_block = (1, 2, 8, ROWS, C_OUT)
    rim_block = (1, 2, 64, C_OUT)
    xq_block = (1, PHASES, C_OUT, C_OUT)
    cot_block = (2, JOINTS, frames // 2, C_OUT)
    edge_block = (1, JOINTS, 2 * GROUP, C_IN)
    end_block = (clips, JOINTS, 2 * GROUP, C_IN)
    small = (8, C_OUT)
    dma = pltpu.SemaphoreType.DMA

    def full(block):
        return (pairs,) + block[1:]

    def by_pair(block, pair):
        return spec(block, lambda i: (jnp.clip(pair(i), 0, pairs - 1),) + (0,) * (len(block) - 1))

    def early(block):
        return by_pair(block, lambda i: i)

    def behind(block):
        return by_pair(block, lambda i: i - 1)

    def late(block):
        return by_pair(block, lambda i: i - pairs)

    def later(block):
        return by_pair(block, lambda i: i - pairs - 1)

    vmem = pl.BlockSpec(memory_space=pltpu.VMEM)
    shapes = [
        ((clips * frames, 128), f32),
        ((clips * GROUP, 128), f32),
        ((2 * HALF_ROWS, C_OUT), bf16),
        ((HALF_ROWS, 2 * C_OUT), bf16),
        ((JOINTS, GROUP, C_IN), f32),
        ((SUBSETS, JOINTS, JOINTS), f32),
        ((SUBSETS * C_IN, C_OUT), bf16),
        ((C_OUT, SUBSETS * C_IN), bf16),
        ((C_IN, C_OUT), bf16),
        ((C_OUT, C_IN), bf16),
        ((TAPS, C_OUT, C_OUT), bf16),
    ]
    masks, edge_masks, kron, kront, own, graph_mask, wg, wgt, ws, wst, taps = pl.pallas_call(
        prepare,
        in_specs=[pl.BlockSpec(memory_space=pltpu.SMEM)] + [vmem] * 6,
        out_specs=[vmem] * 11,
        out_shape=[jax.ShapeDtypeStruct(shape, kind) for shape, kind in shapes],
        compiler_params=pltpu.CompilerParams(vmem_limit_bytes=60 * 2**20),
        name="prepare",
    )(lengths, frame_mask, subsets, edge_weight, graph_weight, shortcut_weight, temporal_weight)
    masks = masks.reshape(pairs, PHASES, 2 * GROUP, 128)

    xq, xe, hidden, stats, rims, rim_mask = call(
        graph_forward,
        pairs + 1,
        [
            (natural, early(x_block)),
            (natural, spec(end_block, lambda i: (0, 0, 0, 0))),
            (natural, spec(end_block, lambda i: (0, 0, frames // end_block[2] - 1, 0))),
            (masks, early(mask_block)),
            (edge_masks, None),
            (kron, None),
            (own, None),
            (wg, None),
            (ws, None),
        ],
        [
            (full(xq_block), bf16, early(xq_block)),
            (full(xe_block), bf16, early(xe_block)),
            (full(wide_block), bf16, behind(wide_block)),
            (small, f32, None),
            (full(edge_block), bf16, None),
            (edge_masks.shape, f32, None),
        ],
        [
            pltpu.VMEM((PHASES, 2, JOINTS, GROUP, C_IN), f32),
            pltpu.VMEM((PHASES, ROWS, SUBSETS * C_IN), bf16),
            pltpu.VMEM((4, ROWS, C_IN), bf16),
            pltpu.VMEM((4, GROUP, C_OUT), f32),
            pltpu.VMEM((2, 2 * GROUP, 128), f32),
            pltpu.VMEM(full(edge_block), bf16),
            pltpu.VMEM(full(edge_block), bf16),
            pltpu.VMEM(full(edge_block), bf16),
            pltpu.VMEM(edge_masks.shape, f32),
            pltpu.VMEM(edge_masks.shape, f32),
        ]
        + [dma((2,))] * 4
        + sum_scratch(),
        "graph_forward",
        collective_id=1,
        has_side_effects=True,
    )

    active, conv, conv_stats = call(
        conv_forward,
        pairs,
        [
            (hidden, wide_block),
            (rims, edge_block),
            (masks, mask_block),
            (rim_mask, (2 * GROUP, 128)),
            (stats, None),
            (norm_params, None),
            (kron, None),
            (own, None),
            (wg, None),
            (taps, None),
        ],
        [
            (full(a_block), bf16, a_block),
            (full(out_block), f32, out_block),
            (small, f32, None),
        ],
        [
            pltpu.VMEM((C_OUT, C_OUT), bf16),
            pltpu.VMEM((2, ROWS, HALF), f32),
            pltpu.VMEM((4, 2, ROWS, HALF), f32),
            pltpu.VMEM((2, GROUP, C_OUT), f32),
        ]
        + sum_scratch(),
        "conv_forward",
        collective_id=2,
        has_side_effects=True,
    )

    def both_ways(block):
        return by_pair(block, lambda i: jnp.where(i < pairs, i, i - pairs))

    grad_rows = padded(TAPS * C_OUT + C_IN)
    outputs, conv_grad, short_grad, left_rim, right_rim, grads, back = call(
        middle,
        2 * pairs + 1,
        [
            (conv, early(out_block)),
            (xe, both_ways(xe_block)),
            (cot, early(cot_block)),
            (active, later(a_block)),
            (masks, both_ways(mask_block)),
            (stats, None),
            (conv_stats, None),
            (norm_params, None),
            (ws, None),
        ],
        [
            (cot.shape, bf16, early(cot_block)),
            (full(out_block), bf16, late(out_block)),
            (full(out_block), bf16, late(out_block)),
            (full(rim_block), bf16, None),
            (full(rim_block), bf16, None),
            ((grad_rows, C_OUT), bf16, None),
            (small, f32, None),
        ],
        [
            pltpu.VMEM((2, 2, JOINTS, frames // 2, HALF), f32),
            pltpu.VMEM((2, 2, JOINTS, frames // 2, HALF), f32),
            pltpu.VMEM((3, GROUP, C_OUT), f32),
            pltpu.VMEM(full(out_block), f32),
            pltpu.VMEM(full(out_block), f32),
            pltpu.VMEM((C_OUT, DEPTH), bf16),
            pltpu.VMEM((2, ROWS, HALF), f32),
            pltpu.VMEM((TAPS, C_OUT, C_OUT), f32),
            pltpu.VMEM((C_IN, C_OUT), f32),
        ]
        + [pltpu.VMEM(full(rim_block), bf16)] * 4
        + [dma((pairs,))] * 4
        + sum_scratch(),
        "middle",
        collective_id=3,
        has_side_effects=True,
    )

    graph_rows = padded(SUBSETS * C_IN)
    hidden_grad, first_sums, grad_piece, graph_grad = call(
        conv_back,
        2 * pairs + 1,
        [
            (conv_grad, early(out_block)),
            (left_rim, early(rim_block)),
            (right_rim, early(rim_block)),
            (taps, None),
            (hidden, early(wide_block)),
            (masks, by_pair(mask_block, lambda i: jnp.where(i <= pairs, i - 1, i - pairs - 1))),
            (stats, None),
            (norm_params, None),
            (xq, later(xq_block)),
            (kron, None),
            (own, None),
            (grads, None),
        ],
        [
            (full(wide_block), bf16, later(wide_block)),
            (small, f32, None),
            ((grad_rows // lax.axis_size(("tm", "batch")), C_OUT), bf16, None),
            ((graph_rows, C_OUT), bf16, None),
        ],
        [
            pltpu.VMEM((2, 2, ROWS, HALF), f32),
            pltpu.VMEM((8, ROWS, C_OUT), bf16),
            pltpu.VMEM((2, GROUP, C_OUT), f32),
            pltpu.VMEM(full(wide_block), f32),
            pltpu.VMEM(full(wide_block), bf16),
            pltpu.VMEM((PHASES, ROWS, C_OUT), f32),
            pltpu.VMEM((PHASES, ROWS, SUBSETS * C_IN), bf16),
            pltpu.VMEM((SUBSETS * C_IN, C_OUT), f32),
        ]
        + sum_scratch()
        + Scatter.scratch(grad_rows),
        "conv_back",
        collective_id=4,
        has_side_effects=True,
    )

    input_grad, grad_sums, graph_sum, edge_sum = call(
        graph_back,
        2 * pairs,
        [
            (hidden_grad, early(wide_block)),
            (xq, early(xq_block)),
            (short_grad, late(out_block)),
            (wgt, None),
            (wst, None),
            (kront, None),
            (own, None),
            (grad_piece, None),
            (graph_grad, None),
        ],
        [
            (natural.shape, bf16, late(x_block)),
            ((grad_rows, C_OUT), bf16, None),
            ((graph_rows, C_OUT), bf16, None),
            ((32, 128), f32, None),
        ],
        [
            pltpu.VMEM((pairs, PHASES, SUBSETS, C_OUT, C_OUT), bf16),
            pltpu.VMEM((PHASES, JOINTS, GROUP, 2 * C_IN), f32),
            pltpu.VMEM((2 * C_OUT, C_OUT), f32),
            pltpu.VMEM((JOINTS, GROUP, 2 * C_IN), f32),
        ]
        + sum_scratch((32, 128))
        + Gather.scratch(grad_rows)
        + Scatter.scratch(graph_rows)
        + Gather.scratch(graph_rows),
        "graph_back",
        collective_id=5,
        has_side_effects=True,
    )

    tap_spec = spec((TAPS // 3, C_IN, C_OUT), lambda i: (i // 2, i % 2, 0))
    graph_spec = spec((64, C_OUT), lambda i: (i % 2, i // 2))
    states = [
        (graph_weight, graph_moment, graph_square, graph_average),
        (temporal_weight, temporal_moment, temporal_square, temporal_average),
        (shortcut_weight, shortcut_moment, shortcut_square, shortcut_average),
        (edge_weight, edge_moment, edge_square, edge_average),
        (norm_params, norm_moment, norm_square, norm_average),
    ]
    places = [graph_spec, tap_spec, None, None, None]
    state_ins = [(array, place) for group, place in zip(states, places) for array in group]
    clip_spec = spec((clips // 6, JOINTS, frames, C_IN), lambda i: (i, 0, 0, 0))
    out_spec = spec((clips // 6, JOINTS, frames // 2, C_OUT), lambda i: (i, 0, 0, 0))
    new = call(
        update,
        6,
        [
            (grad_sums, None),
            (graph_sum, None),
            (edge_sum, None),
            (graph_mask, None),
            (stats, None),
            (conv_stats, None),
            (back, None),
            (first_sums, None),
            (input_grad, clip_spec),
            (outputs, out_spec),
        ]
        + state_ins,
        [(natural.shape, bf16, clip_spec), (cot.shape, bf16, out_spec), ((GROUP, 128), f32, None)]
        + [(array.shape, f32, place) for array, place in state_ins],
        [pltpu.VMEM((GROUP, 128), f32), pltpu.VMEM((6, C_OUT), f32)],
        "update",
    )
    return (
        jnp.transpose(new[1], (0, 2, 1, 3)),
        jnp.transpose(new[0], (0, 2, 1, 3)),
        new[2][0, 0:1],
        *new[3:],
    )


def solution(mesh):
    rows = P("batch", "tm", None, None)
    in_specs = (rows, rows, P("batch"), P("batch", "tm")) + (P(),) * 21
    out_specs = (rows, rows) + (P(),) * 21
    return jax.shard_map(shards, mesh=mesh, in_specs=in_specs, out_specs=out_specs, check_vma=False)
```

time: 233 us -> 199 us (0.85)
  Pallas kernels: 231 us -> 196 us
    pallas_call x7 -> x6, Pallas kernels: 227 us -> 192 us  [call(): pl.pallas_call(body, grid=(steps,), in_specs=[to_spec(where, array.shape)...]
where the time goes in v3:
time: 199 us; the launch traced here: 198 us
  Pallas kernels  196 us (98%)
    pallas_call x6, Pallas kernels, call(): pl.pallas_call(body, grid=(steps,), in_specs=[to_spec(where, array.shape)...  192 us
    pallas_call x1, Pallas kernels, shards(): pl.pallas_call(prepare, in_specs=[pl.BlockSpec(memory_space=pltpu.SMEM)]...  3.98 us

profile of v3, /device:TPU:0, one launch (start us, length us, event | category | flops | bytes accessed | tf_op | source)
XLA Modules:
  0.0 198.4 jit_solution(17002155144456060133)
XLA Ops:
  0.7 4.0 %prepare.1 = (f32[768,128]{1,0:T(8,128)}, f32[96,128]{1,0:T(8,128)}, bf16[400,256]{1,0:T(8,128)(2,1)}, bf16[200,512]{1,0:T(8,128)(2,1)}, f32[25,8,128]{2,1,0:T(8...) custom-call(s32[12]{0:T(128)} %length_ref.1, ...), custom_call_target="tpu_custom_call" | custom-call | tf_op jit(solution)/shard_map/prepare/pallas_call | solution.py:1265
  4.6 28.2 %graph_forward.1 = (bf16[6,8,256,256]{3,2,1,0:T(8,128)(2,1)}, bf16[6,4,400,128]{3,2,1,0:T(8,128)(2,1)}, bf16[6,8,400,256]{3,2,1,0:T(8,128)(2,1)}, f32[8,256]{1,0...) custom-call(bf16[12,25,64,128]{3,2,1,0:T(8,128)(2,1)} %bitcast.6, bf16[12,25,64,128]{3,2,1,0:T(8,128)(2,1)} %bitcast.7, ...), custom_call_target="tpu_custom_call" | custom-call | tf_op jit(solution)/shard_map/graph_forward/pallas_call | solution.py:1193
  32.9 27.6 %conv_forward.1 = (bf16[6,2,8,400,256]{4,3,2,1,0:T(8,128)(2,1)}, f32[6,4,400,256]{3,2,1,0:T(8,128)}, f32[8,256]{1,0:T(8,128)}) custom-call(bf16[6,8,400,256]{3,2,1,0:T(8,128)(2,1)} %get-tuple-element.87.h_ref, bf16[6,25,16,128]{3,2,1,0:T(8,128)(2,1)} %get-tuple-element.88.xh_ref, f32[6,8,16,128]{3,2,1,0:T(8,128)} %bitcast.10, ...), custom_call_target="tpu_custom_call" | custom-call | tf_op jit(solution)/shard_map/conv_forward/pallas_call | solution.py:1193
  60.5 45.2 %middle.1 = (bf16[12,25,32,256]{3,2,1,0:T(8,128)(2,1)}, bf16[6,4,400,256]{3,2,1,0:T(8,128)(2,1)}, bf16[6,4,400,256]{3,2,1,0:T(8,128)(2,1)}, bf16[6,2,64,256]{3,2...) custom-call(f32[6,4,400,256]{3,2,1,0:T(8,128)} %get-tuple-element.92.conv_ref, ...), custom_call_target="tpu_custom_call" | custom-call | tf_op jit(solution)/shard_map/middle/pallas_call | solution.py:1193
  105.7 42.4 %conv_back.1 = (bf16[6,8,400,256]{3,2,1,0:T(8,128)(2,1)}, f32[8,256]{1,0:T(8,128)}, bf16[80,256]{1,0:T(8,128)(2,1)}, bf16[512,256]{1,0:T(8,128)(2,1)}) custom-call(bf16[6,4,400,256]{3,2,1,0:T(8,128)(2,1)} %get-tuple-element.96.cg_ref, bf16[6,2,64,256]{3,2,1,0:T(8,128)(2,1)} %get-tuple-element.97.left_ref, ...), custom_call_target="tpu_custom_call" | custom-call | tf_op jit(solution)/shard_map/conv_back/pallas_call | solution.py:1193
  148.1 31.8 %graph_back.1 = (bf16[12,25,64,128]{3,2,1,0:T(8,128)(2,1)}, bf16[2560,256]{1,0:T(8,128)(2,1)}, bf16[512,256]{1,0:T(8,128)(2,1)}, f32[32,128]{1,0:T(8,128)}) custom-call(bf16[6,8,400,256]{3,2,1,0:T(8,128)(2,1)} %get-tuple-element.101.hg_ref, bf16[6,8,256,256]{3,2,1,0:T(8,128)(2,1)} %get-tuple-element.99.xq_ref, ...), custom_call_target="tpu_custom_call" | custom-call | tf_op jit(solution)/shard_map/graph_back/pallas_call | solution.py:1193
  179.9 17.2 %update.1 = (bf16[12,25,64,128]{3,2,1,0:T(8,128)(2,1)}, bf16[12,25,32,256]{3,2,1,0:T(8,128)(2,1)}, f32[8,128]{1,0:T(8,128)}, f32[128,768]{1,0:T(8,128)}, f32[128...) custom-call(bf16[2560,256]{1,0:T(8,128)(2,1)} %get-tuple-element.108, ...), custom_call_target="tpu_custom_call" | custom-call | tf_op jit(solution)/shard_map/update/pallas_call | solution.py:1193
  197.2 1.2 slice.3

commit v4 on v3

--- a/solution.py
+++ b/solution.py
@@ -295,9 +295,9 @@
 
 
 def graph_forward(
-    x_ref, head_ref, tail_ref, m_ref, em_ref, kron_ref, own_ref, wg_ref, ws_ref,
+    x_ref, all_ref, m_ref, em_ref, kron_ref, own_ref, wg_ref, ws_ref,
     xq_ref, xe_ref, h_ref, st_ref, rim_ref, rim_mask_ref,
-    xs, xg, xe, sums, counts, mine, lefts, rights, mask_lefts, mask_rights,
+    xs, xg, xe, head, tail, end_sems, sums, counts, mine, lefts, rights, mask_lefts, mask_rights,
     sent_right, got_left, sent_left, got_right, *sum_buffers,
 ):
     step = pl.program_id(0)
@@ -308,19 +308,21 @@
         with_neighbours(0, mine, mine, lefts, rights, sems, act)
         with_neighbours(1, em_ref, em_ref, mask_lefts, mask_rights, sems, act)
 
+    depth = head.shape[2]
+    end_copies = [
+        pltpu.make_async_copy(all_ref.at[:, :, 0:depth], head, end_sems.at[0]),
+        pltpu.make_async_copy(
+            all_ref.at[:, :, all_ref.shape[2] - depth : all_ref.shape[2]], tail, end_sems.at[1]
+        ),
+    ]
+
     @pl.when(step == 0)
     def _():
         for ref in (lefts, rights, mask_lefts, mask_rights):
             ref[...] = jnp.zeros_like(ref)
         greet()
-        for pair in range(mine.shape[0]):
-            ends = []
-            for clip in (2 * pair, 2 * pair + 1):
-                above = pltpu.roll(tail_ref[clip].astype(f32)[:, GROUP:], 4, 1)
-                below = pltpu.roll(head_ref[clip].astype(f32)[:, :GROUP], 4, 1)
-                sub = lax.broadcasted_iota(jnp.int32, above.shape, 1)
-                ends.append(jnp.where(sub < 4, above, below))
-            mine[pair] = jnp.concatenate(ends, axis=1).astype(bf16)
+        for copy in end_copies:
+            copy.start()
         sums[...] = jnp.zeros_like(sums)
         counts[...] = jnp.zeros_like(counts)
 
@@ -375,6 +377,16 @@
 
     @pl.when(step == 1)
     def _():
+        for copy in end_copies:
+            copy.wait()
+        for pair in range(mine.shape[0]):
+            ends = []
+            for clip in (2 * pair, 2 * pair + 1):
+                above = pltpu.roll(tail[clip].astype(f32)[:, GROUP:], 4, 1)
+                below = pltpu.roll(head[clip].astype(f32)[:, :GROUP], 4, 1)
+                sub = lax.broadcasted_iota(jnp.int32, above.shape, 1)
+                ends.append(jnp.where(sub < 4, above, below))
+            mine[pair] = jnp.concatenate(ends, axis=1).astype(bf16)
         await_greetings()
         rims("start")
 
@@ -385,14 +397,17 @@
             total = JOINTS * jnp.sum(counts[k], axis=0, keepdims=True)
             rows.append(jnp.concatenate([total, total], axis=1))
         rows.append(jnp.zeros((2, C_OUT), f32))
-        st_ref[...] = sum_all(jnp.concatenate(rows, axis=0), sum_buffers)
+        total = Total(sum_buffers)
+        total.start(0, jnp.concatenate(rows, axis=0))
         rims("wait")
         sub = lax.broadcasted_iota(jnp.int32, mask_lefts.shape, 0) % GROUP
         rim_mask_ref[...] = jnp.where(sub < 4, mask_lefts[...], mask_rights[...])
+        total.start(1, total.end(0))
         for pair in range(lefts.shape[0]):
             sub = lax.broadcasted_iota(jnp.int32, lefts.shape[1:], 1) % GROUP
             both = jnp.where(sub < 4, lefts[pair].astype(f32), rights[pair].astype(f32))
             rim_ref[pair] = both.astype(bf16)
+        st_ref[...] = total.end(1)
 
 
 def insert_and_roll(tiles, fill, side):
@@ -417,9 +432,9 @@
     _, _, scale, shift = first_moments(st_ref[...], norm_ref[...])
     scale, shift = 0.5 * scale, 0.5 * shift
 
-    def activate(values, mask):
-        half = values * scale + shift
-        return (half + half * jnp.tanh(half)).reshape(-1, 2 * GROUP, C_OUT) * mask
+    def activate(values, offset):
+        half = values.reshape(-1, 2 * GROUP, C_OUT) * scale + offset
+        return half + half * jnp.tanh(half)
 
     def wide(mask):
         return jnp.concatenate([mask, mask], axis=1)[None]
@@ -429,7 +444,7 @@
     parts = [rim_rows[:, side * GROUP : (side + 1) * GROUP] for side in range(2)]
     put_wide(parts, pad)
     rim_hidden = dot(mix_rows(parts, own_ref[...], kron_ref, pad), wg_ref[...])
-    rim_active = activate(rim_hidden, wide(rim_mask)).reshape(ROWS, C_OUT)
+    rim_active = activate(rim_hidden, wide(rim_mask) * shift).reshape(ROWS, C_OUT)
     for lane in range(2):
         rims[lane] = rim_active[:, lane * HALF : (lane + 1) * HALF]
     for p in range(2):
@@ -445,10 +460,10 @@
     a_ref[0, 1, 7, 0:64, :] = jnp.zeros((64, C_OUT), bf16)
     for c in range(PHASES):
         p, q = c % 2, c // 2
-        mask = wide(m_ref[0, c])
+        offset = wide(m_ref[0, c]) * shift
         for start in range(0, JOINTS, CUT):
             rows = slice(start * 2 * GROUP, (start + CUT) * 2 * GROUP)
-            active = activate(h_ref[0, c, rows, :].astype(f32), mask)
+            active = activate(h_ref[0, c, rows, :].astype(f32), offset)
             a_ref[0, p, q + 2, rows, :] = active.reshape(-1, C_OUT).astype(bf16)
             if p == 1 and q == 1:
                 continue
@@ -465,12 +480,12 @@
         window = a_ref[0, j % 2, j // 2 : j // 2 + 4].reshape(4 * ROWS, C_OUT)
         part = dot(window, taps_ref[j])
         total = part if total is None else total + part
-    conv_ref[0] = total.reshape(4, ROWS, C_OUT)
     for q in range(4):
         block = total[q * ROWS : (q + 1) * ROWS].reshape(JOINTS, 2 * GROUP, C_OUT)
         live = block * wide(m_ref[0, 2 * q])
+        conv_ref[0, q] = live.reshape(ROWS, C_OUT)
         sums[0] += fold(live)
-        sums[1] += fold(live * block)
+        sums[1] += fold(live * live)
 
     @pl.when(step == pl.num_programs(0) - 1)
     def _():
@@ -545,11 +560,11 @@
                 short = short_all[rows]
                 half = conv * scale_conv + short * scale_short + shift
                 turn = jnp.tanh(half)
-                grow = (0.5 + 0.5 * turn).reshape(CUT, 2 * GROUP, C_OUT) * mask
+                grow = (1.0 + turn).reshape(CUT, 2 * GROUP, C_OUT) * mask
                 half = half.reshape(CUT, 2 * GROUP, C_OUT)
                 turn = turn.reshape(CUT, 2 * GROUP, C_OUT)
-                result = (half + half) * grow
-                slope = grow + grow * (half - half * turn)
+                result = half * grow
+                slope = grow * (1.0 + (half - half * turn))
                 cot = jnp.concatenate(
                     [
                         jnp.concatenate(
@@ -584,7 +599,7 @@
 
     @pl.when(step == pairs - 1)
     def _():
-        rows = [jnp.sum(sums[k], axis=0, keepdims=True) for k in range(3)]
+        rows = [0.5 * jnp.sum(sums[k], axis=0, keepdims=True) for k in range(3)]
         rows.append(jnp.zeros((5, C_OUT), f32))
         await_greetings()
         total_ref[...] = sum_all(jnp.concatenate(rows, axis=0), sum_buffers)
@@ -602,19 +617,22 @@
         lead_s, slope_s, shift_s = terms(norm[4:5], mean_short, rstd_short, back_short)
         mask = m_ref[0, 2 * q]
         mask = jnp.concatenate([mask, mask], axis=1)[None]
+        half_c, half_s = 0.5 * lead_c, 0.5 * lead_s
+        offset_c, offset_s = mask * shift_c, mask * shift_s
         short_all = dot(xe_ref[0, q], ws_ref[...])
         for start in range(0, JOINTS, CUT):
             rows = slice(start * 2 * GROUP, (start + CUT) * 2 * GROUP)
             up = up_kept[pair, q, rows, :]
 
-            def masked(values):
-                return (values.reshape(CUT, 2 * GROUP, C_OUT) * mask).reshape(-1, C_OUT)
-
-            cg = up * lead_c - masked(conv_kept[pair, q, rows, :] * slope_c + shift_c)
+            def taken(values, slope, offset):
+                shifted = values.reshape(CUT, 2 * GROUP, C_OUT) * slope + offset
+                return shifted.reshape(-1, C_OUT)
+
+            cg = up * half_c - taken(conv_kept[pair, q, rows, :], slope_c, offset_c)
             cg_ref[0, q, rows, :] = cg.astype(bf16)
             for lane in range(2):
                 edges[lane, rows, :] = cg[:, lane * HALF : (lane + 1) * HALF]
-            sg = up * lead_s - masked(short_all[rows] * slope_s + shift_s)
+            sg = up * half_s - taken(short_all[rows], slope_s, offset_s)
             sg_ref[0, q, rows, :] = sg.astype(bf16)
         for lane in range(2):
             at = slice(lane * HALF, (lane + 1) * HALF)
@@ -673,14 +691,15 @@
 
 
 class Places:
-    def __init__(self, rows):
+    def __init__(self, rows, cores):
         tm = lax.axis_index("tm")
-        self.core = tm % 2
-        self.line = tm // 2
-        self.lines = lax.axis_size("tm") // 2
+        self.cores = cores
+        self.core = tm % cores
+        self.line = tm // cores
+        self.lines = lax.axis_size("tm") // cores
         self.batch = lax.axis_index("batch")
         self.batches = lax.axis_size("batch")
-        self.half = rows // 2
+        self.half = rows // cores
         self.part = self.half // self.lines
         self.piece = self.part // self.batches
 
@@ -690,7 +709,7 @@
     def line_peers(self):
         for d in range(1, self.lines):
             to = lax.rem(self.line + d, self.lines)
-            yield d, to, {"tm": 2 * to + self.core}
+            yield d, to, {"tm": self.cores * to + self.core}
 
     def batch_peers(self):
         for d in range(1, self.batches):
@@ -701,23 +720,26 @@
         return pl.ds(pl.multiple_of(index * count, 16), count)
 
 
-def three_levels(rows):
-    lines, batches = lax.axis_size("tm") // 2, lax.axis_size("batch")
-    half = rows // 2
+def three_levels(rows, cores):
+    lines, batches = lax.axis_size("tm") // cores, lax.axis_size("batch")
+    half = rows // cores
     return lines, batches, half, half // lines, half // lines // batches
 
 
 class Scatter(Places):
-    def __init__(self, source, refs):
-        super().__init__(source.shape[0])
+    def __init__(self, source, refs, cores=2):
+        super().__init__(source.shape[0], cores)
         self.source = source
         self.here, self.up, self.out, self.firsts, self.seconds, self.thirds = refs[0:6]
+        if cores == 1:
+            self.here = source
         self.sems = refs[6:12]
 
     @staticmethod
-    def scratch(rows):
-        lines, batches, half, part, piece = three_levels(rows)
-        shapes = ((half,), (part,), (piece,), (half,), (lines, part), (batches, piece))
+    def scratch(rows, cores=2):
+        lines, batches, half, part, piece = three_levels(rows, cores)
+        core = half if cores == 2 else 16
+        shapes = ((core,), (part,), (piece,), (core,), (lines, part), (batches, piece))
         found = [pltpu.VMEM((*shape, C_OUT), bf16) for shape in shapes]
         for count in (1, lines, batches):
             found += [pltpu.SemaphoreType.DMA((count,))] * 2
@@ -767,15 +789,15 @@
 
 
 class Gather(Places):
-    def __init__(self, rows, refs):
-        super().__init__(rows)
+    def __init__(self, rows, refs, cores=2):
+        super().__init__(rows, cores)
         self.gathered, self.joined, self.full = refs[0:3]
         self.sems = refs[3:9]
 
     @staticmethod
-    def scratch(rows):
-        lines, batches, half, part, piece = three_levels(rows)
-        shapes = ((batches, piece), (lines, part), (2, half))
+    def scratch(rows, cores=2):
+        lines, batches, half, part, piece = three_levels(rows, cores)
+        shapes = ((batches, piece), (lines, part), (cores, half))
         found = [pltpu.VMEM((*shape, C_OUT), bf16) for shape in shapes]
         for count in (batches, lines, 1):
             found += [pltpu.SemaphoreType.DMA((count,))] * 2
@@ -906,11 +928,11 @@
         offset = lead * back_sum / count_in - slope * mean
         for c in range(PHASES):
             mask = m_ref[0, c]
-            mask = jnp.concatenate([mask, mask], axis=1)[None]
+            shifts = jnp.concatenate([mask, mask], axis=1)[None] * offset
             for start in range(0, JOINTS, CUT):
                 rows = slice(start * 2 * GROUP, (start + CUT) * 2 * GROUP)
                 hidden = kept[pair, c, rows, :].astype(f32)
-                taken = (hidden * slope + offset).reshape(CUT, 2 * GROUP, C_OUT) * mask
+                taken = hidden.reshape(CUT, 2 * GROUP, C_OUT) * slope + shifts
                 taken = taken.reshape(-1, C_OUT)
                 hg_ref[0, c, rows, :] = (fg[pair, c, rows, :] * lead - taken).astype(bf16)
             seen = xq_ref[0, c, 0:HALF_ROWS, :].astype(f32).reshape(JOINTS, GROUP, 2 * C_IN)
@@ -958,8 +980,8 @@
     pairs = pl.num_programs(0) // 2
     total = Total(buffers[0:6])
     gather_taps = Gather(taps_sum_ref.shape[0], buffers[6:15])
-    scatter = Scatter(grad_ref, buffers[15:27])
-    gather = Gather(grad_ref.shape[0], buffers[27:36])
+    scatter = Scatter(grad_ref, buffers[15:27], 1)
+    gather = Gather(grad_ref.shape[0], buffers[27:36], 1)
 
     @pl.when(step == 0)
     def _():
@@ -970,12 +992,14 @@
     def side_by_side(values):
         return jnp.concatenate([values[:, 0:GROUP], values[:, GROUP : 2 * GROUP]], axis=2)
 
-    @pl.when(step < pairs)
-    def _():
+    own = own_ref[...]
+    own = jnp.concatenate([own, own], axis=2)
+
+    def spread_out(first):
         rest = jnp.zeros((C_OUT - HALF_ROWS, C_OUT), f32)
         found = None
         owned = None
-        for c in range(PHASES):
+        for c in range(first, first + 4):
             if c % 2 == 0:
                 pair_back = dot(hg_ref[0, c : c + 2].reshape(2 * ROWS, C_OUT), wgt_ref[...])
                 pair_back = pair_back.reshape(2, JOINTS, 2 * GROUP, SUBSETS * C_IN)
@@ -988,28 +1012,28 @@
                     owned = part if owned is None else owned + part
                 both = jnp.concatenate([both.reshape(HALF_ROWS, 2 * C_IN), rest], axis=0)
                 spread[step, c, k] = both.astype(bf16)
-        for c in range(PHASES):
+        for c in range(first, first + 4):
             both = spread[step, c, 1:3].reshape(2 * C_OUT, C_OUT)
             part = dot_nt(both, xq_ref[0, c])
             found = part if found is None else found + part
         eg[...] += found
         own_grad[...] += owned
 
-    @pl.when(step >= pairs)
-    def _():
+    def mix_back(first):
         pair = step - pairs
-        own = own_ref[...]
-        own = jnp.concatenate([own, own], axis=2)
-        short = dot(sg_ref[0].reshape(4 * ROWS, C_OUT), wst_ref[...])
-        short = short.reshape(4, JOINTS, 2 * GROUP, C_IN)
-        for c in range(PHASES):
+        for c in range(first, first + 4):
             mixed = dot(kront_ref[...], spread[pair, c, 1:3].reshape(2 * C_OUT, C_OUT))
             direct = spread[pair, c, 0, 0:HALF_ROWS, :].astype(f32)
             result = mixed.reshape(JOINTS, GROUP, 2 * C_IN)
             result = result + direct.reshape(JOINTS, GROUP, 2 * C_IN) * own
+            if c % 4 == 0:
+                short = dot(sg_ref[0, c // 2 : c // 2 + 2].reshape(2 * ROWS, C_OUT), wst_ref[...])
+                short = short.reshape(2, JOINTS, 2 * GROUP, C_IN)
             if c % 2 == 0:
-                result = result + side_by_side(short[c // 2])
+                result = result + side_by_side(short[c % 4 // 2])
             staged[c] = result
+
+    def put_natural():
         for side in range(2):
             lanes = slice(side * C_IN, (side + 1) * C_IN)
             for start in range(0, JOINTS, CUT):
@@ -1018,28 +1042,7 @@
                 rows = rows.reshape(CUT, GROUP * PHASES, C_IN)
                 ig_ref[side, start : start + CUT] = rows.astype(bf16)
 
-    @pl.when(step == 0)
-    def _():
-        await_greetings()
-        scatter.start(0)
-        gather_taps.start(0, piece_ref[...])
-
-    for level, at in ((0, 1), (1, 2)):
-
-        @pl.when(step == at)
-        def _(level=level):
-            scatter.end(level)
-            scatter.start(level + 1)
-
-    @pl.when(step == 4)
-    def _():
-        scatter.end(2)
-        gather.start(0, scatter.out[...])
-        gather_taps.end(0)
-        gather_taps.start(1)
-
-    @pl.when(step == pairs - 1)
-    def _():
+    def pack_edges():
         lines = lax.broadcasted_iota(jnp.int32, (C_OUT, C_OUT), 0)
         spots = lax.broadcasted_iota(jnp.int32, (C_OUT, C_OUT), 1)
         same = lines % GROUP == spots % GROUP
@@ -1064,34 +1067,81 @@
             packed = packed + jnp.dot(
                 narrow, place, preferred_element_type=f32, precision=lax.Precision.HIGHEST
             )
-        total.start(0, packed)
-
-    @pl.when(step == pairs)
-    def _():
+        return packed
+
+    def begin():
+        await_greetings()
+        scatter.start(1)
+        gather_taps.start(0, piece_ref[...])
+
+    def second():
+        scatter.end(1)
+        scatter.start(2)
+
+    def taps_second():
+        gather_taps.end(0)
+        gather_taps.start(1)
+
+    def third():
+        scatter.end(2)
+        gather.start(0, scatter.out[...])
+        total.start(0, pack_edges())
+
+    def fourth():
+        total.start(1, total.end(0))
+
+    def fifth():
         gather.end(0)
         gather.start(1)
 
-    @pl.when(step == pairs + 1)
-    def _():
-        total.start(1, total.end(0))
-
-    @pl.when(step == pairs + 2)
-    def _():
+    def taps_third():
         gather_taps.end(1)
         gather_taps.start(2)
 
-    @pl.when(step == pairs + 3)
-    def _():
-        gather.end(1)
-        gather.start(2)
-
-    @pl.when(step == 2 * pairs - 1)
-    def _():
+    def finish():
         edge_ref[...] = total.end(1)
         gather_taps.end(2)
         taps_sum_ref[...] = gather_taps.full[...].reshape(taps_sum_ref.shape)
-        gather.end(2)
-        sum_ref[...] = gather.full[...].reshape(sum_ref.shape)
+        gather.end(1)
+        sum_ref[...] = gather.joined[...].reshape(sum_ref.shape)
+
+    schedule = {
+        (3, 1): second,
+        (4, 0): taps_second,
+        (pairs - 1, 1): third,
+        (pairs + 1, 1): fourth,
+        (pairs + 2, 1): fifth,
+        (pairs + 3, 0): taps_third,
+        (2 * pairs - 1, 1): finish,
+    }
+
+    def advance(half):
+        for (at, part), act in schedule.items():
+            if part == half:
+                pl.when(step == at)(act)
+
+    pl.when(step == 2)(begin)
+
+    @pl.when(step < pairs)
+    def _():
+        spread_out(0)
+
+    @pl.when(step >= pairs)
+    def _():
+        mix_back(0)
+
+    advance(0)
+
+    @pl.when(step < pairs)
+    def _():
+        spread_out(4)
+
+    @pl.when(step >= pairs)
+    def _():
+        mix_back(4)
+        put_natural()
+
+    advance(1)
 
 
 def update(
@@ -1143,7 +1193,7 @@
             whole = whole + jnp.sum(values * values)
         size = jnp.sqrt(jnp.full((GROUP, 128), whole, f32))
         squares[...] = jnp.minimum(1.0, clip_limit / (size + 1e-06))
-        out_norm[...] = size
+        out_norm[0] = jnp.max(size)
         every = (slice(None), slice(None))
         apply(groups[4], outs[4], every, norm_grad[...], rate_small, 0.0)
         for k in range(SUBSETS):
@@ -1153,7 +1203,7 @@
         row = (3 * (step // 2) + k) * C_OUT
         lane = (step % 2) * C_IN
         at = (pl.ds(pl.multiple_of(row, C_OUT), C_OUT), pl.ds(pl.multiple_of(lane, C_IN), C_IN))
-        apply(groups[1], outs[1], k, grads_ref[at].astype(f32).T, rate_matrix, decay_matrix)
+        apply(groups[1], outs[1], k, grads_ref[at].T.astype(f32), rate_matrix, decay_matrix)
     rows = graph_grad_ref[pl.ds(pl.multiple_of(step * 64, 64), 64), :].astype(f32)
     every = (slice(None), slice(None))
     apply(groups[0], outs[0], every, rows, rate_matrix, decay_matrix)
@@ -1277,8 +1327,7 @@
         pairs + 1,
         [
             (natural, early(x_block)),
-            (natural, spec(end_block, lambda i: (0, 0, 0, 0))),
-            (natural, spec(end_block, lambda i: (0, 0, frames // end_block[2] - 1, 0))),
+            (natural, pl.BlockSpec(memory_space=pl.ANY)),
             (masks, early(mask_block)),
             (edge_masks, None),
             (kron, None),
@@ -1298,6 +1347,9 @@
             pltpu.VMEM((PHASES, 2, JOINTS, GROUP, C_IN), f32),
             pltpu.VMEM((PHASES, ROWS, SUBSETS * C_IN), bf16),
             pltpu.VMEM((4, ROWS, C_IN), bf16),
+            pltpu.VMEM(end_block, bf16),
+            pltpu.VMEM(end_block, bf16),
+            dma((2,)),
             pltpu.VMEM((4, GROUP, C_OUT), f32),
             pltpu.VMEM((2, 2 * GROUP, 128), f32),
             pltpu.VMEM(full(edge_block), bf16),
@@ -1460,8 +1512,8 @@
         ]
         + sum_scratch((32, 128))
         + Gather.scratch(grad_rows)
-        + Scatter.scratch(graph_rows)
-        + Gather.scratch(graph_rows),
+        + Scatter.scratch(graph_rows, 1)
+        + Gather.scratch(graph_rows, 1),
         "graph_back",
         collective_id=5,
         has_side_effects=True,
@@ -1496,7 +1548,7 @@
             (outputs, out_spec),
         ]
         + state_ins,
-        [(natural.shape, bf16, clip_spec), (cot.shape, bf16, out_spec), ((GROUP, 128), f32, None)]
+        [(natural.shape, bf16, clip_spec), (cot.shape, bf16, out_spec), ((1,), f32, pl.BlockSpec(memory_space=pltpu.SMEM))]
         + [(array.shape, f32, place) for array, place in state_ins],
         [pltpu.VMEM((GROUP, 128), f32), pltpu.VMEM((6, C_OUT), f32)],
         "update",
@@ -1504,7 +1556,7 @@
     return (
         jnp.transpose(new[1], (0, 2, 1, 3)),
         jnp.transpose(new[0], (0, 2, 1, 3)),
-        new[2][0, 0:1],
+        new[2],
         *new[3:],
     )
 

time: 199 us -> 196 us (0.985)
  no operation moved by 1% of the time
where the time goes in v4:
time: 196 us
  Pallas kernels  195 us (99%)
    pallas_call x6, Pallas kernels, call(): pl.pallas_call(body, grid=(steps,), in_specs=[to_spec(where, array.shape)...  191 us
    pallas_call x1, Pallas kernels, shards(): pl.pallas_call(prepare, in_specs=[pl.BlockSpec(memory_space=pltpu.SMEM)]...  3.98 us

profile of v4, /device:TPU:0, one launch (start us, length us, event | category | flops | bytes accessed | tf_op | source)
XLA Modules:
  0.0 195.8 jit_solution(14418451945971843498)
XLA Ops:
  0.7 4.0 %prepare.1 = (f32[768,128]{1,0:T(8,128)}, f32[96,128]{1,0:T(8,128)}, bf16[400,256]{1,0:T(8,128)(2,1)}, bf16[200,512]{1,0:T(8,128)(2,1)}, f32[25,8,128]{2,1,0:T(8...) custom-call(s32[12]{0:T(128)} %length_ref.1, ...), custom_call_target="tpu_custom_call" | custom-call | tf_op jit(solution)/shard_map/prepare/pallas_call | solution.py:1315
  4.6 27.2 %graph_forward.1 = (bf16[6,8,256,256]{3,2,1,0:T(8,128)(2,1)}, bf16[6,4,400,128]{3,2,1,0:T(8,128)(2,1)}, bf16[6,8,400,256]{3,2,1,0:T(8,128)(2,1)}, f32[8,256]{1,0...) custom-call(bf16[12,25,64,128]{3,2,1,0:T(8,128)(2,1)} %bitcast.5, bf16[12,25,64,128]{3,2,1,0:T(8,128)(2,1)} %bitcast.6, ...), custom_call_target="tpu_custom_call" | custom-call | tf_op jit(solution)/shard_map/graph_forward/pallas_call | solution.py:1243
  31.9 27.0 %conv_forward.1 = (bf16[6,2,8,400,256]{4,3,2,1,0:T(8,128)(2,1)}, f32[6,4,400,256]{3,2,1,0:T(8,128)}, f32[8,256]{1,0:T(8,128)}) custom-call(bf16[6,8,400,256]{3,2,1,0:T(8,128)(2,1)} %get-tuple-element.87.h_ref, bf16[6,25,16,128]{3,2,1,0:T(8,128)(2,1)} %get-tuple-element.88.xh_ref, f32[6,8,16,128]{3,2,1,0:T(8,128)} %bitcast.8, ...), custom_call_target="tpu_custom_call" | custom-call | tf_op jit(solution)/shard_map/conv_forward/pallas_call | solution.py:1243
  58.9 44.7 %middle.1 = (bf16[12,25,32,256]{3,2,1,0:T(8,128)(2,1)}, bf16[6,4,400,256]{3,2,1,0:T(8,128)(2,1)}, bf16[6,4,400,256]{3,2,1,0:T(8,128)(2,1)}, bf16[6,2,64,256]{3,2...) custom-call(f32[6,4,400,256]{3,2,1,0:T(8,128)} %get-tuple-element.92.conv_ref, ...), custom_call_target="tpu_custom_call" | custom-call | tf_op jit(solution)/shard_map/middle/pallas_call | solution.py:1243
  103.7 42.3 %conv_back.1 = (bf16[6,8,400,256]{3,2,1,0:T(8,128)(2,1)}, f32[8,256]{1,0:T(8,128)}, bf16[80,256]{1,0:T(8,128)(2,1)}, bf16[512,256]{1,0:T(8,128)(2,1)}) custom-call(bf16[6,4,400,256]{3,2,1,0:T(8,128)(2,1)} %get-tuple-element.96.cg_ref, bf16[6,2,64,256]{3,2,1,0:T(8,128)(2,1)} %get-tuple-element.97.left_ref, ...), custom_call_target="tpu_custom_call" | custom-call | tf_op jit(solution)/shard_map/conv_back/pallas_call | solution.py:1243
  146.0 32.4 %graph_back.1 = (bf16[12,25,64,128]{3,2,1,0:T(8,128)(2,1)}, bf16[2560,256]{1,0:T(8,128)(2,1)}, bf16[512,256]{1,0:T(8,128)(2,1)}, f32[32,128]{1,0:T(8,128)}) custom-call(bf16[6,8,400,256]{3,2,1,0:T(8,128)(2,1)} %get-tuple-element.101.hg_ref, bf16[6,8,256,256]{3,2,1,0:T(8,128)(2,1)} %get-tuple-element.99.xq_ref, ...), custom_call_target="tpu_custom_call" | custom-call | tf_op jit(solution)/shard_map/graph_back/pallas_call | solution.py:1243
  178.4 17.2 %update.1 = (bf16[12,25,64,128]{3,2,1,0:T(8,128)(2,1)}, bf16[12,25,32,256]{3,2,1,0:T(8,128)(2,1)}, f32[1]{0:T(128)}, f32[128,768]{1,0:T(8,128)}, f32[128,768]{1,...) custom-call(bf16[2560,256]{1,0:T(8,128)(2,1)} %get-tuple-element.108, ...), custom_call_target="tpu_custom_call" | custom-call | tf_op jit(solution)/shard_map/update/pallas_call | solution.py:1243

commit v5 on v4

--- a/solution.py
+++ b/solution.py
@@ -212,63 +212,66 @@
     length_ref, frame_ref, subset_ref, edge_ref, graph_ref, short_ref, taps_ref,
     m_ref, em_ref, kron_ref, kront_ref, own_ref, gm_ref, wg_ref, wgt_ref, ws_ref, wst_ref, low_ref,
 ):
-    clips, frames = frame_ref.shape
-    first = lax.axis_index("tm") * frames
-    row = lax.broadcasted_iota(jnp.int32, (clips, frames), 0)
-    ids = lax.broadcasted_iota(jnp.int32, (clips, frames), 1) + first
-    ends = jnp.zeros((clips, frames), jnp.int32)
-    for clip in range(clips):
-        ends = jnp.where(row == clip, length_ref[clip], ends)
-    mask = ((ids < ends) & (frame_ref[...] > 0)).astype(bf16)
-    every = jnp.ones((frames, 128), bf16)
-
-    def spread(rows, clip_of, frame_of):
-        at = lax.broadcasted_iota(jnp.int32, (rows, clips), 0)
-        chosen = (clip_of(at) == lax.broadcasted_iota(jnp.int32, (rows, clips), 1)).astype(bf16)
-        lines = dot(chosen, mask)
-        at = lax.broadcasted_iota(jnp.int32, (rows, frames), 0)
-        kept = frame_of(at) == lax.broadcasted_iota(jnp.int32, (rows, frames), 1)
-        return dot(jnp.where(kept, lines, 0.0).astype(bf16), every)
-
-    side = 2 * GROUP
-    m_ref[...] = spread(
-        clips * frames,
-        lambda at: 2 * (at // (PHASES * side)) + at // GROUP % 2,
-        lambda at: PHASES * (at % GROUP) + at // side % PHASES,
-    )
-    em_ref[...] = spread(
-        clips * GROUP, lambda at: at // GROUP, lambda at: (at % GROUP + frames - 4) % frames
-    )
-    subsets = subset_ref[...]
-    degree = jnp.sum((subsets > 0).astype(f32), axis=0, keepdims=True)
-    lift = one_hot_rows(HALF_ROWS, JOINTS)
-    row = lax.broadcasted_iota(jnp.int32, (JOINTS, C_OUT), 0)
-    drop = (row == lax.broadcasted_iota(jnp.int32, (JOINTS, C_OUT), 1) // GROUP).astype(bf16)
-    row = lax.broadcasted_iota(jnp.int32, (HALF_ROWS, C_OUT), 0)
-    same = row % GROUP == lax.broadcasted_iota(jnp.int32, (HALF_ROWS, C_OUT), 1) % GROUP
-    for k in range(SUBSETS):
-        share = (subsets == k + 1).astype(f32) / degree
-        gm_ref[k] = share
-        low = (share * edge_ref[k]).astype(bf16)
-        if k == 0:
-            row = lax.broadcasted_iota(jnp.int32, (JOINTS, JOINTS), 0)
-            col = lax.broadcasted_iota(jnp.int32, (JOINTS, JOINTS), 1)
-            diagonal = jnp.sum(jnp.where(row == col, low.astype(f32), 0.0), axis=1, keepdims=True)
-            wide = jnp.broadcast_to(diagonal, (JOINTS, C_IN)).astype(bf16)
-            own_ref[...] = dot(lift, wide).reshape(JOINTS, GROUP, C_IN)
-        else:
-            ahead = dot(lift, dot_tn(low, drop).astype(bf16))
-            rows = slice((k - 1) * HALF_ROWS, k * HALF_ROWS)
-            kron_ref[rows, :] = jnp.where(same, ahead, 0.0).astype(bf16)
-            behind = dot(lift, dot(low, drop).astype(bf16))
-            lanes = slice((k - 1) * C_OUT, k * C_OUT)
-            kront_ref[:, lanes] = jnp.where(same, behind, 0.0).astype(bf16)
-        block = graph_ref[:, k * C_OUT : (k + 1) * C_OUT]
-        wg_ref[k * C_IN : (k + 1) * C_IN, :] = block.astype(bf16)
-        wgt_ref[:, k * C_IN : (k + 1) * C_IN] = block.T.astype(bf16)
-    ws_ref[...] = short_ref[...].astype(bf16)
-    wst_ref[...] = short_ref[...].T.astype(bf16)
     low_ref[...] = taps_ref[...].astype(bf16)
+
+    @pl.when(pl.program_id(0) == 0)
+    def _():
+        clips, frames = frame_ref.shape
+        first = lax.axis_index("tm") * frames
+        row = lax.broadcasted_iota(jnp.int32, (clips, frames), 0)
+        ids = lax.broadcasted_iota(jnp.int32, (clips, frames), 1) + first
+        ends = jnp.zeros((clips, frames), jnp.int32)
+        for clip in range(clips):
+            ends = jnp.where(row == clip, length_ref[clip], ends)
+        mask = ((ids < ends) & (frame_ref[...] > 0)).astype(bf16)
+        every = jnp.ones((frames, 128), bf16)
+
+        def spread(rows, clip_of, frame_of):
+            at = lax.broadcasted_iota(jnp.int32, (rows, clips), 0)
+            chosen = (clip_of(at) == lax.broadcasted_iota(jnp.int32, (rows, clips), 1)).astype(bf16)
+            lines = dot(chosen, mask)
+            at = lax.broadcasted_iota(jnp.int32, (rows, frames), 0)
+            kept = frame_of(at) == lax.broadcasted_iota(jnp.int32, (rows, frames), 1)
+            return dot(jnp.where(kept, lines, 0.0).astype(bf16), every)
+
+        side = 2 * GROUP
+        m_ref[...] = spread(
+            clips * frames,
+            lambda at: 2 * (at // (PHASES * side)) + at // GROUP % 2,
+            lambda at: PHASES * (at % GROUP) + at // side % PHASES,
+        )
+        em_ref[...] = spread(
+            clips * GROUP, lambda at: at // GROUP, lambda at: (at % GROUP + frames - 4) % frames
+        )
+        subsets = subset_ref[...]
+        degree = jnp.sum((subsets > 0).astype(f32), axis=0, keepdims=True)
+        lift = one_hot_rows(HALF_ROWS, JOINTS)
+        row = lax.broadcasted_iota(jnp.int32, (JOINTS, C_OUT), 0)
+        drop = (row == lax.broadcasted_iota(jnp.int32, (JOINTS, C_OUT), 1) // GROUP).astype(bf16)
+        row = lax.broadcasted_iota(jnp.int32, (HALF_ROWS, C_OUT), 0)
+        same = row % GROUP == lax.broadcasted_iota(jnp.int32, (HALF_ROWS, C_OUT), 1) % GROUP
+        for k in range(SUBSETS):
+            share = (subsets == k + 1).astype(f32) / degree
+            gm_ref[k] = share
+            low = (share * edge_ref[k]).astype(bf16)
+            if k == 0:
+                row = lax.broadcasted_iota(jnp.int32, (JOINTS, JOINTS), 0)
+                col = lax.broadcasted_iota(jnp.int32, (JOINTS, JOINTS), 1)
+                diagonal = jnp.sum(jnp.where(row == col, low.astype(f32), 0.0), axis=1, keepdims=True)
+                wide = jnp.broadcast_to(diagonal, (JOINTS, C_IN)).astype(bf16)
+                own_ref[...] = dot(lift, wide).reshape(JOINTS, GROUP, C_IN)
+            else:
+                ahead = dot(lift, dot_tn(low, drop).astype(bf16))
+                rows = slice((k - 1) * HALF_ROWS, k * HALF_ROWS)
+                kron_ref[rows, :] = jnp.where(same, ahead, 0.0).astype(bf16)
+                behind = dot(lift, dot(low, drop).astype(bf16))
+                lanes = slice((k - 1) * C_OUT, k * C_OUT)
+                kront_ref[:, lanes] = jnp.where(same, behind, 0.0).astype(bf16)
+            block = graph_ref[:, k * C_OUT : (k + 1) * C_OUT]
+            wg_ref[k * C_IN : (k + 1) * C_IN, :] = block.astype(bf16)
+            wgt_ref[:, k * C_IN : (k + 1) * C_IN] = block.T.astype(bf16)
+        ws_ref[...] = short_ref[...].astype(bf16)
+        wst_ref[...] = short_ref[...].T.astype(bf16)
 
 
 def mix_rows(parts, scales, kron_ref, wide_ref):
@@ -1298,7 +1301,10 @@
     def later(block):
         return by_pair(block, lambda i: i - pairs - 1)
 
-    vmem = pl.BlockSpec(memory_space=pltpu.VMEM)
+    given = (
+        lengths, frame_mask, subsets, edge_weight, graph_weight, shortcut_weight, temporal_weight
+    )
+    taps_block = (TAPS // 3, C_OUT, C_OUT)
     shapes = [
         ((clips * frames, 128), f32),
         ((clips * GROUP, 128), f32),
@@ -1314,12 +1320,15 @@
     ]
     masks, edge_masks, kron, kront, own, graph_mask, wg, wgt, ws, wst, taps = pl.pallas_call(
         prepare,
-        in_specs=[pl.BlockSpec(memory_space=pltpu.SMEM)] + [vmem] * 6,
-        out_specs=[vmem] * 11,
+        grid=(3,),
+        in_specs=[pl.BlockSpec(memory_space=pltpu.SMEM)]
+        + [whole_spec(array.shape) for array in given[1:-1]]
+        + [by_step(taps_block)],
+        out_specs=[whole_spec(shape) for shape, _ in shapes[:-1]] + [by_step(taps_block)],
         out_shape=[jax.ShapeDtypeStruct(shape, kind) for shape, kind in shapes],
         compiler_params=pltpu.CompilerParams(vmem_limit_bytes=60 * 2**20),
         name="prepare",
-    )(lengths, frame_mask, subsets, edge_weight, graph_weight, shortcut_weight, temporal_weight)
+    )(*given)
     masks = masks.reshape(pairs, PHASES, 2 * GROUP, 128)
 
     xq, xe, hidden, stats, rims, rim_mask = call(

time: 196 us -> 197 us (level)
  no operation moved by 1% of the time
where the time goes in v5:
time: 197 us
  Pallas kernels  196 us (99%)
    pallas_call x6, Pallas kernels, call(): pl.pallas_call(body, grid=(steps,), in_specs=[to_spec(where, array.shape)...  191 us
    pallas_call x1, Pallas kernels, shards(): pl.pallas_call(prepare, grid=(3,), in_specs=[pl.BlockSpec(memory_space=pl...  4.95 us

profile of v5, /device:TPU:0, one launch (start us, length us, event | category | flops | bytes accessed | tf_op | source)
XLA Modules:
  0.0 196.8 jit_solution(7064392050950207889)
XLA Ops:
  0.7 5.0 %prepare.1 = (f32[768,128]{1,0:T(8,128)}, f32[96,128]{1,0:T(8,128)}, bf16[400,256]{1,0:T(8,128)(2,1)}, bf16[200,512]{1,0:T(8,128)(2,1)}, f32[25,8,128]{2,1,0:T(8...) custom-call(s32[12]{0:T(128)} %length_ref.1, ...), custom_call_target="tpu_custom_call" | custom-call | tf_op jit(solution)/shard_map/prepare/pallas_call | solution.py:1321
  5.6 27.2 %graph_forward.1 = (bf16[6,8,256,256]{3,2,1,0:T(8,128)(2,1)}, bf16[6,4,400,128]{3,2,1,0:T(8,128)(2,1)}, bf16[6,8,400,256]{3,2,1,0:T(8,128)(2,1)}, f32[8,256]{1,0...) custom-call(bf16[12,25,64,128]{3,2,1,0:T(8,128)(2,1)} %bitcast.5, bf16[12,25,64,128]{3,2,1,0:T(8,128)(2,1)} %bitcast.6, ...), custom_call_target="tpu_custom_call" | custom-call | tf_op jit(solution)/shard_map/graph_forward/pallas_call | solution.py:1246
  32.8 27.0 %conv_forward.1 = (bf16[6,2,8,400,256]{4,3,2,1,0:T(8,128)(2,1)}, f32[6,4,400,256]{3,2,1,0:T(8,128)}, f32[8,256]{1,0:T(8,128)}) custom-call(bf16[6,8,400,256]{3,2,1,0:T(8,128)(2,1)} %get-tuple-element.87.h_ref, bf16[6,25,16,128]{3,2,1,0:T(8,128)(2,1)} %get-tuple-element.88.xh_ref, f32[6,8,16,128]{3,2,1,0:T(8,128)} %bitcast.8, ...), custom_call_target="tpu_custom_call" | custom-call | tf_op jit(solution)/shard_map/conv_forward/pallas_call | solution.py:1246
  59.9 44.7 %middle.1 = (bf16[12,25,32,256]{3,2,1,0:T(8,128)(2,1)}, bf16[6,4,400,256]{3,2,1,0:T(8,128)(2,1)}, bf16[6,4,400,256]{3,2,1,0:T(8,128)(2,1)}, bf16[6,2,64,256]{3,2...) custom-call(f32[6,4,400,256]{3,2,1,0:T(8,128)} %get-tuple-element.92.conv_ref, ...), custom_call_target="tpu_custom_call" | custom-call | tf_op jit(solution)/shard_map/middle/pallas_call | solution.py:1246
  104.6 42.3 %conv_back.1 = (bf16[6,8,400,256]{3,2,1,0:T(8,128)(2,1)}, f32[8,256]{1,0:T(8,128)}, bf16[80,256]{1,0:T(8,128)(2,1)}, bf16[512,256]{1,0:T(8,128)(2,1)}) custom-call(bf16[6,4,400,256]{3,2,1,0:T(8,128)(2,1)} %get-tuple-element.96.cg_ref, bf16[6,2,64,256]{3,2,1,0:T(8,128)(2,1)} %get-tuple-element.97.left_ref, ...), custom_call_target="tpu_custom_call" | custom-call | tf_op jit(solution)/shard_map/conv_back/pallas_call | solution.py:1246
  146.9 32.4 %graph_back.1 = (bf16[12,25,64,128]{3,2,1,0:T(8,128)(2,1)}, bf16[2560,256]{1,0:T(8,128)(2,1)}, bf16[512,256]{1,0:T(8,128)(2,1)}, f32[32,128]{1,0:T(8,128)}) custom-call(bf16[6,8,400,256]{3,2,1,0:T(8,128)(2,1)} %get-tuple-element.101.hg_ref, bf16[6,8,256,256]{3,2,1,0:T(8,128)(2,1)} %get-tuple-element.99.xq_ref, ...), custom_call_target="tpu_custom_call" | custom-call | tf_op jit(solution)/shard_map/graph_back/pallas_call | solution.py:1246
  179.4 17.2 %update.1 = (bf16[12,25,64,128]{3,2,1,0:T(8,128)(2,1)}, bf16[12,25,32,256]{3,2,1,0:T(8,128)(2,1)}, f32[1]{0:T(128)}, f32[128,768]{1,0:T(8,128)}, f32[128,768]{1,...) custom-call(bf16[2560,256]{1,0:T(8,128)(2,1)} %get-tuple-element.108, ...), custom_call_target="tpu_custom_call" | custom-call | tf_op jit(solution)/shard_map/update/pallas_call | solution.py:1246
